TPU v7x, 32 devices: a whole 2x2x4 slice. The times are simulated.
32 devices in a mesh: groups: 2 (over y), fsdp: 4 (over z), tp: 2 (over x), sub: 2 (over core).
Axes of the slice: x: 2, y: 2, z: 4, core: 2. Of those that a mesh axis runs over, the one named last changes fastest.
Arguments:
- inputs: bfloat16 [64, 4, 8192], P(('groups', 'fsdp', 'sub'), None, 'tp'), parts along dimension 0, may hold values from -6 to 6
- queries: bfloat16 [64, 4, 4096], P(('groups', 'fsdp', 'sub'), None, 'tp'), parts along dimension 0, may hold values from -40 to 40
- kv_cache: bfloat16 [2, 64, 256, 512], P(None, ('groups', 'fsdp', 'sub'), None, 'tp'), parts along dimension 1, may hold values from -4 to 4
- lengths: int32 [64], P(('groups', 'fsdp', 'sub')), parts along dimension 0, may hold values from 32 to 256, as said below
- base: bfloat16 [2, 8192, 512], P(None, None, 'tp'), may hold values from -0.0625 to 0.0625
- a_factor: bfloat16 [2, 256, 8192], P(None, 'tp', ('fsdp', 'sub')), may hold values from -0.0625 to 0.0625
- b_factor: bfloat16 [2, 512, 256], P(None, 'tp', ('fsdp', 'sub')), may hold values from -0.375 to 0.375
Outputs:
- fresh_kv: bfloat16 [2, 64, 4, 512], P(None, ('groups', 'fsdp', 'sub'), None, 'tp'), parts along dimension 1
- attended: bfloat16 [64, 4, 4096], P(('groups', 'fsdp', 'sub'), None, 'tp'), parts along dimension 0
There are 2 independent parts, one for each index of `groups`. A program takes and returns all parts, laid end to end along the dimension named above; an argument that names none is the same for every part. Nothing has to cross between parts.
Inputs may be any that keep to these rules, and one draw needn't show every extreme that they name: `lengths`: some row in every draw has exactly 256.
All inputs are finite; a program needn't handle non-finite values.
Results may differ from a plain program's by a relative error of at most 0.0055.
Values may be sent and summed in bfloat16 or wider, within the bound.
No kernel may reach another device: no remote copies, remote signals or barrier semaphores. Data moves between devices by JAX's collectives and lax.ppermute only.
A program may use at most 64 MiB of HBM per device.

v0:
```python
import jax
import jax.numpy as jnp
from jax import lax
from jax.sharding import PartitionSpec as P

HD = 128
KVH = 4
QH = 32


def attend(queries, kv_cache, fresh, lengths):
    rows, steps = (queries.shape[0], queries.shape[1])
    heads_kv = fresh.shape[3] // HD
    group = QH // KVH
    cached = kv_cache.shape[2]
    scale = HD ** (-0.5)
    query = queries.reshape(rows, steps, heads_kv, group, HD)
    keys_old = kv_cache[0].reshape(rows, cached, heads_kv, HD)
    values_old = kv_cache[1].reshape(rows, cached, heads_kv, HD)
    keys_new = fresh[0].reshape(rows, steps, heads_kv, HD)
    values_new = fresh[1].reshape(rows, steps, heads_kv, HD)
    old_scores = (
        jnp.einsum("bskgh,blkh->bkgsl", query, keys_old, preferred_element_type=jnp.float32) * scale
    )
    new_scores = (
        jnp.einsum("bskgh,bukh->bkgsu", query, keys_new, preferred_element_type=jnp.float32) * scale
    )
    positions = jnp.arange(cached, dtype=jnp.int32)
    valid_old = (positions[None, :] < lengths[:, None])[:, None, None, None, :]
    order = jnp.arange(steps, dtype=jnp.int32)
    valid_new = (order[None, :] <= order[:, None])[None, None, None, :, :]
    old_scores = jnp.where(valid_old, old_scores, -jnp.inf)
    new_scores = jnp.where(valid_new, new_scores, -jnp.inf)
    top = jnp.maximum(jnp.max(old_scores, axis=-1), jnp.max(new_scores, axis=-1))
    old_exp = jnp.where(valid_old, jnp.exp(old_scores - top[..., None]), 0.0)
    new_exp = jnp.where(valid_new, jnp.exp(new_scores - top[..., None]), 0.0)
    total = jnp.sum(old_exp, axis=-1) + jnp.sum(new_exp, axis=-1)
    old_weights = (old_exp / total[..., None]).astype(jnp.bfloat16)
    new_weights = (new_exp / total[..., None]).astype(jnp.bfloat16)
    mixed = jnp.einsum(
        "bkgsl,blkh->bskgh", old_weights, values_old, preferred_element_type=jnp.float32
    )
    mixed = mixed + jnp.einsum(
        "bkgsu,bukh->bskgh", new_weights, values_new, preferred_element_type=jnp.float32
    )
    return mixed.astype(jnp.bfloat16).reshape(rows, steps, heads_kv * group * HD)


def make_project(merged, row_count, steps):

    def project(running, piece, start):
        width = piece.shape[2]
        tokens = piece.reshape(row_count * steps, width)
        return jnp.einsum("td,mdc->mtc", tokens, merged, preferred_element_type=jnp.float32)

    return project


def local(inputs, queries, kv_cache, lengths, base, a_factor, b_factor):
    ranks = lax.all_gather(a_factor, "tp", axis=1, tiled=True)
    up_rows = lax.all_gather(b_factor, ("fsdp", "sub"), axis=2, tiled=True)
    row_count, steps = (inputs.shape[0], inputs.shape[1])
    columns = base.shape[2]
    initial = jnp.zeros((2, row_count * steps, columns), jnp.float32)
    slab_width = ranks.shape[2]
    frozen = lax.dynamic_slice_in_dim(
        base, lax.axis_index(("fsdp", "sub")) * slab_width, ranks.shape[2], 1
    )
    delta = jnp.einsum("mrd,mcr->mdc", ranks, up_rows, preferred_element_type=jnp.float32)
    own_rows = (frozen.astype(jnp.float32) + delta).astype(jnp.bfloat16)
    merged = lax.all_gather(own_rows, ("fsdp", "sub"), axis=1, tiled=True)
    project = make_project(merged, row_count, steps)
    projected = project(initial, lax.all_gather(inputs, "tp", axis=2, tiled=True), jnp.int32(0))
    fresh = projected.astype(jnp.bfloat16).reshape(2, row_count, steps, columns)
    attended = attend(queries, kv_cache, fresh, lengths)
    return (fresh, attended)


def solution(mesh):
    return jax.shard_map(
        local,
        mesh=mesh,
        in_specs=(
            P(("groups", "fsdp", "sub"), None, "tp"),
            P(("groups", "fsdp", "sub"), None, "tp"),
            P(None, ("groups", "fsdp", "sub"), None, "tp"),
            P(("groups", "fsdp", "sub")),
            P(None, None, "tp"),
            P(None, "tp", ("fsdp", "sub")),
            P(None, "tp", ("fsdp", "sub")),
        ),
        out_specs=(
            P(None, ("groups", "fsdp", "sub"), None, "tp"),
            P(("groups", "fsdp", "sub"), None, "tp"),
        ),
        check_vma=False,
    )
```

profile of v0, /device:TPU:0, one launch (start us, length us, event | category | flops | bytes accessed | tf_op | source)
XLA Modules:
  0.0 133.1 jit_solution(17828451757689443132)
XLA Ops:
  7.2 0.0 copy-start
  7.2 0.0 all-gather.3.cloned.1.call-start
  7.2 0.7 all-gather.3.cloned.1.call-update
  7.9 0.0 all-gather.5.cloned.1.call-start
  8.0 16.1 %all_gather.13 = bf16[2,256,256]{1,2,0:T(8,128)(2,1)S(1)} all-gather(bf16[2,256,32]{1,2,0:T(8,128)(2,1)} %param.13), channel_id=1, replica_groups=mesh['groups'=2,'fsdp'=4,'tp'=2,'sub'=2] {'fsdp','sub'}, dimensions={2}, use_global_device_ids=true | all-gather | bytes 294912 | tf_op jit(solution)/shard_map/all_gather | solution.py:61
  24.1 9.5 %all-gather.3.cloned.1.call-done = bf16[2,256,1024]{2,1,0:T(8,128)(2,1)} async-done(((bf16[2,128,1024]{2,1,0:T(8,128)(2,1)}), bf16[2,256,1024]{2,1,0:T(8,128)(2,1)}) %all-gather.3.cloned.1.call-update) | async-done | bytes 1048592 | tf_op jit(solution)/shard_map/all_gather | solution.py:60
  33.6 3.2 %add_convert_fusion = bf16[2,1024,256]{2,1,0:T(8,128)(2,1)} fusion(bf16[2,256,1024]{2,1,0:T(8,128)(2,1)} %all-gather.3.cloned.1.call-done, bf16[2,256,256]{1,2,0:T(8,128)(2,1)S(1)} %all_gather.13, bf16[2,8192,256]{2,1,0:T(8,128)(2,1)} %param.11, s32[]{:T(128)S(6)} %select_n.20), kind=kOutput, calls=%fused_computation | convolution fusion | flops 270008320 | bytes 3407876 | tf_op jit(solution)/shard_map/mrd,mcr->mdc/dot_general | solution.py:69
  36.8 0.0 all-gather.5.cloned.1.call-update
  36.8 6.1 %all_gather.15 = bf16[4,4,8192]{2,1,0:T(4,128)(2,1)S(1)} all-gather(bf16[4,4,4096]{2,1,0:T(4,128)(2,1)} %param.7), channel_id=1, replica_groups=mesh['groups'=2,'fsdp'=4,'tp'=2,'sub'=2] {'tp'}, dimensions={2}, use_global_device_ids=true | all-gather | bytes 393216 | tf_op jit(solution)/shard_map/all_gather | solution.py:73
  42.9 0.1 reshape.63
  43.0 0.9 reshape.61
  43.9 1.4 %fusion.23 = (bf16[1,4,256,256]{3,2,1,0:T(8,128)(2,1)S(1)}, bf16[1,4,256,256]{3,2,1,0:T(8,128)(2,1)S(1)}) fusion(bf16[2,4,256,256]{3,2,1,0:T(8,128)(2,1)} %param.9), kind=kLoop, calls=%fused_computation.35 | loop fusion | bytes 2097152 | tf_op jit(solution)/shard_map/slice | solution.py:19
  45.3 0.2 copy.34
  45.5 0.2 copy.35
  45.7 0.0 copy-done
  45.7 0.1 iota_compare_fusion
  45.8 0.3 fusion.25
  46.1 72.9 %all-gather.5.cloned.1.call-done = bf16[2,8192,256]{2,1,0:T(8,128)(2,1)} async-done(((bf16[2,1024,256]{2,1,0:T(8,128)(2,1)}), bf16[2,8192,256]{2,1,0:T(8,128)(2,1)}) %all-gather.5.cloned.1.call-update) | async-done | bytes 8388624 | tf_op jit(solution)/shard_map/all_gather | solution.py:71
  119.0 4.6 %fusion.6 = bf16[2,16,256]{2,1,0:T(8,128)(2,1)S(1)} fusion(bf16[16,8192,1]{1,0,2:T(8,128)(2,1)S(1)} %reshape.63, bf16[2,8192,256]{2,1,0:T(8,128)(2,1)} %all-gather.5.cloned.1.call-done), kind=kOutput, calls=%fused_computation.12 | convolution fusion | flops 134225920 | bytes 8667136 | tf_op jit(solution)/shard_map/td,mdc->mtc/dot_general | solution.py:54
  123.6 0.6 reshape.60
  124.2 0.4 fusion.26
  124.7 0.1 fusion.14
  124.8 0.2 fusion.7
  125.0 0.3 convolution_bitcast_fusion.1
  125.3 0.3 fusion.3
  125.6 0.6 reshape.62
  (7 shorter events, 0.1 us)
Async XLA Ops:
  7.2 38.5 %copy-start = (s32[4]{0:T(128)S(1)}, s32[4]{0:T(128)}, u32[]{:S(2)}) copy-start(s32[4]{0:T(128)} %param.10) | copy-start | bytes 52
  7.2 26.4 %all-gather.3.cloned.1.call-start = ((), (), s32[]{:S(2)}) async-start(), calls=%async_computation | async-start | bytes 1572864 | tf_op jit(solution)/shard_map/all_gather | solution.py:60
  7.9 111.1 %all-gather.5.cloned.1.call-start = ((), (), s32[]{:S(2)}) async-start(), calls=%async_computation.1 | async-start | bytes 9437184 | tf_op jit(solution)/shard_map/all_gather | solution.py:71
Sparse Core Ops, SparseCore 0:
  9.6 23.9 all-gather.2
  36.9 82.0 all-gather.4
where the time goes:
time: 133 us
  waiting for transfers between devices  83.2 us (63%)
  blocking collectives  22.2 us (17%)
  between operations  14.1 us (11%)
  matrix products  9.03 us (7%)
  local copies, waits for them, and re-layouts  4.06 us (3%)
    all_gather x1, waiting for transfers between devices, local(): merged = lax.all_gather(own_rows, ('fsdp', 'sub'), axis=1, tiled=True)  72.9 us
    all_gather x1, blocking collectives, local(): up_rows = lax.all_gather(b_factor, ('fsdp', 'sub'), axis=2, tiled=True)  16.1 us
    all_gather x1, waiting for transfers between devices, local(): ranks = lax.all_gather(a_factor, 'tp', axis=1, tiled=True)  9.53 us
    all_gather x1, blocking collectives, local(): lax.all_gather(inputs, 'tp', axis=2, tiled=True)  6.12 us
    dot_general x1, matrix products, project(): jnp.einsum('td,mdc->mtc', tokens, merged, preferred_element_type=jnp.floa...  4.57 us
    dot_general x1, matrix products, local(): jnp.einsum('mrd,mcr->mdc', ranks, up_rows, preferred_element_type=jnp.flo...  3.17 us
  transfers between devices with their start and end apart: 2, of which 2 were waited for; matrix products, arithmetic and copies ran while one was open for 2% of the time, Pallas kernels for 0%

commit v1 on v0

v1 whole, which is shorter than its diff:
```python
import functools

import jax
import jax.numpy as jnp
from jax import lax
from jax.experimental import pallas as pl
from jax.experimental.pallas import tpu as pltpu
from jax.sharding import PartitionSpec as P

HD = 128
KVH = 4
QH = 32
NEG = -1e30
VMEM_LIMIT = 40 * 2**20

NT = (((1,), (1,)), ((), ()))
NN = (((1,), (0,)), ((), ()))


def dot(x, y, dims=NN):
    return lax.dot_general(x, y, dims, preferred_element_type=jnp.float32)


def vmem():
    return pl.BlockSpec(memory_space=pltpu.VMEM)


def params():
    return pltpu.CompilerParams(vmem_limit_bytes=VMEM_LIMIT)


def cache_kernel(group, len_ref, q_ref, kv_ref, q_out, acc_out, top_out, sum_out):
    rows, steps, width = q_ref.shape
    heads, cached = width // (group * HD), kv_ref.shape[2]
    tokens = rows * steps
    flat = jnp.concatenate([q_ref[b].astype(jnp.float32) for b in range(rows)], axis=0)
    flat = flat.astype(jnp.bfloat16)
    count = group * tokens
    row_of = (lax.broadcasted_iota(jnp.int32, (count, 1), 0) % tokens) // steps
    filled = jnp.zeros((count, 1), jnp.int32)
    for b in range(rows):
        filled = jnp.where(row_of == b, len_ref[b], filled)
    position = lax.broadcasted_iota(jnp.int32, (count, cached), 1)
    for g in range(heads):
        query = jnp.concatenate(
            [flat[:, (g * group + h) * HD : (g * group + h + 1) * HD] for h in range(group)], axis=0
        )
        q_out[g] = query
        cols = slice(g * HD, (g + 1) * HD)
        scores = []
        for b in range(rows):
            valid = jnp.logical_and(row_of == b, position < filled)
            scores.append(jnp.where(valid, dot(query, kv_ref[0, b, :, cols], NT) * HD**-0.5, NEG))
        top = functools.reduce(jnp.maximum, [jnp.max(x, axis=1, keepdims=True) for x in scores])
        total = jnp.zeros((count, 1), jnp.float32)
        mixed = jnp.zeros((count, HD), jnp.float32)
        for b in range(rows):
            weight = jnp.exp(scores[b] - top)
            total = total + jnp.sum(weight, axis=1, keepdims=True)
            high = weight.astype(jnp.bfloat16)
            low = (weight - high.astype(jnp.float32)).astype(jnp.bfloat16)
            values = kv_ref[1, b, :, cols]
            mixed = mixed + dot(high, values) + dot(low, values)
        acc_out[g] = mixed
        top_out[g] = jnp.broadcast_to(top, (count, HD))
        sum_out[g] = jnp.broadcast_to(total, (count, HD))


def early_kernel(blocks, place_ref, base_ref, *refs):
    x_refs, a_refs, out_ref = refs[:blocks], refs[blocks:-1], refs[-1]
    step, width, columns = pl.program_id(0), base_ref.shape[1], base_ref.shape[2]
    tokens, slab, ranks = x_refs[0].shape[0], a_refs[0].shape[2], a_refs[0].shape[1]

    def stacked(start, size):
        return jnp.concatenate([x[:, pl.ds(start, size)] for x in x_refs], axis=0)

    @pl.when(step == 0)
    def _():
        for m in range(2):
            total = jnp.zeros((blocks * tokens, ranks), jnp.float32)
            for i, a in enumerate(a_refs):
                start = pl.multiple_of(place_ref[1 + i] * slab, slab)
                total = total + dot(stacked(start, slab), a[m], NT)
            out_ref[:, 2 * columns + m * ranks : 2 * columns + (m + 1) * ranks] = total
        out_ref[:, : 2 * columns] = jnp.zeros((blocks * tokens, 2 * columns), jnp.float32)

    x = stacked(pl.multiple_of(step * width, width), width)
    for m in range(2):
        cols = slice(m * columns, (m + 1) * columns)
        out_ref[:, cols] = out_ref[:, cols] + dot(x, base_ref[m])


def late_kernel(blocks, columns, place_ref, part_ref, *refs):
    x_refs, outs = refs[:blocks], refs[-blocks:]
    a_refs = refs[blocks:-blocks]
    tokens, slab, ranks = x_refs[0].shape[0], a_refs[0].shape[2], a_refs[0].shape[1]
    acc = part_ref.shape[1]
    sums = [part_ref[:, : 2 * columns]]
    for m in range(2):
        total = part_ref[:, 2 * columns + m * ranks : 2 * columns + (m + 1) * ranks]
        for i, a in enumerate(a_refs):
            start = pl.multiple_of(place_ref[i] * slab, slab)
            x = jnp.concatenate([x[:, pl.ds(start, slab)] for x in x_refs], axis=0)
            total = total + dot(x, a[m], NT)
        sums.append(total)
    whole = jnp.concatenate(sums, axis=1)
    shift = place_ref[len(a_refs)]
    for j, out in enumerate(outs):
        value = jnp.zeros((tokens, acc), jnp.float32)
        for k in range(blocks):
            mine = lax.rem(shift - k + blocks, blocks) == j
            value = jnp.where(mine, whole[k * tokens : (k + 1) * tokens], value)
        out[...] = value.astype(out.dtype)


def rank_kernel(columns, mine_ref, *refs):
    total = mine_ref[:, 2 * columns :]
    for other in refs[:-1]:
        total = total + other[:, 2 * columns :].astype(jnp.float32)
    refs[-1][...] = total.astype(jnp.bfloat16)


def final_kernel(blocks, steps, group, place_ref, mine_ref, *refs):
    others, refs = refs[: blocks - 1], refs[blocks - 1 :]
    rank_refs, refs = refs[:blocks], refs[blocks:]
    up_ref, q_ref, acc_ref, top_ref, sum_ref, fresh_out, out = refs
    tokens, columns = mine_ref.shape[0], fresh_out.shape[3]
    rows, heads = tokens // steps, columns // HD
    ranks = rank_refs[0].shape[1] // 2
    fresh = []
    for m in range(2):
        cols = slice(m * columns, (m + 1) * columns)
        total = mine_ref[:, cols]
        for other in others:
            total = total + other[:, cols].astype(jnp.float32)
        for i, rank in enumerate(rank_refs):
            start = pl.multiple_of(place_ref[i] * ranks, ranks)
            total = total + dot(rank[:, m * ranks : (m + 1) * ranks], up_ref[m, pl.ds(start, ranks)])
        for b in range(rows):
            fresh_out[m, b] = total[b * steps : (b + 1) * steps].astype(jnp.bfloat16)
        fresh.append(total.astype(jnp.bfloat16))
    count = group * tokens
    token = lax.broadcasted_iota(jnp.int32, (count, tokens), 0) % tokens
    key = lax.broadcasted_iota(jnp.int32, (count, tokens), 1)
    valid = jnp.logical_and(token // steps == key // steps, key <= token)
    for g in range(heads):
        cols = slice(g * HD, (g + 1) * HD)
        scores = jnp.where(valid, dot(q_ref[g], fresh[0][:, cols], NT) * HD**-0.5, NEG)
        top_old = top_ref[g][:, :1]
        top = jnp.maximum(top_old, jnp.max(scores, axis=1, keepdims=True))
        scale = jnp.exp(top_old - top)
        weight = jnp.where(valid, jnp.exp(scores - top), 0.0)
        total = sum_ref[g][:, :1] * scale + jnp.sum(weight, axis=1, keepdims=True)
        weight = (weight / total).astype(jnp.bfloat16)
        mixed = acc_ref[g] * (scale / total) + dot(weight, fresh[1][:, cols])
        for h in range(group):
            lanes = slice((g * group + h) * HD, (g * group + h + 1) * HD)
            for b in range(rows):
                at = h * tokens + b * steps
                out[b, :, lanes] = mixed[at : at + steps].astype(jnp.bfloat16)


def smem():
    return pl.BlockSpec(memory_space=pltpu.SMEM)


def local(sizes, inputs, queries, kv_cache, lengths, base, a_factor, b_factor):
    fsdp, tp, sub = sizes
    inner = fsdp // tp
    row_count, steps, wide = inputs.shape
    tokens, columns, ranks = row_count * steps, base.shape[2], a_factor.shape[1]
    heads, group = columns // HD, QH // KVH
    f, t, s = lax.axis_index("fsdp"), lax.axis_index("tp"), lax.axis_index("sub")
    p, r = f // inner, f % inner
    bf16, f32 = jnp.bfloat16, jnp.float32

    def over_fsdp(x, k):
        return lax.ppermute(x, "fsdp", [(i, i ^ k) for i in range(fsdp)])

    def over_sub(x, k):
        return lax.ppermute(x, "sub", [(i, i ^ k) for i in range(sub)])

    slabs = [(0, 0, a_factor)]
    for k in range(1, inner):
        slabs.append((k, 0, over_fsdp(a_factor, k)))
    slabs = slabs + [(k, e, over_sub(a, e)) for k, _, a in slabs for e in range(1, sub)]
    early = [x for x in slabs if x[0] == 0]
    late = [x for x in slabs if x[0] != 0]

    x = inputs.reshape(tokens, wide)
    xs = []
    for k in range(tp):
        pairs = []
        for i in range(fsdp):
            for j in range(tp):
                pairs.append((i * tp + j, (j * inner + i % inner) * tp + (i // inner + k) % tp))
        xs.append(lax.ppermute(x, ("fsdp", "tp"), pairs))

    up = b_factor.transpose(0, 2, 1)[:, None]

    def join(mine, other, bit):
        low = jnp.where(bit == 0, mine, other)
        high = jnp.where(bit == 0, other, mine)
        return jnp.concatenate([low, high], axis=1)

    for axis, size, index in (("sub", sub, s), ("fsdp", fsdp, f)):
        k = 1
        while k < size:
            other = lax.ppermute(up, axis, [(i, i ^ k) for i in range(size)])
            up = join(up, other, (index // k) % 2)
            k = k * 2
    up = up.reshape(2, -1, columns)

    count = group * tokens
    per_head = jax.ShapeDtypeStruct((heads, count, HD), f32)
    query, mixed, top, total = pl.pallas_call(
        functools.partial(cache_kernel, group),
        out_shape=(jax.ShapeDtypeStruct((heads, count, HD), bf16), per_head, per_head, per_head),
        in_specs=[smem(), vmem(), vmem()],
        out_specs=[vmem()] * 4,
        compiler_params=params(),
        name="cached",
    )(lengths, queries, kv_cache)

    def place_of(items):
        return [((r ^ k) * sub + (s ^ e)).astype(jnp.int32) for k, e, _ in items]

    width = 2 * columns + 2 * ranks
    chunk = wide // 4
    part = pl.pallas_call(
        functools.partial(early_kernel, tp),
        out_shape=jax.ShapeDtypeStruct((tp * tokens, width), f32),
        grid_spec=pltpu.PrefetchScalarGridSpec(
            num_scalar_prefetch=1,
            grid=(wide // chunk,),
            in_specs=[
                pl.BlockSpec((2, chunk, columns), lambda i, at: (0, at[0] * (wide // chunk) + i, 0))
            ]
            + [vmem()] * (tp + len(early)),
            out_specs=vmem(),
        ),
        compiler_params=params(),
        name="early",
    )(jnp.stack([p.astype(jnp.int32)] + place_of(early)), base, *xs, *[a for _, _, a in early])

    shift = ((t - p + tp) % tp).astype(jnp.int32)
    parts = pl.pallas_call(
        functools.partial(late_kernel, tp, columns),
        out_shape=[jax.ShapeDtypeStruct((tokens, width), f32 if j == 0 else bf16) for j in range(tp)],
        in_specs=[smem()] + [vmem()] * (1 + tp + len(late)),
        out_specs=[vmem()] * tp,
        compiler_params=params(),
        name="late",
    )(jnp.stack(place_of(late) + [shift]), part, *xs, *[a for _, _, a in late])

    others = []
    for j in range(1, tp):
        pairs = [(i, (i + j * inner) % fsdp) for i in range(fsdp)]
        others.append(lax.ppermute(parts[j], "fsdp", pairs))
    own = pl.pallas_call(
        functools.partial(rank_kernel, columns),
        out_shape=jax.ShapeDtypeStruct((tokens, 2 * ranks), bf16),
        in_specs=[vmem()] * tp,
        out_specs=vmem(),
        compiler_params=params(),
        name="ranks",
    )(parts[0], *others)
    rank_parts = [own]
    for i in range(1, tp):
        rank_parts.append(lax.ppermute(own, "tp", [(j, (j + i) % tp) for j in range(tp)]))
    rank_place = jnp.stack([((t - i + tp) % tp).astype(jnp.int32) for i in range(tp)])

    fresh, attended = pl.pallas_call(
        functools.partial(final_kernel, tp, steps, group),
        out_shape=(
            jax.ShapeDtypeStruct((2, row_count, steps, columns), bf16),
            jax.ShapeDtypeStruct(queries.shape, bf16),
        ),
        in_specs=[smem()] + [vmem()] * (2 * tp + 5),
        out_specs=[vmem(), vmem()],
        compiler_params=params(),
        name="final",
    )(rank_place, parts[0], *others, *rank_parts, up, query, mixed, top, total)
    return fresh, attended


def solution(mesh):
    sizes = tuple(mesh.shape[axis] for axis in ("fsdp", "tp", "sub"))
    return jax.shard_map(
        functools.partial(local, sizes),
        mesh=mesh,
        in_specs=(
            P(("groups", "fsdp", "sub"), None, "tp"),
            P(("groups", "fsdp", "sub"), None, "tp"),
            P(None, ("groups", "fsdp", "sub"), None, "tp"),
            P(("groups", "fsdp", "sub")),
            P(None, None, "tp"),
            P(None, "tp", ("fsdp", "sub")),
            P(None, "tp", ("fsdp", "sub")),
        ),
        out_specs=(
            P(None, ("groups", "fsdp", "sub"), None, "tp"),
            P(("groups", "fsdp", "sub"), None, "tp"),
        ),
        check_vma=False,
    )
```

time: 133 us -> 48.8 us (0.37)
  waiting for transfers between devices: 83.2 us -> 18.4 us
  blocking collectives: 22.2 us -> 0 us
  between operations: 14.1 us -> 0.72 us
  starting transfers between devices: 0.08 us -> 13.3 us
  matrix products: 9.03 us -> 0 us
  Pallas kernels: 0 us -> 6.92 us
  local copies, waits for them, and re-layouts: 4.06 us -> 8.1 us
    all_gather x2 -> x0, waiting for transfers between devices: 82.5 us -> none  [the longest x1 72.9 us: local(): merged = lax.all_gather(own_rows, ('fsdp', 'sub'), axis=1, tiled=True)]
    all_gather x2 -> x0, blocking collectives: 22.2 us -> none  [the longest x1 16.1 us: local(): up_rows = lax.all_gather(b_factor, ('fsdp', 'sub'), axis=2, tiled=True)]
    ppermute x0 -> x10, waiting for transfers between devices: none -> 18.4 us  [the longest x1 10.1 us: over_fsdp(): return lax.ppermute(x, 'fsdp', [(i, i ^ k) for i in range(fsdp)])]
    ppermute x0 -> x10, starting transfers between devices: none -> 13.3 us  [the longest x2 6.01 us: local(): xs.append(lax.ppermute(x, ('fsdp', 'tp'), pairs))]
    dot_general x6 -> x0, matrix products: 9.03 us -> none  [the longest x1 4.57 us: project(): jnp.einsum('td,mdc->mtc', tokens, merged, preferred_element_type=jnp.floa...]
    pallas_call x0 -> x5, Pallas kernels: none -> 6.92 us  [the longest x1 2.46 us: local(): pl.pallas_call(functools.partial(early_kernel, tp), out_shape=jax.ShapeDt...]
    unnamed x4 -> x10, local copies, waits for them, and re-layouts: 0.41 us -> 7.14 us
    slice x2 -> x0, local copies, waits for them, and re-layouts: 1.39 us -> none  [the longest x1 1.38 us: attend(): values_old = kv_cache[1].reshape(rows, cached, heads_kv, HD)]
  transfers between devices with their start and end apart: 2 -> 10, of which waited for: 2 -> 4; matrix products, arithmetic and copies ran while one was open for 2% -> 4% of each run, Pallas kernels for 0% -> 10%
where the time goes in v1:
time: 48.8 us; the launch traced here: 48.4 us
  waiting for transfers between devices  18.4 us (38%)
  starting transfers between devices  13.3 us (27%)
  local copies, waits for them, and re-layouts  8.1 us (17%)
  Pallas kernels  6.92 us (14%)
  other arithmetic  1.08 us (2%)
  between operations  0.72 us (1%)
    ppermute x1, waiting for transfers between devices, over_fsdp(): return lax.ppermute(x, 'fsdp', [(i, i ^ k) for i in range(fsdp)])  10.1 us
    unnamed x10, local copies, waits for them, and re-layouts  7.14 us
    ppermute x2, starting transfers between devices, local(): xs.append(lax.ppermute(x, ('fsdp', 'tp'), pairs))  6.01 us
    ppermute x1, waiting for transfers between devices, local(): others.append(lax.ppermute(parts[j], 'fsdp', pairs))  4.52 us
    ppermute x3, starting transfers between devices, local(): other = lax.ppermute(up, axis, [(i, i ^ k) for i in range(size)])  3.33 us
    ppermute x1, starting transfers between devices, over_fsdp(): return lax.ppermute(x, 'fsdp', [(i, i ^ k) for i in range(fsdp)])  3.09 us
    ppermute x1, waiting for transfers between devices, local(): lax.ppermute(own, 'tp', [(j, (j + i) % tp) for j in range(tp)])  3.01 us
    pallas_call x1, Pallas kernels, local(): pl.pallas_call(functools.partial(early_kernel, tp), out_shape=jax.ShapeDt...  2.46 us
  transfers between devices with their start and end apart: 10, of which 4 were waited for; matrix products, arithmetic and copies ran while one was open for 4% of the time, Pallas kernels for 10%

profile of v1, /device:TPU:0, one launch (start us, length us, event | category | flops | bytes accessed | tf_op | source)
XLA Modules:
  0.0 48.4 jit_solution(17942547890273031649)
XLA Ops:
  0.6 3.1 %collective-permute-start.3 = (bf16[2,128,1024]{2,1,0:T(8,128)(2,1)}, bf16[2,128,1024]{2,1,0:T(8,128)(2,1)S(1)}, u32[]{:S(2)}, u32[]{:S(2)}) collective-permute-start(bf16[2,128,1024]{2,1,0:T(8,128)(2,1)} %refs_2_.1), channel_id=1, source_target_pairs={{0,4},{4,0},{8,12},{12,8},{1,5},{5,1},{9,13},{13,9},{2,6},{6,2},{1... | collective-permute-start | bytes 1572872 | tf_op jit(solution)/shard_map/ppermute | solution.py:178
  3.7 0.0 collective-permute-start.7
  3.7 0.9 %reshape.10 = bf16[16,4096]{1,0:T(8,128)(2,1)S(1)} reshape(bf16[4,4,4096]{2,1,0:T(4,128)(2,1)} %param.7) | data formatting | bytes 262144 | tf_op jit(solution)/shard_map/reshape | solution.py:190
  4.7 0.7 %collective-permute-start = (bf16[16,4096]{1,0:T(8,128)(2,1)S(1)}, bf16[16,4096]{1,0:T(8,128)(2,1)S(1)}, u32[]{:S(2)}, u32[]{:S(2)}) collective-permute-start(bf16[16,4096]{1,0:T(8,128)(2,1)S(1)} %reshape.10), channel_id=1, source_target_pairs={{0,0},{2,8},{4,4},{6,12},{8,2},{10,10},{12,6},{14,14},{1,1},{3,9},... | collective-permute-start | bytes 393224 | tf_op jit(solution)/shard_map/ppermute | solution.py:197
  5.3 5.3 %collective-permute-start.1 = (bf16[16,4096]{1,0:T(8,128)(2,1)S(1)}, bf16[16,4096]{1,0:T(8,128)(2,1)S(1)}, u32[]{:S(2)}, u32[]{:S(2)}) collective-permute-start(bf16[16,4096]{1,0:T(8,128)(2,1)S(1)} %reshape.10), channel_id=1, source_target_pairs={{0,2},{2,10},{4,6},{6,14},{8,0},{10,8},{12,4},{14,12},{1,3},{3,11}... | collective-permute-start | bytes 393224 | tf_op jit(solution)/shard_map/ppermute | solution.py:197
  10.7 0.0 collective-permute-start.2
  10.7 0.0 collective-permute-done.7
  10.7 0.8 %broadcast_select_fusion.5 = (bf16[2,1,32,256]{3,2,0,1:T(8,128)(2,1)S(1)}, bf16[2,1,32,256]{3,2,0,1:T(8,128)(2,1)S(1)}) fusion(bf16[2,1,32,256]{3,2,0,1:T(8,128)(2,1)S(1)} %collective-permute-done.7, pred[]{:T(512)S(6)} %eq.22, bf16[2,256,32]{1,2,0:T(8,128)(2,1)} %param.13), kind=kLoop, calls=%fused_computation.8 | loop fusion | flops 32768 | bytes 131073 | tf_op jit(solution)/shard_map/jit(_where)/select_n | solution.py:202
  11.5 0.5 %collective-permute-start.8 = (bf16[2,2,32,256]{3,2,0,1:T(8,128)(2,1)S(1)}, bf16[2,2,32,256]{3,2,0,1:T(8,128)(2,1)S(1)}, u32[]{:S(2)}, u32[]{:S(2)}) collective-permute-start(bf16[2,2,32,256]{3,2,0,1:T(8,128)(2,1)S(1)} %pad_maximum_fusion.2), channel_id=1, source_target_pairs={{0,4},{4,0},{8,12},{12,8},{1,5},{5,1},{9,13},{13,9},{2,6},{6,2},{1... | collective-permute-start | bytes 196616 | tf_op jit(solution)/shard_map/ppermute | solution.py:209
  12.0 0.1 pad_add_fusion.place_ref
  12.1 10.1 %collective-permute-done.3.refs_2_ = bf16[2,128,1024]{2,1,0:T(8,128)(2,1)S(1)} collective-permute-done((bf16[2,128,1024]{2,1,0:T(8,128)(2,1)}, bf16[2,128,1024]{2,1,0:T(8,128)(2,1)S(1)}, u32[]{:S(2)}, u32[]{:S(2)}) %collective-permute-start.3) | collective-permute-done | bytes 524320 | tf_op jit(solution)/shard_map/ppermute | solution.py:178
  22.2 0.0 collective-permute-start.4
  22.2 0.7 %collective-permute-done.8 = bf16[2,2,32,256]{3,2,0,1:T(8,128)(2,1)S(1)} collective-permute-done((bf16[2,2,32,256]{3,2,0,1:T(8,128)(2,1)S(1)}, bf16[2,2,32,256]{3,2,0,1:T(8,128)(2,1)S(1)}, u32[]{:S(2)}, u32[]{:S(2)}) %collective-permute-start.8) | collective-permute-done | bytes 65568 | tf_op jit(solution)/shard_map/ppermute | solution.py:209
  22.9 2.8 %collective-permute-start.9 = (bf16[2,4,32,256]{3,2,0,1:T(8,128)(2,1)S(1)}, bf16[2,4,32,256]{3,2,0,1:T(8,128)(2,1)S(1)}, u32[]{:S(2)}, u32[]{:S(2)}) collective-permute-start(bf16[2,4,32,256]{3,2,0,1:T(8,128)(2,1)S(1)} %pad_maximum_fusion.1), channel_id=1, source_target_pairs={{0,8},{4,12},{8,0},{12,4},{1,9},{5,13},{9,1},{13,5},{2,10},{6,14},... | collective-permute-start | bytes 393224 | tf_op jit(solution)/shard_map/ppermute | solution.py:209
  25.7 0.1 pad_add_fusion.1.place_ref
  25.8 0.0 copy-start.1
  25.8 1.2 %copy-done.1 = bf16[2,4,256,256]{3,2,1,0:T(8,128)(2,1)S(1)} copy-done((bf16[2,4,256,256]{3,2,1,0:T(8,128)(2,1)S(1)}, bf16[2,4,256,256]{3,2,1,0:T(8,128)(2,1)}, u32[]{:S(2)}) %copy-start.1) | copy-done | bytes 1048600
  27.0 0.0 copy-start.3
  27.0 0.8 %copy-done.3 = bf16[4,4,2048]{2,1,0:T(4,128)(2,1)S(1)} copy-done((bf16[4,4,2048]{2,1,0:T(4,128)(2,1)S(1)}, bf16[4,4,2048]{2,1,0:T(4,128)(2,1)}, u32[]{:S(2)}) %copy-start.3) | copy-done | bytes 65560
  27.9 0.0 copy-start.4
  27.9 0.7 %copy-done.4 = s32[4]{0:T(128)S(1)} copy-done((s32[4]{0:T(128)S(1)}, s32[4]{0:T(128)}, u32[]{:S(2)}) %copy-start.4) | copy-done | bytes 40
  28.5 1.5 %cached.1 = (bf16[2,128,128]{2,1,0:T(8,128)(2,1)S(1)}, f32[2,128,128]{2,1,0:T(8,128)S(1)}, f32[2,128,128]{2,1,0:T(8,128)S(1)}, f32[2,128,128]{2,1,0:T(8,128)S(1)}) custom-call(s32[4]{0:T(128)S(1)} %copy-done.4, bf16[4,4,2048]{2,1,0:T(4,128)(2,1)S(1)} %copy-done.3, bf16[2,4,256,256]{3,2,1,0:T(8,128)(2,1)S(1)} %copy-done.1), custom_call_target="tpu_custom_call" | custom-call | tf_op jit(solution)/shard_map/cached/pallas_call | solution.py:216
  30.1 0.1 pad_add_fusion.2.place_ref
  30.2 0.0 collective-permute-done.refs_0_
  30.2 0.0 collective-permute-done.1.refs_1_
  30.2 0.0 collective-permute-done.2.refs_3_
  30.2 0.0 copy-start
  30.2 3.4 %copy-done = bf16[2,8192,256]{2,1,0:T(8,128)(2,1)S(1)} copy-done((bf16[2,8192,256]{2,1,0:T(8,128)(2,1)S(1)}, bf16[2,8192,256]{2,1,0:T(8,128)(2,1)}, u32[]{:S(2)}) %copy-start) | copy-done | bytes 8388632
  33.6 0.0 copy-start.2
  33.6 1.0 %copy-done.2 = bf16[2,128,1024]{2,1,0:T(8,128)(2,1)S(1)} copy-done((bf16[2,128,1024]{2,1,0:T(8,128)(2,1)S(1)}, bf16[2,128,1024]{2,1,0:T(8,128)(2,1)}, u32[]{:S(2)}) %copy-start.2) | copy-done | bytes 524312
  34.6 2.5 %early.1.part_ref = f32[32,768]{1,0:T(8,128)S(1)} custom-call(s32[3]{0:T(128)S(1)} %pad_add_fusion.2.place_ref, bf16[2,8192,256]{2,1,0:T(8,128)(2,1)S(1)} %copy-done, bf16[16,4096]{1,0:T(8,128)(2,1)S(1)} %collective-permute-done.refs_0_, bf16[16,4096]{1,0:T(8,128)(2,1)S(1)} %collective-permute-done.1.refs_1_, bf16[2,128,1024]{2,1,0:T(8,128)(2,1)S(1)} %copy-done.2, ...), custom_call_target="tpu_custom_call" | custom-call | tf_op jit(solution)/shard_map/early/pallas_call | solution.py:230
  37.1 0.0 collective-permute-done.4.refs_3_
  37.1 1.0 %late.1 = (f32[16,768]{1,0:T(8,128)S(1)}, bf16[16,768]{1,0:T(8,128)(2,1)S(1)}) custom-call(s32[3]{0:T(128)S(1)} %pad_add_fusion.1.place_ref, f32[32,768]{1,0:T(8,128)S(1)} %early.1.part_ref, bf16[16,4096]{1,0:T(8,128)(2,1)S(1)} %collective-permute-done.refs_0_, bf16[16,4096]{1,0:T(8,128)(2,1)S(1)} %collective-permute-done.1.refs_1_, ...), custom_call_target="tpu_custom_call" | custom-call | tf_op jit(solution)/shard_map/late/pallas_call | solution.py:247
  38.1 0.2 collective-permute-start.5
  38.3 0.0 collective-permute-done.9
  38.4 4.5 %collective-permute-done.5.refs_0_ = bf16[16,768]{1,0:T(8,128)(2,1)S(1)} collective-permute-done((bf16[16,768]{1,0:T(8,128)(2,1)S(1)}, bf16[16,768]{1,0:T(8,128)(2,1)S(1)}, u32[]{:S(2)}, u32[]{:S(2)}) %collective-permute-start.5) | collective-permute-done | bytes 24608 | tf_op jit(solution)/shard_map/ppermute | solution.py:259
  42.9 0.6 %collective-permute-start.6 = (bf16[16,256]{1,0:T(8,128)(2,1)S(1)}, bf16[16,256]{1,0:T(8,128)(2,1)S(1)}, u32[]{:S(2)}, u32[]{:S(2)}) collective-permute-start(bf16[16,256]{1,0:T(8,128)(2,1)S(1)} %ranks.1.refs_1_), channel_id=1, source_target_pairs={{0,2},{2,0},{1,3},{3,1},{4,6},{6,4},{5,7},{7,5},{8,10},{10,8},{9,1... | collective-permute-start | bytes 24584 | tf_op jit(solution)/shard_map/ppermute | solution.py:270
  43.5 3.0 %collective-permute-done.6.refs_2_ = bf16[16,256]{1,0:T(8,128)(2,1)S(1)} collective-permute-done((bf16[16,256]{1,0:T(8,128)(2,1)S(1)}, bf16[16,256]{1,0:T(8,128)(2,1)S(1)}, u32[]{:S(2)}, u32[]{:S(2)}) %collective-permute-start.6) | collective-permute-done | bytes 8224 | tf_op jit(solution)/shard_map/ppermute | solution.py:270
  46.5 1.9 %final.1 = (bf16[2,4,4,256]{3,2,1,0:T(4,128)(2,1)}, bf16[4,4,2048]{2,1,0:T(4,128)(2,1)}) custom-call(s32[2]{0:T(128)S(1)} %pad_add_fusion.place_ref, f32[16,768]{1,0:T(8,128)S(1)} %get-tuple-element.8.mine_ref, bf16[16,768]{1,0:T(8,128)(2,1)S(1)} %collective-permute-done.5.refs_0_, bf16[16,256]{1,0:T(8,128)(2,1)S(1)} %ranks.1.refs_1_, ...), custom_call_target="tpu_custom_call" | custom-call | tf_op jit(solution)/shard_map/final/pallas_call | solution.py:273
  (7 shorter events, 0.1 us)
Async XLA Ops:
  0.6 21.5 %collective-permute-start.3 = (bf16[2,128,1024]{2,1,0:T(8,128)(2,1)}, bf16[2,128,1024]{2,1,0:T(8,128)(2,1)S(1)}, u32[]{:S(2)}, u32[]{:S(2)}) collective-permute-start(bf16[2,128,1024]{2,1,0:T(8,128)(2,1)} %refs_2_.1), channel_id=1, source_target_pairs={{0,4},{4,0},{8,12},{12,8},{1,5},{5,1},{9,13},{13,9},{2,6},{6,2},{1... | collective-permute-start | bytes 1572872 | tf_op jit(solution)/shard_map/ppermute | solution.py:178
  3.7 7.0 %collective-permute-start.7 = (bf16[2,1,32,256]{3,2,0,1:T(8,128)(2,1)}, bf16[2,1,32,256]{3,2,0,1:T(8,128)(2,1)S(1)}, u32[]{:S(2)}, u32[]{:S(2)}) collective-permute-start(bf16[2,1,32,256]{3,2,0,1:T(8,128)(2,1)} %bitcast.15), channel_id=1, source_target_pairs={{0,1},{1,0},{2,3},{3,2},{4,5},{5,4},{6,7},{7,6},{8,9},{9,8},{10,11... | collective-permute-start | bytes 98312 | tf_op jit(solution)/shard_map/ppermute | solution.py:209
  4.7 25.5 %collective-permute-start = (bf16[16,4096]{1,0:T(8,128)(2,1)S(1)}, bf16[16,4096]{1,0:T(8,128)(2,1)S(1)}, u32[]{:S(2)}, u32[]{:S(2)}) collective-permute-start(bf16[16,4096]{1,0:T(8,128)(2,1)S(1)} %reshape.10), channel_id=1, source_target_pairs={{0,0},{2,8},{4,4},{6,12},{8,2},{10,10},{12,6},{14,14},{1,1},{3,9},... | collective-permute-start | bytes 393224 | tf_op jit(solution)/shard_map/ppermute | solution.py:197
  5.3 24.8 %collective-permute-start.1 = (bf16[16,4096]{1,0:T(8,128)(2,1)S(1)}, bf16[16,4096]{1,0:T(8,128)(2,1)S(1)}, u32[]{:S(2)}, u32[]{:S(2)}) collective-permute-start(bf16[16,4096]{1,0:T(8,128)(2,1)S(1)} %reshape.10), channel_id=1, source_target_pairs={{0,2},{2,10},{4,6},{6,14},{8,0},{10,8},{12,4},{14,12},{1,3},{3,11}... | collective-permute-start | bytes 393224 | tf_op jit(solution)/shard_map/ppermute | solution.py:197
  10.7 19.5 %collective-permute-start.2 = (bf16[2,128,1024]{2,1,0:T(8,128)(2,1)}, bf16[2,128,1024]{2,1,0:T(8,128)(2,1)S(1)}, u32[]{:S(2)}, u32[]{:S(2)}) collective-permute-start(bf16[2,128,1024]{2,1,0:T(8,128)(2,1)} %refs_2_.1), channel_id=1, source_target_pairs={{0,1},{1,0},{2,3},{3,2},{4,5},{5,4},{6,7},{7,6},{8,9},{9,8},{10,11... | collective-permute-start | bytes 1572872 | tf_op jit(solution)/shard_map/ppermute | solution.py:181
  11.5 11.4 %collective-permute-start.8 = (bf16[2,2,32,256]{3,2,0,1:T(8,128)(2,1)S(1)}, bf16[2,2,32,256]{3,2,0,1:T(8,128)(2,1)S(1)}, u32[]{:S(2)}, u32[]{:S(2)}) collective-permute-start(bf16[2,2,32,256]{3,2,0,1:T(8,128)(2,1)S(1)} %pad_maximum_fusion.2), channel_id=1, source_target_pairs={{0,4},{4,0},{8,12},{12,8},{1,5},{5,1},{9,13},{13,9},{2,6},{6,2},{1... | collective-permute-start | bytes 196616 | tf_op jit(solution)/shard_map/ppermute | solution.py:209
  22.2 14.9 %collective-permute-start.4 = (bf16[2,128,1024]{2,1,0:T(8,128)(2,1)S(1)}, bf16[2,128,1024]{2,1,0:T(8,128)(2,1)S(1)}, u32[]{:S(2)}, u32[]{:S(2)}) collective-permute-start(bf16[2,128,1024]{2,1,0:T(8,128)(2,1)S(1)} %collective-permute-done.3.refs_2_), channel_id=1, source_target_pairs={{0,1},{1,0},{2,3},{3,2},{4,5},{5,4},{6,7},{7,6},{8,9},{9,8},{10,11... | collective-permute-start | bytes 1572872 | tf_op jit(solution)/shard_map/ppermute | solution.py:181
  22.9 15.4 %collective-permute-start.9 = (bf16[2,4,32,256]{3,2,0,1:T(8,128)(2,1)S(1)}, bf16[2,4,32,256]{3,2,0,1:T(8,128)(2,1)S(1)}, u32[]{:S(2)}, u32[]{:S(2)}) collective-permute-start(bf16[2,4,32,256]{3,2,0,1:T(8,128)(2,1)S(1)} %pad_maximum_fusion.1), channel_id=1, source_target_pairs={{0,8},{4,12},{8,0},{12,4},{1,9},{5,13},{9,1},{13,5},{2,10},{6,14},... | collective-permute-start | bytes 393224 | tf_op jit(solution)/shard_map/ppermute | solution.py:209
  25.8 1.2 %copy-start.1 = (bf16[2,4,256,256]{3,2,1,0:T(8,128)(2,1)S(1)}, bf16[2,4,256,256]{3,2,1,0:T(8,128)(2,1)}, u32[]{:S(2)}) copy-start(bf16[2,4,256,256]{3,2,1,0:T(8,128)(2,1)} %kv_ref.1) | copy-start | bytes 3145732
  27.0 0.8 %copy-start.3 = (bf16[4,4,2048]{2,1,0:T(4,128)(2,1)S(1)}, bf16[4,4,2048]{2,1,0:T(4,128)(2,1)}, u32[]{:S(2)}) copy-start(bf16[4,4,2048]{2,1,0:T(4,128)(2,1)} %q_ref.1) | copy-start | bytes 196612
  27.9 0.7 %copy-start.4 = (s32[4]{0:T(128)S(1)}, s32[4]{0:T(128)}, u32[]{:S(2)}) copy-start(s32[4]{0:T(128)} %len_ref.1) | copy-start | bytes 52
  30.2 3.4 %copy-start = (bf16[2,8192,256]{2,1,0:T(8,128)(2,1)S(1)}, bf16[2,8192,256]{2,1,0:T(8,128)(2,1)}, u32[]{:S(2)}) copy-start(bf16[2,8192,256]{2,1,0:T(8,128)(2,1)} %base_ref.1) | copy-start | bytes 25165828
  33.6 1.0 %copy-start.2 = (bf16[2,128,1024]{2,1,0:T(8,128)(2,1)S(1)}, bf16[2,128,1024]{2,1,0:T(8,128)(2,1)}, u32[]{:S(2)}) copy-start(bf16[2,128,1024]{2,1,0:T(8,128)(2,1)} %refs_2_.1) | copy-start | bytes 1572868
  38.1 4.8 %collective-permute-start.5 = (bf16[16,768]{1,0:T(8,128)(2,1)S(1)}, bf16[16,768]{1,0:T(8,128)(2,1)S(1)}, u32[]{:S(2)}, u32[]{:S(2)}) collective-permute-start(bf16[16,768]{1,0:T(8,128)(2,1)S(1)} %get-tuple-element.9), channel_id=1, source_target_pairs={{0,8},{4,12},{8,0},{12,4},{1,9},{5,13},{9,1},{13,5},{2,10},{6,14},... | collective-permute-start | bytes 73736 | tf_op jit(solution)/shard_map/ppermute | solution.py:259
  42.9 3.7 %collective-permute-start.6 = (bf16[16,256]{1,0:T(8,128)(2,1)S(1)}, bf16[16,256]{1,0:T(8,128)(2,1)S(1)}, u32[]{:S(2)}, u32[]{:S(2)}) collective-permute-start(bf16[16,256]{1,0:T(8,128)(2,1)S(1)} %ranks.1.refs_1_), channel_id=1, source_target_pairs={{0,2},{2,0},{1,3},{3,1},{4,6},{6,4},{5,7},{7,5},{8,10},{10,8},{9,1... | collective-permute-start | bytes 24584 | tf_op jit(solution)/shard_map/ppermute | solution.py:270

commit v2 on v1

--- a/solution.py
+++ b/solution.py
@@ -11,7 +11,6 @@
 KVH = 4
 QH = 32
 NEG = -1e30
-VMEM_LIMIT = 40 * 2**20
 
 NT = (((1,), (1,)), ((), ()))
 NN = (((1,), (0,)), ((), ()))
@@ -25,11 +24,28 @@
     return pl.BlockSpec(memory_space=pltpu.VMEM)
 
 
-def params():
-    return pltpu.CompilerParams(vmem_limit_bytes=VMEM_LIMIT)
-
-
-def cache_kernel(group, len_ref, q_ref, kv_ref, q_out, acc_out, top_out, sum_out):
+def params(mib=40):
+    return pltpu.CompilerParams(vmem_limit_bytes=mib * 2**20)
+
+
+def cache_kernel(
+    group, len_ref, place_ref, q_hbm, kv_hbm, base_hbm, a_hbm,
+    q_out, acc_out, top_out, sum_out, base_out, a_out, q_ref, kv_ref, sems,
+):
+    wide = base_out.shape[1]
+    start = pl.multiple_of(place_ref[0] * wide, wide)
+    copies = [
+        pltpu.make_async_copy(q_hbm, q_ref, sems.at[0]),
+        pltpu.make_async_copy(kv_hbm.at[0], kv_ref.at[0], sems.at[1]),
+        pltpu.make_async_copy(kv_hbm.at[1], kv_ref.at[1], sems.at[2]),
+        pltpu.make_async_copy(a_hbm, a_out, sems.at[3]),
+        pltpu.make_async_copy(base_hbm.at[0, pl.ds(start, wide)], base_out.at[0], sems.at[4]),
+        pltpu.make_async_copy(base_hbm.at[1, pl.ds(start, wide)], base_out.at[1], sems.at[5]),
+    ]
+    for copy in copies:
+        copy.start()
+    for copy in copies[:3]:
+        copy.wait()
     rows, steps, width = q_ref.shape
     heads, cached = width // (group * HD), kv_ref.shape[2]
     tokens = rows * steps
@@ -64,44 +80,38 @@
         acc_out[g] = mixed
         top_out[g] = jnp.broadcast_to(top, (count, HD))
         sum_out[g] = jnp.broadcast_to(total, (count, HD))
+    for copy in copies[3:]:
+        copy.wait()
 
 
 def early_kernel(blocks, place_ref, base_ref, *refs):
-    x_refs, a_refs, out_ref = refs[:blocks], refs[blocks:-1], refs[-1]
-    step, width, columns = pl.program_id(0), base_ref.shape[1], base_ref.shape[2]
-    tokens, slab, ranks = x_refs[0].shape[0], a_refs[0].shape[2], a_refs[0].shape[1]
-
-    def stacked(start, size):
-        return jnp.concatenate([x[:, pl.ds(start, size)] for x in x_refs], axis=0)
-
-    @pl.when(step == 0)
-    def _():
-        for m in range(2):
-            total = jnp.zeros((blocks * tokens, ranks), jnp.float32)
-            for i, a in enumerate(a_refs):
-                start = pl.multiple_of(place_ref[1 + i] * slab, slab)
-                total = total + dot(stacked(start, slab), a[m], NT)
-            out_ref[:, 2 * columns + m * ranks : 2 * columns + (m + 1) * ranks] = total
-        out_ref[:, : 2 * columns] = jnp.zeros((blocks * tokens, 2 * columns), jnp.float32)
-
-    x = stacked(pl.multiple_of(step * width, width), width)
+    x_refs, a_refs = refs[:blocks], refs[blocks:-2]
+    out_ref, x_out = refs[-2:]
+    columns, slab, ranks = base_ref.shape[2], a_refs[0].shape[2], a_refs[0].shape[1]
+    rows, steps, wide = x_refs[0].shape
+    for k, x_ref in enumerate(x_refs):
+        x = jnp.concatenate([x_ref[b].astype(jnp.float32) for b in range(rows)], axis=0)
+        x_out[k * rows * steps : (k + 1) * rows * steps] = x.astype(jnp.bfloat16)
+    count = blocks * rows * steps
     for m in range(2):
-        cols = slice(m * columns, (m + 1) * columns)
-        out_ref[:, cols] = out_ref[:, cols] + dot(x, base_ref[m])
-
-
-def late_kernel(blocks, columns, place_ref, part_ref, *refs):
-    x_refs, outs = refs[:blocks], refs[-blocks:]
-    a_refs = refs[blocks:-blocks]
-    tokens, slab, ranks = x_refs[0].shape[0], a_refs[0].shape[2], a_refs[0].shape[1]
-    acc = part_ref.shape[1]
+        out_ref[:, m * columns : (m + 1) * columns] = dot(x_out[...], base_ref[m])
+        total = jnp.zeros((count, ranks), jnp.float32)
+        for i, a in enumerate(a_refs):
+            start = pl.multiple_of(place_ref[i] * slab, slab)
+            total = total + dot(x_out[:, pl.ds(start, slab)], a[m], NT)
+        out_ref[:, 2 * columns + m * ranks : 2 * columns + (m + 1) * ranks] = total
+
+
+def late_kernel(blocks, columns, place_ref, part_ref, x_ref, *refs):
+    a_refs, outs = refs[:-blocks], refs[-blocks:]
+    tokens, acc = outs[0].shape
+    slab, ranks = a_refs[0].shape[2], a_refs[0].shape[1]
     sums = [part_ref[:, : 2 * columns]]
     for m in range(2):
         total = part_ref[:, 2 * columns + m * ranks : 2 * columns + (m + 1) * ranks]
         for i, a in enumerate(a_refs):
             start = pl.multiple_of(place_ref[i] * slab, slab)
-            x = jnp.concatenate([x[:, pl.ds(start, slab)] for x in x_refs], axis=0)
-            total = total + dot(x, a[m], NT)
+            total = total + dot(x_ref[:, pl.ds(start, slab)], a[m], NT)
         sums.append(total)
     whole = jnp.concatenate(sums, axis=1)
     shift = place_ref[len(a_refs)]
@@ -180,83 +190,92 @@
     def over_sub(x, k):
         return lax.ppermute(x, "sub", [(i, i ^ k) for i in range(sub)])
 
-    slabs = [(0, 0, a_factor)]
-    for k in range(1, inner):
-        slabs.append((k, 0, over_fsdp(a_factor, k)))
-    slabs = slabs + [(k, e, over_sub(a, e)) for k, _, a in slabs for e in range(1, sub)]
-    early = [x for x in slabs if x[0] == 0]
-    late = [x for x in slabs if x[0] != 0]
-
-    x = inputs.reshape(tokens, wide)
-    xs = []
-    for k in range(tp):
+    def spread(x, k):
         pairs = []
         for i in range(fsdp):
             for j in range(tp):
                 pairs.append((i * tp + j, (j * inner + i % inner) * tp + (i // inner + k) % tp))
-        xs.append(lax.ppermute(x, ("fsdp", "tp"), pairs))
-
-    up = b_factor.transpose(0, 2, 1)[:, None]
+        return lax.ppermute(x, ("fsdp", "tp"), pairs)
+
+    xs = [None] + [spread(inputs, k) for k in range(1, tp)]
+    far = [over_fsdp(a_factor, k) for k in range(1, inner)]
+    near = [(0, e, over_sub(a_factor, e)) for e in range(1, sub)]
+    xs[0] = spread(inputs, 0)
 
     def join(mine, other, bit):
         low = jnp.where(bit == 0, mine, other)
         high = jnp.where(bit == 0, other, mine)
         return jnp.concatenate([low, high], axis=1)
 
-    for axis, size, index in (("sub", sub, s), ("fsdp", fsdp, f)):
-        k = 1
-        while k < size:
-            other = lax.ppermute(up, axis, [(i, i ^ k) for i in range(size)])
-            up = join(up, other, (index // k) % 2)
-            k = k * 2
-    up = up.reshape(2, -1, columns)
+    def gather(x, axis, index, start, stop):
+        size = {"fsdp": fsdp, "sub": sub}[axis]
+        while start < stop:
+            other = lax.ppermute(x, axis, [(i, i ^ start) for i in range(size)])
+            x = join(x, other, (index // start) % 2)
+            start = start * 2
+        return x
+
+    up = gather(b_factor.transpose(0, 2, 1)[:, None], "fsdp", f, 1, inner)
 
     count = group * tokens
     per_head = jax.ShapeDtypeStruct((heads, count, HD), f32)
-    query, mixed, top, total = pl.pallas_call(
+    *state, rows_base, near_a = pl.pallas_call(
         functools.partial(cache_kernel, group),
-        out_shape=(jax.ShapeDtypeStruct((heads, count, HD), bf16), per_head, per_head, per_head),
-        in_specs=[smem(), vmem(), vmem()],
-        out_specs=[vmem()] * 4,
+        out_shape=[
+            jax.ShapeDtypeStruct((heads, count, HD), bf16),
+            per_head,
+            per_head,
+            per_head,
+            jax.ShapeDtypeStruct((2, wide, columns), bf16),
+            jax.ShapeDtypeStruct(a_factor.shape, bf16),
+        ],
+        in_specs=[smem(), smem()] + [pl.BlockSpec(memory_space=pltpu.HBM)] * 4,
+        out_specs=[vmem()] * 6,
+        scratch_shapes=[
+            pltpu.VMEM(queries.shape, bf16),
+            pltpu.VMEM(kv_cache.shape, bf16),
+            pltpu.SemaphoreType.DMA((6,)),
+        ],
         compiler_params=params(),
         name="cached",
-    )(lengths, queries, kv_cache)
+    )(lengths, p.astype(jnp.int32)[None], queries, kv_cache, base, a_factor)
 
     def place_of(items):
         return [((r ^ k) * sub + (s ^ e)).astype(jnp.int32) for k, e, _ in items]
 
+    xs, near_a = lax.optimization_barrier((xs, near_a))
+    near = [(0, 0, near_a)] + near
     width = 2 * columns + 2 * ranks
-    chunk = wide // 4
-    part = pl.pallas_call(
+    part, x = pl.pallas_call(
         functools.partial(early_kernel, tp),
-        out_shape=jax.ShapeDtypeStruct((tp * tokens, width), f32),
-        grid_spec=pltpu.PrefetchScalarGridSpec(
-            num_scalar_prefetch=1,
-            grid=(wide // chunk,),
-            in_specs=[
-                pl.BlockSpec((2, chunk, columns), lambda i, at: (0, at[0] * (wide // chunk) + i, 0))
-            ]
-            + [vmem()] * (tp + len(early)),
-            out_specs=vmem(),
-        ),
+        out_shape=[
+            jax.ShapeDtypeStruct((tp * tokens, width), f32),
+            jax.ShapeDtypeStruct((tp * tokens, wide), bf16),
+        ],
+        in_specs=[smem()] + [vmem()] * (1 + tp + len(near)),
+        out_specs=[vmem()] * 2,
         compiler_params=params(),
         name="early",
-    )(jnp.stack([p.astype(jnp.int32)] + place_of(early)), base, *xs, *[a for _, _, a in early])
-
+    )(jnp.stack(place_of(near)), rows_base, *xs, *[a for _, _, a in near])
+
+    far, part, up = lax.optimization_barrier((far, part, up))
+    late = [(k, e, over_sub(a, e) if e else a) for k, a in enumerate(far, 1) for e in range(sub)]
     shift = ((t - p + tp) % tp).astype(jnp.int32)
     parts = pl.pallas_call(
         functools.partial(late_kernel, tp, columns),
         out_shape=[jax.ShapeDtypeStruct((tokens, width), f32 if j == 0 else bf16) for j in range(tp)],
-        in_specs=[smem()] + [vmem()] * (1 + tp + len(late)),
+        in_specs=[smem()] + [vmem()] * (2 + len(late)),
         out_specs=[vmem()] * tp,
         compiler_params=params(),
         name="late",
-    )(jnp.stack(place_of(late) + [shift]), part, *xs, *[a for _, _, a in late])
-
+    )(jnp.stack(place_of(late) + [shift]), part, x, *[a for _, _, a in late])
+
+    parts, up = lax.optimization_barrier((parts, up))
     others = []
     for j in range(1, tp):
         pairs = [(i, (i + j * inner) % fsdp) for i in range(fsdp)]
         others.append(lax.ppermute(parts[j], "fsdp", pairs))
+    up = gather(up, "fsdp", f, inner, fsdp)
     own = pl.pallas_call(
         functools.partial(rank_kernel, columns),
         out_shape=jax.ShapeDtypeStruct((tokens, 2 * ranks), bf16),
@@ -265,6 +284,9 @@
         compiler_params=params(),
         name="ranks",
     )(parts[0], *others)
+    own, up = lax.optimization_barrier((own, up))
+    up = gather(up, "sub", s, 1, sub)
+    up = up.reshape(2, sub, fsdp, -1, columns).swapaxes(1, 2).reshape(2, -1, columns)
     rank_parts = [own]
     for i in range(1, tp):
         rank_parts.append(lax.ppermute(own, "tp", [(j, (j + i) % tp) for j in range(tp)]))
@@ -280,7 +302,7 @@
         out_specs=[vmem(), vmem()],
         compiler_params=params(),
         name="final",
-    )(rank_place, parts[0], *others, *rank_parts, up, query, mixed, top, total)
+    )(rank_place, parts[0], *others, *rank_parts, up, *state)
     return fresh, attended
 
 

time: 48.8 us -> 41.7 us (0.85)
  local copies, waits for them, and re-layouts: 8.1 us -> 3.78 us
  waiting for transfers between devices: 18.4 us -> 15.5 us
  Pallas kernels: 6.92 us -> 7.69 us
  other arithmetic: 1.08 us -> 0.32 us
    ppermute x1, waiting for transfers between devices: 10.1 us -> 0.01 us  [over_fsdp(): return lax.ppermute(x, 'fsdp', [(i, i ^ k) for i in range(fsdp)])]
    ppermute x5, waiting for transfers between devices: 0.71 us -> 6.38 us  [the longest x3 6.38 us: gather(): other = lax.ppermute(x, axis, [(i, i ^ start) for i in range(size)])]
    unnamed x10, local copies, waits for them, and re-layouts: 7.14 us -> 3.76 us
    ppermute x2, waiting for transfers between devices: 0.01 us -> 1.79 us  [over_sub(): return lax.ppermute(x, 'sub', [(i, i ^ k) for i in range(sub)])]
    reshape x1, local copies, waits for them, and re-layouts: 0.94 us -> 0.02 us  [local(): up.reshape(2, sub, fsdp, -1, columns).swapaxes(1, 2).reshape(2, -1, columns)]
    pallas_call x2, Pallas kernels: 4 us -> 4.78 us  [the longest x1 3.01 us: local(): pl.pallas_call(functools.partial(cache_kernel, group), out_shape=[jax.Sha...]
    select_n x3, other arithmetic: 0.8 us -> 0.05 us  [join(): low = jnp.where(bit == 0, mine, other)]
    ppermute x1, waiting for transfers between devices: 3.01 us -> 2.34 us  [local(): lax.ppermute(own, 'tp', [(j, (j + i) % tp) for j in range(tp)])]
  transfers between devices with their start and end apart: 10 -> 10, of which waited for: 4 -> 5; matrix products, arithmetic and copies ran while one was open for 4% -> 1% of each run, Pallas kernels for 10% -> 12%
where the time goes in v2:
time: 41.7 us; the launch traced here: 41.4 us
  waiting for transfers between devices  15.5 us (37%)
  starting transfers between devices  13.4 us (32%)
  Pallas kernels  7.69 us (18%)
  local copies, waits for them, and re-layouts  3.78 us (9%)
  between operations  0.81 us (2%)
    ppermute x3, waiting for transfers between devices, gather(): other = lax.ppermute(x, axis, [(i, i ^ start) for i in range(size)])  6.38 us
    ppermute x2, starting transfers between devices, spread(): return lax.ppermute(x, ('fsdp', 'tp'), pairs)  6.01 us
    ppermute x1, waiting for transfers between devices, local(): others.append(lax.ppermute(parts[j], 'fsdp', pairs))  4.95 us
    unnamed x10, local copies, waits for them, and re-layouts  3.76 us
    ppermute x3, starting transfers between devices, gather(): other = lax.ppermute(x, axis, [(i, i ^ start) for i in range(size)])  3.37 us
    pallas_call x1, Pallas kernels, local(): pl.pallas_call(functools.partial(cache_kernel, group), out_shape=[jax.Sha...  3.01 us
    ppermute x1, starting transfers between devices, over_fsdp(): return lax.ppermute(x, 'fsdp', [(i, i ^ k) for i in range(fsdp)])  2.65 us
    ppermute x1, waiting for transfers between devices, local(): lax.ppermute(own, 'tp', [(j, (j + i) % tp) for j in range(tp)])  2.34 us
  transfers between devices with their start and end apart: 10, of which 5 were waited for; matrix products, arithmetic and copies ran while one was open for 1% of the time, Pallas kernels for 12%

profile of v2, /device:TPU:0, one launch (start us, length us, event | category | flops | bytes accessed | tf_op | source)
XLA Modules:
  0.0 41.4 jit_solution(6796050781327930619)
XLA Ops:
  0.6 0.0 copy-start.4
  0.6 0.5 %collective-permute-start.3 = (bf16[2,128,1024]{2,1,0:T(8,128)(2,1)}, bf16[2,128,1024]{2,1,0:T(8,128)(2,1)S(1)}, u32[]{:S(2)}, u32[]{:S(2)}) collective-permute-start(bf16[2,128,1024]{2,1,0:T(8,128)(2,1)} %a_hbm.1), channel_id=1, source_target_pairs={{0,1},{1,0},{2,3},{3,2},{4,5},{5,4},{6,7},{7,6},{8,9},{9,8},{10,11... | collective-permute-start | bytes 1572872 | tf_op jit(solution)/shard_map/ppermute | solution.py:191
  1.2 2.7 %collective-permute-start = (bf16[2,128,1024]{2,1,0:T(8,128)(2,1)}, bf16[2,128,1024]{2,1,0:T(8,128)(2,1)S(1)}, u32[]{:S(2)}, u32[]{:S(2)}) collective-permute-start(bf16[2,128,1024]{2,1,0:T(8,128)(2,1)} %a_hbm.1), channel_id=1, source_target_pairs={{0,4},{4,0},{8,12},{12,8},{1,5},{5,1},{9,13},{13,9},{2,6},{6,2},{1... | collective-permute-start | bytes 1572872 | tf_op jit(solution)/shard_map/ppermute | solution.py:188
  3.8 1.6 %collective-permute-start.1 = (bf16[4,4,4096]{2,1,0:T(4,128)(2,1)}, bf16[4,4,4096]{2,1,0:T(4,128)(2,1)S(1)}, u32[]{:S(2)}, u32[]{:S(2)}) collective-permute-start(bf16[4,4,4096]{2,1,0:T(4,128)(2,1)} %param.7), channel_id=1, source_target_pairs={{0,0},{2,8},{4,4},{6,12},{8,2},{10,10},{12,6},{14,14},{1,1},{3,9},... | collective-permute-start | bytes 393224 | tf_op jit(solution)/shard_map/ppermute | solution.py:198
  5.4 4.5 %collective-permute-start.2 = (bf16[4,4,4096]{2,1,0:T(4,128)(2,1)}, bf16[4,4,4096]{2,1,0:T(4,128)(2,1)S(1)}, u32[]{:S(2)}, u32[]{:S(2)}) collective-permute-start(bf16[4,4,4096]{2,1,0:T(4,128)(2,1)} %param.7), channel_id=1, source_target_pairs={{0,2},{2,10},{4,6},{6,14},{8,0},{10,8},{12,4},{14,12},{1,3},{3,11}... | collective-permute-start | bytes 393224 | tf_op jit(solution)/shard_map/ppermute | solution.py:198
  9.8 0.4 %collective-permute-start.4 = (bf16[2,1,32,256]{3,2,0,1:T(8,128)(2,1)}, bf16[2,1,32,256]{3,2,0,1:T(8,128)(2,1)S(1)}, u32[]{:S(2)}, u32[]{:S(2)}) collective-permute-start(bf16[2,1,32,256]{3,2,0,1:T(8,128)(2,1)} %bitcast.19), channel_id=1, source_target_pairs={{0,4},{4,0},{8,12},{12,8},{1,5},{5,1},{9,13},{13,9},{2,6},{6,2},{1... | collective-permute-start | bytes 98312 | tf_op jit(solution)/shard_map/ppermute | solution.py:213
  10.3 0.1 pad_add_fusion.2.place_ref
  10.3 0.0 copy-start
  10.3 1.2 %copy-done = bf16[2,4,256,256]{3,2,1,0:T(8,128)(2,1)S(1)} copy-done((bf16[2,4,256,256]{3,2,1,0:T(8,128)(2,1)S(1)}, bf16[2,4,256,256]{3,2,1,0:T(8,128)(2,1)}, u32[]{:S(2)}) %copy-start) | copy-done | bytes 1048600
  11.6 0.0 copy-start.1
  11.6 1.0 %copy-done.1 = bf16[2,128,1024]{2,1,0:T(8,128)(2,1)S(1)} copy-done((bf16[2,128,1024]{2,1,0:T(8,128)(2,1)S(1)}, bf16[2,128,1024]{2,1,0:T(8,128)(2,1)}, u32[]{:S(2)}) %copy-start.1) | copy-done | bytes 524312
  12.6 0.0 copy-start.2
  12.6 0.8 %copy-done.2 = bf16[4,4,2048]{2,1,0:T(4,128)(2,1)S(1)} copy-done((bf16[4,4,2048]{2,1,0:T(4,128)(2,1)S(1)}, bf16[4,4,2048]{2,1,0:T(4,128)(2,1)}, u32[]{:S(2)}) %copy-start.2) | copy-done | bytes 65560
  13.5 0.0 copy-start.3
  13.5 0.7 %copy-done.3 = s32[4]{0:T(128)S(1)} copy-done((s32[4]{0:T(128)S(1)}, s32[4]{0:T(128)}, u32[]{:S(2)}) %copy-start.3) | copy-done | bytes 40
  14.1 3.0 %cached.1 = (bf16[2,128,128]{2,1,0:T(8,128)(2,1)S(1)}, f32[2,128,128]{2,1,0:T(8,128)S(1)}, f32[2,128,128]{2,1,0:T(8,128)S(1)}, f32[2,128,128]{2,1,0:T(8,128)S(1)...) custom-call(s32[4]{0:T(128)S(1)} %copy-done.3, s32[1]{0:T(128)} %bitcast.7.place_ref, ...), custom_call_target="tpu_custom_call" | custom-call | tf_op jit(solution)/shard_map/cached/pallas_call | solution.py:222
  17.1 5.7 %collective-permute-done.4 = bf16[2,1,32,256]{3,2,0,1:T(8,128)(2,1)S(1)} collective-permute-done((bf16[2,1,32,256]{3,2,0,1:T(8,128)(2,1)}, bf16[2,1,32,256]{3,2,0,1:T(8,128)(2,1)S(1)}, u32[]{:S(2)}, u32[]{:S(2)}) %collective-permute-start.4) | collective-permute-done | bytes 32800 | tf_op jit(solution)/shard_map/ppermute | solution.py:213
  22.9 0.0 copy-done.4
  22.9 0.0 collective-permute-done.1.refs_0_
  22.9 0.0 collective-permute-done.2.refs_1_
  22.9 0.0 collective-permute-done.3.refs_3_
  22.9 1.8 %early.1 = (f32[32,768]{1,0:T(8,128)S(1)}, bf16[32,4096]{1,0:T(8,128)(2,1)S(1)}) custom-call(s32[2]{0:T(128)S(1)} %pad_add_fusion.2.place_ref, bf16[2,4096,256]{2,1,0:T(8,128)(2,1)S(1)} %get-tuple-element.23.base_ref, bf16[4,4,4096]{2,1,0:T(4,128)(2,1)S(1)} %collective-permute-done.1.refs_0_, bf16[4,4,4096]{2,1,0:T(4,128)(2,1)S(1)} %collective-permute-done.2.refs_1_, ...), custom_call_target="tpu_custom_call" | custom-call | tf_op jit(solution)/shard_map/early/pallas_call | solution.py:249
  24.7 0.0 collective-permute-done.refs_0_
  24.7 0.1 collective-permute-start.5
  24.8 0.1 pad_add_fusion.1.place_ref
  24.9 1.8 %collective-permute-done.5.refs_1_ = bf16[2,128,1024]{2,1,0:T(8,128)(2,1)S(1)} collective-permute-done((bf16[2,128,1024]{2,1,0:T(8,128)(2,1)S(1)}, bf16[2,128,1024]{2,1,0:T(8,128)(2,1)S(1)}, u32[]{:S(2)}, u32[]{:S(2)}) %collective-permute-start.5) | collective-permute-done | bytes 524320 | tf_op jit(solution)/shard_map/ppermute | solution.py:191
  26.7 1.0 %late.1 = (f32[16,768]{1,0:T(8,128)S(1)}, bf16[16,768]{1,0:T(8,128)(2,1)S(1)}) custom-call(s32[3]{0:T(128)S(1)} %pad_add_fusion.1.place_ref, f32[32,768]{1,0:T(8,128)S(1)} %get-tuple-element.29.part_ref, bf16[32,4096]{1,0:T(8,128)(2,1)S(1)} %get-tuple-element.30.x_ref, bf16[2,128,1024]{2,1,0:T(8,128)(2,1)S(1)} %collective-permute-done.refs_0_, ...), custom_call_target="tpu_custom_call" | custom-call | tf_op jit(solution)/shard_map/late/pallas_call | solution.py:264
  27.7 2.8 %collective-permute-start.7 = (bf16[2,2,32,256]{3,2,0,1:T(8,128)(2,1)S(1)}, bf16[2,2,32,256]{3,2,0,1:T(8,128)(2,1)S(1)}, u32[]{:S(2)}, u32[]{:S(2)}) collective-permute-start(bf16[2,2,32,256]{3,2,0,1:T(8,128)(2,1)S(1)} %pad_maximum_fusion.2), channel_id=1, source_target_pairs={{0,8},{4,12},{8,0},{12,4},{1,9},{5,13},{9,1},{13,5},{2,10},{6,14},... | collective-permute-start | bytes 196616 | tf_op jit(solution)/shard_map/ppermute | solution.py:213
  30.5 0.2 collective-permute-start.6
  30.7 5.0 %collective-permute-done.6.refs_0_ = bf16[16,768]{1,0:T(8,128)(2,1)S(1)} collective-permute-done((bf16[16,768]{1,0:T(8,128)(2,1)S(1)}, bf16[16,768]{1,0:T(8,128)(2,1)S(1)}, u32[]{:S(2)}, u32[]{:S(2)}) %collective-permute-start.6) | collective-permute-done | bytes 24608 | tf_op jit(solution)/shard_map/ppermute | solution.py:277
  35.6 0.0 collective-permute-done.7
  35.7 0.1 collective-permute-start.9
  35.8 0.1 pad_add_fusion.place_ref
  35.9 0.6 %collective-permute-start.8 = (bf16[16,256]{1,0:T(8,128)(2,1)S(1)}, bf16[16,256]{1,0:T(8,128)(2,1)S(1)}, u32[]{:S(2)}, u32[]{:S(2)}) collective-permute-start(bf16[16,256]{1,0:T(8,128)(2,1)S(1)} %ranks.1.refs_1_), channel_id=1, source_target_pairs={{0,2},{2,0},{1,3},{3,1},{4,6},{6,4},{5,7},{7,5},{8,10},{10,8},{9,1... | collective-permute-start | bytes 24584 | tf_op jit(solution)/shard_map/ppermute | solution.py:292
  36.4 0.6 %collective-permute-done.9 = bf16[2,4,32,256]{3,2,0,1:T(8,128)(2,1)S(1)} collective-permute-done((bf16[2,4,32,256]{3,2,0,1:T(8,128)(2,1)S(1)}, bf16[2,4,32,256]{3,2,0,1:T(8,128)(2,1)S(1)}, u32[]{:S(2)}, u32[]{:S(2)}) %collective-permute-start.9) | collective-permute-done | bytes 131104 | tf_op jit(solution)/shard_map/ppermute | solution.py:213
  37.2 2.3 %collective-permute-done.8.refs_2_ = bf16[16,256]{1,0:T(8,128)(2,1)S(1)} collective-permute-done((bf16[16,256]{1,0:T(8,128)(2,1)S(1)}, bf16[16,256]{1,0:T(8,128)(2,1)S(1)}, u32[]{:S(2)}, u32[]{:S(2)}) %collective-permute-start.8) | collective-permute-done | bytes 8224 | tf_op jit(solution)/shard_map/ppermute | solution.py:292
  39.5 1.9 %final.1 = (bf16[2,4,4,256]{3,2,1,0:T(4,128)(2,1)}, bf16[4,4,2048]{2,1,0:T(4,128)(2,1)}) custom-call(s32[2]{0:T(128)S(1)} %pad_add_fusion.place_ref, f32[16,768]{1,0:T(8,128)S(1)} %get-tuple-element.35.mine_ref, bf16[16,768]{1,0:T(8,128)(2,1)S(1)} %collective-permute-done.6.refs_0_, bf16[16,256]{1,0:T(8,128)(2,1)S(1)} %ranks.1.refs_1_, ...), custom_call_target="tpu_custom_call" | custom-call | tf_op jit(solution)/shard_map/final/pallas_call | solution.py:295
  (8 shorter events, 0.1 us)
Async XLA Ops:
  0.6 22.2 %copy-start.4 = (bf16[2,256,32]{1,2,0:T(8,128)(2,1)S(1)}, bf16[2,256,32]{1,2,0:T(8,128)(2,1)}, u32[]{:S(2)}) copy-start(bf16[2,256,32]{1,2,0:T(8,128)(2,1)} %param.13) | copy-start | bytes 98308
  0.6 22.3 %collective-permute-start.3 = (bf16[2,128,1024]{2,1,0:T(8,128)(2,1)}, bf16[2,128,1024]{2,1,0:T(8,128)(2,1)S(1)}, u32[]{:S(2)}, u32[]{:S(2)}) collective-permute-start(bf16[2,128,1024]{2,1,0:T(8,128)(2,1)} %a_hbm.1), channel_id=1, source_target_pairs={{0,1},{1,0},{2,3},{3,2},{4,5},{5,4},{6,7},{7,6},{8,9},{9,8},{10,11... | collective-permute-start | bytes 1572872 | tf_op jit(solution)/shard_map/ppermute | solution.py:191
  1.2 23.5 %collective-permute-start = (bf16[2,128,1024]{2,1,0:T(8,128)(2,1)}, bf16[2,128,1024]{2,1,0:T(8,128)(2,1)S(1)}, u32[]{:S(2)}, u32[]{:S(2)}) collective-permute-start(bf16[2,128,1024]{2,1,0:T(8,128)(2,1)} %a_hbm.1), channel_id=1, source_target_pairs={{0,4},{4,0},{8,12},{12,8},{1,5},{5,1},{9,13},{13,9},{2,6},{6,2},{1... | collective-permute-start | bytes 1572872 | tf_op jit(solution)/shard_map/ppermute | solution.py:188
  3.8 19.1 %collective-permute-start.1 = (bf16[4,4,4096]{2,1,0:T(4,128)(2,1)}, bf16[4,4,4096]{2,1,0:T(4,128)(2,1)S(1)}, u32[]{:S(2)}, u32[]{:S(2)}) collective-permute-start(bf16[4,4,4096]{2,1,0:T(4,128)(2,1)} %param.7), channel_id=1, source_target_pairs={{0,0},{2,8},{4,4},{6,12},{8,2},{10,10},{12,6},{14,14},{1,1},{3,9},... | collective-permute-start | bytes 393224 | tf_op jit(solution)/shard_map/ppermute | solution.py:198
  5.4 17.5 %collective-permute-start.2 = (bf16[4,4,4096]{2,1,0:T(4,128)(2,1)}, bf16[4,4,4096]{2,1,0:T(4,128)(2,1)S(1)}, u32[]{:S(2)}, u32[]{:S(2)}) collective-permute-start(bf16[4,4,4096]{2,1,0:T(4,128)(2,1)} %param.7), channel_id=1, source_target_pairs={{0,2},{2,10},{4,6},{6,14},{8,0},{10,8},{12,4},{14,12},{1,3},{3,11}... | collective-permute-start | bytes 393224 | tf_op jit(solution)/shard_map/ppermute | solution.py:198
  9.8 13.0 %collective-permute-start.4 = (bf16[2,1,32,256]{3,2,0,1:T(8,128)(2,1)}, bf16[2,1,32,256]{3,2,0,1:T(8,128)(2,1)S(1)}, u32[]{:S(2)}, u32[]{:S(2)}) collective-permute-start(bf16[2,1,32,256]{3,2,0,1:T(8,128)(2,1)} %bitcast.19), channel_id=1, source_target_pairs={{0,4},{4,0},{8,12},{12,8},{1,5},{5,1},{9,13},{13,9},{2,6},{6,2},{1... | collective-permute-start | bytes 98312 | tf_op jit(solution)/shard_map/ppermute | solution.py:213
  10.3 1.2 %copy-start = (bf16[2,4,256,256]{3,2,1,0:T(8,128)(2,1)S(1)}, bf16[2,4,256,256]{3,2,1,0:T(8,128)(2,1)}, u32[]{:S(2)}) copy-start(bf16[2,4,256,256]{3,2,1,0:T(8,128)(2,1)} %kv_hbm.1) | copy-start | bytes 3145732
  11.6 1.0 %copy-start.1 = (bf16[2,128,1024]{2,1,0:T(8,128)(2,1)S(1)}, bf16[2,128,1024]{2,1,0:T(8,128)(2,1)}, u32[]{:S(2)}) copy-start(bf16[2,128,1024]{2,1,0:T(8,128)(2,1)} %a_hbm.1) | copy-start | bytes 1572868
  12.6 0.8 %copy-start.2 = (bf16[4,4,2048]{2,1,0:T(4,128)(2,1)S(1)}, bf16[4,4,2048]{2,1,0:T(4,128)(2,1)}, u32[]{:S(2)}) copy-start(bf16[4,4,2048]{2,1,0:T(4,128)(2,1)} %q_hbm.1) | copy-start | bytes 196612
  13.5 0.7 %copy-start.3 = (s32[4]{0:T(128)S(1)}, s32[4]{0:T(128)}, u32[]{:S(2)}) copy-start(s32[4]{0:T(128)} %len_ref.1) | copy-start | bytes 52
  24.7 2.0 %collective-permute-start.5 = (bf16[2,128,1024]{2,1,0:T(8,128)(2,1)S(1)}, bf16[2,128,1024]{2,1,0:T(8,128)(2,1)S(1)}, u32[]{:S(2)}, u32[]{:S(2)}) collective-permute-start(bf16[2,128,1024]{2,1,0:T(8,128)(2,1)S(1)} %collective-permute-done.refs_0_), channel_id=1, source_target_pairs={{0,1},{1,0},{2,3},{3,2},{4,5},{5,4},{6,7},{7,6},{8,9},{9,8},{10,11... | collective-permute-start | bytes 1572872 | tf_op jit(solution)/shard_map/ppermute | solution.py:191
  27.7 8.0 %collective-permute-start.7 = (bf16[2,2,32,256]{3,2,0,1:T(8,128)(2,1)S(1)}, bf16[2,2,32,256]{3,2,0,1:T(8,128)(2,1)S(1)}, u32[]{:S(2)}, u32[]{:S(2)}) collective-permute-start(bf16[2,2,32,256]{3,2,0,1:T(8,128)(2,1)S(1)} %pad_maximum_fusion.2), channel_id=1, source_target_pairs={{0,8},{4,12},{8,0},{12,4},{1,9},{5,13},{9,1},{13,5},{2,10},{6,14},... | collective-permute-start | bytes 196616 | tf_op jit(solution)/shard_map/ppermute | solution.py:213
  30.5 5.1 %collective-permute-start.6 = (bf16[16,768]{1,0:T(8,128)(2,1)S(1)}, bf16[16,768]{1,0:T(8,128)(2,1)S(1)}, u32[]{:S(2)}, u32[]{:S(2)}) collective-permute-start(bf16[16,768]{1,0:T(8,128)(2,1)S(1)} %get-tuple-element.36), channel_id=1, source_target_pairs={{0,8},{4,12},{8,0},{12,4},{1,9},{5,13},{9,1},{13,5},{2,10},{6,14},... | collective-permute-start | bytes 73736 | tf_op jit(solution)/shard_map/ppermute | solution.py:277
  35.7 1.4 %collective-permute-start.9 = (bf16[2,4,32,256]{3,2,0,1:T(8,128)(2,1)S(1)}, bf16[2,4,32,256]{3,2,0,1:T(8,128)(2,1)S(1)}, u32[]{:S(2)}, u32[]{:S(2)}) collective-permute-start(bf16[2,4,32,256]{3,2,0,1:T(8,128)(2,1)S(1)} %pad_maximum_fusion.1), channel_id=1, source_target_pairs={{0,1},{1,0},{2,3},{3,2},{4,5},{5,4},{6,7},{7,6},{8,9},{9,8},{10,11... | collective-permute-start | bytes 393224 | tf_op jit(solution)/shard_map/ppermute | solution.py:213
  35.9 3.7 %collective-permute-start.8 = (bf16[16,256]{1,0:T(8,128)(2,1)S(1)}, bf16[16,256]{1,0:T(8,128)(2,1)S(1)}, u32[]{:S(2)}, u32[]{:S(2)}) collective-permute-start(bf16[16,256]{1,0:T(8,128)(2,1)S(1)} %ranks.1.refs_1_), channel_id=1, source_target_pairs={{0,2},{2,0},{1,3},{3,1},{4,6},{6,4},{5,7},{7,5},{8,10},{10,8},{9,1... | collective-permute-start | bytes 24584 | tf_op jit(solution)/shard_map/ppermute | solution.py:292

commit v3 on v2

--- a/solution.py
+++ b/solution.py
@@ -10,6 +10,9 @@
 HD = 128
 KVH = 4
 QH = 32
+
+C_CACHED = 4.0
+C_EARLY = 0.1
 NEG = -1e30
 
 NT = (((1,), (1,)), ((), ()))
@@ -20,6 +23,10 @@
     return lax.dot_general(x, y, dims, preferred_element_type=jnp.float32)
 
 
+def cost(us):
+    return pl.CostEstimate(flops=int(us * 1e9), bytes_accessed=int(us * 3e6), transcendentals=0)
+
+
 def vmem():
     return pl.BlockSpec(memory_space=pltpu.VMEM)
 
@@ -29,18 +36,14 @@
 
 
 def cache_kernel(
-    group, len_ref, place_ref, q_hbm, kv_hbm, base_hbm, a_hbm,
-    q_out, acc_out, top_out, sum_out, base_out, a_out, q_ref, kv_ref, sems,
+    group, len_ref, q_hbm, kv_hbm, a_hbm,
+    q_out, acc_out, top_out, sum_out, a_out, q_ref, kv_ref, sems,
 ):
-    wide = base_out.shape[1]
-    start = pl.multiple_of(place_ref[0] * wide, wide)
     copies = [
         pltpu.make_async_copy(q_hbm, q_ref, sems.at[0]),
         pltpu.make_async_copy(kv_hbm.at[0], kv_ref.at[0], sems.at[1]),
         pltpu.make_async_copy(kv_hbm.at[1], kv_ref.at[1], sems.at[2]),
         pltpu.make_async_copy(a_hbm, a_out, sems.at[3]),
-        pltpu.make_async_copy(base_hbm.at[0, pl.ds(start, wide)], base_out.at[0], sems.at[4]),
-        pltpu.make_async_copy(base_hbm.at[1, pl.ds(start, wide)], base_out.at[1], sems.at[5]),
     ]
     for copy in copies:
         copy.start()
@@ -84,27 +87,56 @@
         copy.wait()
 
 
-def early_kernel(blocks, place_ref, base_ref, *refs):
-    x_refs, a_refs = refs[:blocks], refs[blocks:-2]
-    out_ref, x_out = refs[-2:]
-    columns, slab, ranks = base_ref.shape[2], a_refs[0].shape[2], a_refs[0].shape[1]
+def early_kernel(blocks, chunk, place_ref, base_hbm, *refs):
+    x_refs, refs = refs[:blocks], refs[blocks:]
+    if blocks == 2:
+        x_refs, refs = x_refs + refs[:1], refs[1:]
+    a_refs, (out_ref, x_out, base_ref, sems) = refs[:-4], refs[-4:]
+    columns, slab, ranks = base_hbm.shape[2], a_refs[0].shape[2], a_refs[0].shape[1]
     rows, steps, wide = x_refs[0].shape
-    for k, x_ref in enumerate(x_refs):
-        x = jnp.concatenate([x_ref[b].astype(jnp.float32) for b in range(rows)], axis=0)
+    first = pl.multiple_of(place_ref[len(a_refs) + 1] * wide, wide)
+    copies = []
+    for i in range(wide // chunk):
+        for m in range(2):
+            copies.append(
+                pltpu.make_async_copy(
+                    base_hbm.at[m, pl.ds(first + i * chunk, chunk)],
+                    base_ref.at[m, pl.ds(i * chunk, chunk)],
+                    sems.at[2 * i + m],
+                )
+            )
+    for copy in copies:
+        copy.start()
+    moved = place_ref[len(a_refs)] == 1
+    for k in range(blocks):
+        pieces = []
+        for b in range(rows):
+            x = x_refs[k][b].astype(jnp.float32)
+            if len(x_refs) > blocks:
+                x = jnp.where(moved, x_refs[k + 1][b].astype(jnp.float32), x)
+            pieces.append(x)
+        x = jnp.concatenate(pieces, axis=0)
         x_out[k * rows * steps : (k + 1) * rows * steps] = x.astype(jnp.bfloat16)
     count = blocks * rows * steps
     for m in range(2):
-        out_ref[:, m * columns : (m + 1) * columns] = dot(x_out[...], base_ref[m])
         total = jnp.zeros((count, ranks), jnp.float32)
         for i, a in enumerate(a_refs):
             start = pl.multiple_of(place_ref[i] * slab, slab)
             total = total + dot(x_out[:, pl.ds(start, slab)], a[m], NT)
         out_ref[:, 2 * columns + m * ranks : 2 * columns + (m + 1) * ranks] = total
+    totals = [jnp.zeros((count, columns), jnp.float32) for _ in range(2)]
+    for i in range(wide // chunk):
+        at = slice(i * chunk, (i + 1) * chunk)
+        for m in range(2):
+            copies[2 * i + m].wait()
+            totals[m] = totals[m] + dot(x_out[:, at], base_ref[m, at])
+    for m in range(2):
+        out_ref[:, m * columns : (m + 1) * columns] = totals[m]
 
 
 def late_kernel(blocks, columns, place_ref, part_ref, x_ref, *refs):
     a_refs, outs = refs[:-blocks], refs[-blocks:]
-    tokens, acc = outs[0].shape
+    tokens = outs[0].shape[0]
     slab, ranks = a_refs[0].shape[2], a_refs[0].shape[1]
     sums = [part_ref[:, : 2 * columns]]
     for m in range(2):
@@ -114,13 +146,23 @@
             total = total + dot(x_ref[:, pl.ds(start, slab)], a[m], NT)
         sums.append(total)
     whole = jnp.concatenate(sums, axis=1)
-    shift = place_ref[len(a_refs)]
     for j, out in enumerate(outs):
-        value = jnp.zeros((tokens, acc), jnp.float32)
-        for k in range(blocks):
-            mine = lax.rem(shift - k + blocks, blocks) == j
-            value = jnp.where(mine, whole[k * tokens : (k + 1) * tokens], value)
-        out[...] = value.astype(out.dtype)
+        out[...] = whole[j * tokens : (j + 1) * tokens].astype(out.dtype)
+
+
+def collect_kernel(*refs):
+    rows = refs[0].shape[1]
+    for k, ref in enumerate(refs[:-1]):
+        refs[-1][:, k * rows : (k + 1) * rows] = ref[...]
+
+
+def order_kernel(count, place_ref, *refs):
+    out = refs[-1]
+    rows = refs[0].shape[1] // count
+    for i, ref in enumerate(refs[:-1]):
+        for k in range(count):
+            start = pl.multiple_of(place_ref[i * count + k] * rows, rows)
+            out[:, pl.ds(start, rows)] = ref[:, k * rows : (k + 1) * rows]
 
 
 def rank_kernel(columns, mine_ref, *refs):
@@ -197,10 +239,16 @@
                 pairs.append((i * tp + j, (j * inner + i % inner) * tp + (i // inner + k) % tp))
         return lax.ppermute(x, ("fsdp", "tp"), pairs)
 
-    xs = [None] + [spread(inputs, k) for k in range(1, tp)]
+    if tp == 2:
+        pairs = [(i * tp + i // inner, i * tp + 1 - i // inner) for i in range(fsdp)]
+        near_x = spread(inputs, 1)
+        xs = [inputs, near_x, lax.ppermute(near_x, ("fsdp", "tp"), pairs)]
+    else:
+        xs = jnp.stack([spread(inputs, k) for k in range(tp)])
+        xs = [lax.dynamic_index_in_dim(xs, (t - p - j) % tp, keepdims=False) for j in range(tp)]
+
     far = [over_fsdp(a_factor, k) for k in range(1, inner)]
     near = [(0, e, over_sub(a_factor, e)) for e in range(1, sub)]
-    xs[0] = spread(inputs, 0)
 
     def join(mine, other, bit):
         low = jnp.where(bit == 0, mine, other)
@@ -215,30 +263,36 @@
             start = start * 2
         return x
 
-    up = gather(b_factor.transpose(0, 2, 1)[:, None], "fsdp", f, 1, inner)
+    up = b_factor.transpose(0, 2, 1)
+    direct = fsdp <= 4 and up.shape[1] % 16 == 0
+    if direct:
+        up = [up] + [over_fsdp(up, k) for k in range(1, fsdp)]
+    else:
+        up = gather(gather(up[:, None], "fsdp", f, 1, fsdp), "sub", s, 1, sub)
+        up = up.reshape(2, sub, fsdp, -1, columns).swapaxes(1, 2).reshape(2, -1, columns)
 
     count = group * tokens
     per_head = jax.ShapeDtypeStruct((heads, count, HD), f32)
-    *state, rows_base, near_a = pl.pallas_call(
+    *state, near_a = pl.pallas_call(
         functools.partial(cache_kernel, group),
         out_shape=[
             jax.ShapeDtypeStruct((heads, count, HD), bf16),
             per_head,
             per_head,
             per_head,
-            jax.ShapeDtypeStruct((2, wide, columns), bf16),
             jax.ShapeDtypeStruct(a_factor.shape, bf16),
         ],
-        in_specs=[smem(), smem()] + [pl.BlockSpec(memory_space=pltpu.HBM)] * 4,
-        out_specs=[vmem()] * 6,
+        in_specs=[smem()] + [pl.BlockSpec(memory_space=pltpu.HBM)] * 3,
+        out_specs=[vmem()] * 5,
         scratch_shapes=[
             pltpu.VMEM(queries.shape, bf16),
             pltpu.VMEM(kv_cache.shape, bf16),
-            pltpu.SemaphoreType.DMA((6,)),
+            pltpu.SemaphoreType.DMA((4,)),
         ],
-        compiler_params=params(),
+        compiler_params=params(40),
+        cost_estimate=cost(C_CACHED),
         name="cached",
-    )(lengths, p.astype(jnp.int32)[None], queries, kv_cache, base, a_factor)
+    )(lengths, queries, kv_cache, a_factor)
 
     def place_of(items):
         return [((r ^ k) * sub + (s ^ e)).astype(jnp.int32) for k, e, _ in items]
@@ -247,20 +301,22 @@
     near = [(0, 0, near_a)] + near
     width = 2 * columns + 2 * ranks
     part, x = pl.pallas_call(
-        functools.partial(early_kernel, tp),
+        functools.partial(early_kernel, tp, wide // 4),
         out_shape=[
             jax.ShapeDtypeStruct((tp * tokens, width), f32),
             jax.ShapeDtypeStruct((tp * tokens, wide), bf16),
         ],
-        in_specs=[smem()] + [vmem()] * (1 + tp + len(near)),
+        in_specs=[smem(), pl.BlockSpec(memory_space=pltpu.HBM)] + [vmem()] * (len(xs) + len(near)),
         out_specs=[vmem()] * 2,
-        compiler_params=params(),
+        scratch_shapes=[pltpu.VMEM((2, wide, columns), bf16), pltpu.SemaphoreType.DMA((8,))],
+        compiler_params=params(50),
+        cost_estimate=cost(C_EARLY),
         name="early",
-    )(jnp.stack(place_of(near)), rows_base, *xs, *[a for _, _, a in near])
+    )(jnp.stack(place_of(near) + [(t != p).astype(jnp.int32), p.astype(jnp.int32)]), base, *xs, *[a for _, _, a in near])
 
     far, part, up = lax.optimization_barrier((far, part, up))
-    late = [(k, e, over_sub(a, e) if e else a) for k, a in enumerate(far, 1) for e in range(sub)]
-    shift = ((t - p + tp) % tp).astype(jnp.int32)
+    late_at = [(k, e) for k in range(1, inner) for e in range(sub)]
+    late = [over_sub(far[k - 1], e) if e else far[k - 1] for k, e in late_at]
     parts = pl.pallas_call(
         functools.partial(late_kernel, tp, columns),
         out_shape=[jax.ShapeDtypeStruct((tokens, width), f32 if j == 0 else bf16) for j in range(tp)],
@@ -268,14 +324,35 @@
         out_specs=[vmem()] * tp,
         compiler_params=params(),
         name="late",
-    )(jnp.stack(place_of(late) + [shift]), part, x, *[a for _, _, a in late])
+    )(jnp.stack(place_of([(k, e, None) for k, e in late_at])), part, x, *late)
 
     parts, up = lax.optimization_barrier((parts, up))
     others = []
     for j in range(1, tp):
         pairs = [(i, (i + j * inner) % fsdp) for i in range(fsdp)]
         others.append(lax.ppermute(parts[j], "fsdp", pairs))
-    up = gather(up, "fsdp", f, inner, fsdp)
+
+    if direct:
+        piece = up[0].shape
+        mine = pl.pallas_call(
+            collect_kernel,
+            out_shape=jax.ShapeDtypeStruct((2, fsdp * piece[1], columns), bf16),
+            in_specs=[vmem()] * fsdp,
+            out_specs=vmem(),
+            compiler_params=params(),
+            name="collect",
+        )(*up)
+        up = [mine] + [over_sub(mine, e) for e in range(1, sub)]
+        place = [(f ^ k) * sub + (s ^ e) for e in range(sub) for k in range(fsdp)]
+        up = pl.pallas_call(
+            functools.partial(order_kernel, fsdp),
+            out_shape=jax.ShapeDtypeStruct((2, sub * fsdp * piece[1], columns), bf16),
+            in_specs=[smem()] + [vmem()] * sub,
+            out_specs=vmem(),
+            compiler_params=params(),
+            name="order",
+        )(jnp.stack(place).astype(jnp.int32), *up)
+
     own = pl.pallas_call(
         functools.partial(rank_kernel, columns),
         out_shape=jax.ShapeDtypeStruct((tokens, 2 * ranks), bf16),
@@ -284,9 +361,6 @@
         compiler_params=params(),
         name="ranks",
     )(parts[0], *others)
-    own, up = lax.optimization_barrier((own, up))
-    up = gather(up, "sub", s, 1, sub)
-    up = up.reshape(2, sub, fsdp, -1, columns).swapaxes(1, 2).reshape(2, -1, columns)
     rank_parts = [own]
     for i in range(1, tp):
         rank_parts.append(lax.ppermute(own, "tp", [(j, (j + i) % tp) for j in range(tp)]))

time: 41.7 us -> 38.8 us (0.930)
  waiting for transfers between devices: 15.5 us -> 10.7 us
  Pallas kernels: 7.69 us -> 8.95 us
  starting transfers between devices: 13.4 us -> 14 us
    ppermute x3 -> x1, waiting for transfers between devices: 6.38 us -> 0.01 us  [local(): xs = [inputs, near_x, lax.ppermute(near_x, ('fsdp', 'tp'), pairs)]]
    ppermute x2 -> x1, waiting for transfers between devices: 0.01 us -> 4.78 us  [spread(): return lax.ppermute(x, ('fsdp', 'tp'), pairs)]
    ppermute x1 -> x4, starting transfers between devices: 2.65 us -> 5.96 us  [over_fsdp(): return lax.ppermute(x, 'fsdp', [(i, i ^ k) for i in range(fsdp)])]
    ppermute x2 -> x1, starting transfers between devices: 6.01 us -> 2.99 us  [spread(): return lax.ppermute(x, ('fsdp', 'tp'), pairs)]
    pallas_call x1 -> x3, Pallas kernels: 1.77 us -> 4.28 us  [the longest x1 3.71 us: local(): pl.pallas_call(functools.partial(early_kernel, tp, wide // 4), out_shape=...]
    ppermute x3 -> x1, starting transfers between devices: 3.37 us -> 1.29 us  [local(): xs = [inputs, near_x, lax.ppermute(near_x, ('fsdp', 'tp'), pairs)]]
    ppermute x1, waiting for transfers between devices: 4.95 us -> 3.15 us  [local(): others.append(lax.ppermute(parts[j], 'fsdp', pairs))]
    ppermute x1, starting transfers between devices: 0.59 us -> 2.16 us  [local(): lax.ppermute(own, 'tp', [(j, (j + i) % tp) for j in range(tp)])]
  transfers between devices with their start and end apart: 10 -> 11, of which waited for: 5 -> 4; matrix products, arithmetic and copies ran while one was open for 1% -> 1% of each run, Pallas kernels for 12% -> 16%
where the time goes in v3:
time: 38.8 us; the launch traced here: 38.5 us
  starting transfers between devices  14 us (36%)
  waiting for transfers between devices  10.7 us (28%)
  Pallas kernels  8.95 us (23%)
  local copies, waits for them, and re-layouts  3.85 us (10%)
  between operations  0.83 us (2%)
    ppermute x4, starting transfers between devices, over_fsdp(): return lax.ppermute(x, 'fsdp', [(i, i ^ k) for i in range(fsdp)])  5.96 us
    ppermute x1, waiting for transfers between devices, spread(): return lax.ppermute(x, ('fsdp', 'tp'), pairs)  4.78 us
    unnamed x12, local copies, waits for them, and re-layouts  3.76 us
    pallas_call x1, Pallas kernels, local(): pl.pallas_call(functools.partial(early_kernel, tp, wide // 4), out_shape=...  3.71 us
    ppermute x1, waiting for transfers between devices, local(): others.append(lax.ppermute(parts[j], 'fsdp', pairs))  3.15 us
    ppermute x1, starting transfers between devices, spread(): return lax.ppermute(x, ('fsdp', 'tp'), pairs)  2.99 us
    ppermute x1, starting transfers between devices, local(): lax.ppermute(own, 'tp', [(j, (j + i) % tp) for j in range(tp)])  2.16 us
    pallas_call x1, Pallas kernels, local(): pl.pallas_call(functools.partial(final_kernel, tp, steps, group), out_sha...  1.91 us
  transfers between devices with their start and end apart: 11, of which 4 were waited for; matrix products, arithmetic and copies ran while one was open for 1% of the time, Pallas kernels for 16%

profile of v3, /device:TPU:0, one launch (start us, length us, event | category | flops | bytes accessed | tf_op | source)
XLA Modules:
  0.0 38.5 jit_solution(15727897641345107418)
XLA Ops:
  0.6 0.0 copy-start
  0.6 0.0 copy-start.1
  0.7 3.0 %collective-permute-start.1 = (bf16[4,4,4096]{2,1,0:T(4,128)(2,1)}, bf16[4,4,4096]{2,1,0:T(4,128)(2,1)S(1)}, u32[]{:S(2)}, u32[]{:S(2)}) collective-permute-start(bf16[4,4,4096]{2,1,0:T(4,128)(2,1)} %refs_0_), channel_id=1, source_target_pairs={{0,2},{2,10},{4,6},{6,14},{8,0},{10,8},{12,4},{14,12},{1,3},{3,11}... | collective-permute-start | bytes 393224 | tf_op jit(solution)/shard_map/ppermute | solution.py:240
  3.6 0.0 collective-permute-start.3
  3.6 1.6 %collective-permute-start = (bf16[2,128,1024]{2,1,0:T(8,128)(2,1)}, bf16[2,128,1024]{2,1,0:T(8,128)(2,1)S(1)}, u32[]{:S(2)}, u32[]{:S(2)}) collective-permute-start(bf16[2,128,1024]{2,1,0:T(8,128)(2,1)} %a_hbm.1), channel_id=1, source_target_pairs={{0,4},{4,0},{8,12},{12,8},{1,5},{5,1},{9,13},{13,9},{2,6},{6,2},{1... | collective-permute-start | bytes 1572872 | tf_op jit(solution)/shard_map/ppermute | solution.py:230
  5.2 0.4 %collective-permute-start.4 = (bf16[2,32,256]{2,1,0:T(8,128)(2,1)}, bf16[2,32,256]{2,1,0:T(8,128)(2,1)S(1)}, u32[]{:S(2)}, u32[]{:S(2)}) collective-permute-start(bf16[2,32,256]{2,1,0:T(8,128)(2,1)} %bitcast.17), channel_id=1, source_target_pairs={{0,4},{4,0},{8,12},{12,8},{1,5},{5,1},{9,13},{13,9},{2,6},{6,2},{1... | collective-permute-start | bytes 98312 | tf_op jit(solution)/shard_map/ppermute | solution.py:230
  5.7 1.3 %collective-permute-start.5 = (bf16[2,32,256]{2,1,0:T(8,128)(2,1)}, bf16[2,32,256]{2,1,0:T(8,128)(2,1)S(1)}, u32[]{:S(2)}, u32[]{:S(2)}) collective-permute-start(bf16[2,32,256]{2,1,0:T(8,128)(2,1)} %bitcast.18), channel_id=1, source_target_pairs={{0,8},{4,12},{8,0},{12,4},{1,9},{5,13},{9,1},{13,5},{2,10},{6,14},... | collective-permute-start | bytes 98312 | tf_op jit(solution)/shard_map/ppermute | solution.py:230
  6.9 4.8 %collective-permute-done.1.refs_1_ = bf16[4,4,4096]{2,1,0:T(4,128)(2,1)S(1)} collective-permute-done((bf16[4,4,4096]{2,1,0:T(4,128)(2,1)}, bf16[4,4,4096]{2,1,0:T(4,128)(2,1)S(1)}, u32[]{:S(2)}, u32[]{:S(2)}) %collective-permute-start.1) | collective-permute-done | bytes 131104 | tf_op jit(solution)/shard_map/ppermute | solution.py:240
  11.7 1.3 %collective-permute-start.2 = (bf16[4,4,4096]{2,1,0:T(4,128)(2,1)S(1)}, bf16[4,4,4096]{2,1,0:T(4,128)(2,1)S(1)}, u32[]{:S(2)}, u32[]{:S(2)}) collective-permute-start(bf16[4,4,4096]{2,1,0:T(4,128)(2,1)S(1)} %collective-permute-done.1.refs_1_), channel_id=1, source_target_pairs={{0,2},{4,6},{10,8},{14,12},{1,3},{5,7},{11,9},{15,13},{16,18},{20,... | collective-permute-start | bytes 393224 | tf_op jit(solution)/shard_map/ppermute | solution.py:245
  13.0 0.0 copy-start.2
  13.0 1.2 %copy-done.2 = bf16[2,4,256,256]{3,2,1,0:T(8,128)(2,1)S(1)} copy-done((bf16[2,4,256,256]{3,2,1,0:T(8,128)(2,1)S(1)}, bf16[2,4,256,256]{3,2,1,0:T(8,128)(2,1)}, u32[]{:S(2)}) %copy-start.2) | copy-done | bytes 1048600
  14.2 0.0 copy-start.3
  14.2 1.0 %copy-done.3 = bf16[2,128,1024]{2,1,0:T(8,128)(2,1)S(1)} copy-done((bf16[2,128,1024]{2,1,0:T(8,128)(2,1)S(1)}, bf16[2,128,1024]{2,1,0:T(8,128)(2,1)}, u32[]{:S(2)}) %copy-start.3) | copy-done | bytes 524312
  15.3 0.0 copy-start.4
  15.3 0.8 %copy-done.4 = bf16[4,4,2048]{2,1,0:T(4,128)(2,1)S(1)} copy-done((bf16[4,4,2048]{2,1,0:T(4,128)(2,1)S(1)}, bf16[4,4,2048]{2,1,0:T(4,128)(2,1)}, u32[]{:S(2)}) %copy-start.4) | copy-done | bytes 65560
  16.1 0.0 copy-start.5
  16.1 0.7 %copy-done.5 = s32[4]{0:T(128)S(1)} copy-done((s32[4]{0:T(128)S(1)}, s32[4]{0:T(128)}, u32[]{:S(2)}) %copy-start.5) | copy-done | bytes 40
  16.8 1.8 %cached.1 = (bf16[2,128,128]{2,1,0:T(8,128)(2,1)S(1)}, f32[2,128,128]{2,1,0:T(8,128)S(1)}, f32[2,128,128]{2,1,0:T(8,128)S(1)}, f32[2,128,128]{2,1,0:T(8,128)S(1)}, bf16[2,128,1024]{2,1,0:T(8,128)(2,1)S(1)}) custom-call(s32[4]{0:T(128)S(1)} %copy-done.5, bf16[4,4,2048]{2,1,0:T(4,128)(2,1)S(1)} %copy-done.4, bf16[2,4,256,256]{3,2,1,0:T(8,128)(2,1)S(1)} %copy-done.2, ...), custom_call_target="tpu_custom_call" | custom-call | flops 4000000000 | bytes 12000000 | tf_op jit(solution)/shard_map/cached/pallas_call | solution.py:276
  18.6 0.0 collective-permute-done.2.refs_2_
  18.6 0.0 copy-done.1
  18.6 2.7 %collective-permute-start.6 = (bf16[2,32,256]{2,1,0:T(8,128)(2,1)S(1)}, bf16[2,32,256]{2,1,0:T(8,128)(2,1)S(1)}, u32[]{:S(2)}, u32[]{:S(2)}) collective-permute-start(bf16[2,32,256]{2,1,0:T(8,128)(2,1)S(1)} %bitcast.19), channel_id=1, source_target_pairs={{0,12},{4,8},{8,4},{12,0},{1,13},{5,9},{9,5},{13,1},{2,14},{6,10},... | collective-permute-start | bytes 98312 | tf_op jit(solution)/shard_map/ppermute | solution.py:230
  21.3 0.1 pad_add_fusion.2.place_ref
  21.4 0.0 collective-permute-done.3.refs_4_
  21.4 0.0 copy-done
  21.4 3.7 %early.1 = (f32[32,768]{1,0:T(8,128)S(1)}, bf16[32,4096]{1,0:T(8,128)(2,1)S(1)}) custom-call(s32[4]{0:T(128)S(1)} %pad_add_fusion.2.place_ref, bf16[2,8192,256]{2,1,0:T(8,128)(2,1)} %base_hbm.1, bf16[4,4,4096]{2,1,0:T(4,128)(2,1)S(1)} %copy-done, bf16[4,4,4096]{2,1,0:T(4,128)(2,1)S(1)} %collective-permute-done.1.refs_1_, ...), custom_call_target="tpu_custom_call" | custom-call | flops 100000000 | bytes 300000 | tf_op jit(solution)/shard_map/early/pallas_call | solution.py:303
  25.1 0.0 collective-permute-done.4.refs_1_
  25.1 0.0 collective-permute-done.5.refs_2_
  25.1 0.0 collective-permute-done.6.refs_3_
  25.1 0.0 collective-permute-done.refs_0_
  25.1 0.1 collective-permute-start.7
  25.2 0.1 pad_add_fusion.1.place_ref
  25.3 1.8 %collective-permute-done.7.refs_1_ = bf16[2,128,1024]{2,1,0:T(8,128)(2,1)S(1)} collective-permute-done((bf16[2,128,1024]{2,1,0:T(8,128)(2,1)S(1)}, bf16[2,128,1024]{2,1,0:T(8,128)(2,1)S(1)}, u32[]{:S(2)}, u32[]{:S(2)}) %collective-permute-start.7) | collective-permute-done | bytes 524320 | tf_op jit(solution)/shard_map/ppermute | solution.py:233
  27.1 1.0 %late.1 = (f32[16,768]{1,0:T(8,128)S(1)}, bf16[16,768]{1,0:T(8,128)(2,1)S(1)}) custom-call(s32[2]{0:T(128)S(1)} %pad_add_fusion.1.place_ref, f32[32,768]{1,0:T(8,128)S(1)} %get-tuple-element.33.part_ref, bf16[32,4096]{1,0:T(8,128)(2,1)S(1)} %get-tuple-element.34.x_ref, bf16[2,128,1024]{2,1,0:T(8,128)(2,1)S(1)} %collective-permute-done.refs_0_, ...), custom_call_target="tpu_custom_call" | custom-call | tf_op jit(solution)/shard_map/late/pallas_call | solution.py:320
  28.1 1.5 %collective-permute-start.8 = (bf16[16,768]{1,0:T(8,128)(2,1)S(1)}, bf16[16,768]{1,0:T(8,128)(2,1)S(1)}, u32[]{:S(2)}, u32[]{:S(2)}) collective-permute-start(bf16[16,768]{1,0:T(8,128)(2,1)S(1)} %get-tuple-element.43), channel_id=1, source_target_pairs={{0,8},{4,12},{8,0},{12,4},{1,9},{5,13},{9,1},{13,5},{2,10},{6,14},... | collective-permute-start | bytes 73736 | tf_op jit(solution)/shard_map/ppermute | solution.py:333
  29.6 0.1 collective-permute-start.10
  29.7 3.1 %collective-permute-done.8.refs_0_ = bf16[16,768]{1,0:T(8,128)(2,1)S(1)} collective-permute-done((bf16[16,768]{1,0:T(8,128)(2,1)S(1)}, bf16[16,768]{1,0:T(8,128)(2,1)S(1)}, u32[]{:S(2)}, u32[]{:S(2)}) %collective-permute-start.8) | collective-permute-done | bytes 24608 | tf_op jit(solution)/shard_map/ppermute | solution.py:333
  32.8 2.2 %collective-permute-start.9 = (bf16[16,256]{1,0:T(8,128)(2,1)S(1)}, bf16[16,256]{1,0:T(8,128)(2,1)S(1)}, u32[]{:S(2)}, u32[]{:S(2)}) collective-permute-start(bf16[16,256]{1,0:T(8,128)(2,1)S(1)} %ranks.1.refs_1_), channel_id=1, source_target_pairs={{0,2},{2,0},{1,3},{3,1},{4,6},{6,4},{5,7},{7,5},{8,10},{10,8},{9,1... | collective-permute-start | bytes 24584 | tf_op jit(solution)/shard_map/ppermute | solution.py:366
  35.0 0.1 pad_add_fusion.place_ref
  35.1 0.1 stack.83.place_ref
  35.2 0.0 collective-permute-done.10.refs_1_
  35.2 0.6 %order.1.refs_3_ = bf16[2,256,256]{2,1,0:T(8,128)(2,1)S(1)} custom-call(s32[8]{0:T(128)S(1)} %stack.83.place_ref, bf16[2,128,256]{2,1,0:T(8,128)(2,1)S(1)} %collect.1.refs_0_, bf16[2,128,256]{2,1,0:T(8,128)(2,1)S(1)} %collective-permute-done.10.refs_1_), custom_call_target="tpu_custom_call" | custom-call | tf_op jit(solution)/shard_map/order/pallas_call | solution.py:347
  35.7 0.9 %collective-permute-done.9.refs_2_ = bf16[16,256]{1,0:T(8,128)(2,1)S(1)} collective-permute-done((bf16[16,256]{1,0:T(8,128)(2,1)S(1)}, bf16[16,256]{1,0:T(8,128)(2,1)S(1)}, u32[]{:S(2)}, u32[]{:S(2)}) %collective-permute-start.9) | collective-permute-done | bytes 8224 | tf_op jit(solution)/shard_map/ppermute | solution.py:366
  36.6 1.9 %final.1 = (bf16[2,4,4,256]{3,2,1,0:T(4,128)(2,1)}, bf16[4,4,2048]{2,1,0:T(4,128)(2,1)}) custom-call(s32[2]{0:T(128)S(1)} %pad_add_fusion.place_ref, f32[16,768]{1,0:T(8,128)S(1)} %get-tuple-element.42.mine_ref, bf16[16,768]{1,0:T(8,128)(2,1)S(1)} %collective-permute-done.8.refs_0_, bf16[16,256]{1,0:T(8,128)(2,1)S(1)} %ranks.1.refs_1_, ...), custom_call_target="tpu_custom_call" | custom-call | tf_op jit(solution)/shard_map/final/pallas_call | solution.py:369
  (2 shorter events, 0.0 us)
Async XLA Ops:
  0.6 20.7 %copy-start = (bf16[4,4,4096]{2,1,0:T(4,128)(2,1)S(1)}, bf16[4,4,4096]{2,1,0:T(4,128)(2,1)}, u32[]{:S(2)}) copy-start(bf16[4,4,4096]{2,1,0:T(4,128)(2,1)} %refs_0_) | copy-start | bytes 393220
  0.6 17.9 %copy-start.1 = (bf16[2,256,32]{1,2,0:T(8,128)(2,1)S(1)}, bf16[2,256,32]{1,2,0:T(8,128)(2,1)}, u32[]{:S(2)}) copy-start(bf16[2,256,32]{1,2,0:T(8,128)(2,1)} %param.13) | copy-start | bytes 98308
  0.7 11.1 %collective-permute-start.1 = (bf16[4,4,4096]{2,1,0:T(4,128)(2,1)}, bf16[4,4,4096]{2,1,0:T(4,128)(2,1)S(1)}, u32[]{:S(2)}, u32[]{:S(2)}) collective-permute-start(bf16[4,4,4096]{2,1,0:T(4,128)(2,1)} %refs_0_), channel_id=1, source_target_pairs={{0,2},{2,10},{4,6},{6,14},{8,0},{10,8},{12,4},{14,12},{1,3},{3,11}... | collective-permute-start | bytes 393224 | tf_op jit(solution)/shard_map/ppermute | solution.py:240
  3.6 17.7 %collective-permute-start.3 = (bf16[2,128,1024]{2,1,0:T(8,128)(2,1)}, bf16[2,128,1024]{2,1,0:T(8,128)(2,1)S(1)}, u32[]{:S(2)}, u32[]{:S(2)}) collective-permute-start(bf16[2,128,1024]{2,1,0:T(8,128)(2,1)} %a_hbm.1), channel_id=1, source_target_pairs={{0,1},{1,0},{2,3},{3,2},{4,5},{5,4},{6,7},{7,6},{8,9},{9,8},{10,11... | collective-permute-start | bytes 1572872 | tf_op jit(solution)/shard_map/ppermute | solution.py:233
  3.6 21.5 %collective-permute-start = (bf16[2,128,1024]{2,1,0:T(8,128)(2,1)}, bf16[2,128,1024]{2,1,0:T(8,128)(2,1)S(1)}, u32[]{:S(2)}, u32[]{:S(2)}) collective-permute-start(bf16[2,128,1024]{2,1,0:T(8,128)(2,1)} %a_hbm.1), channel_id=1, source_target_pairs={{0,4},{4,0},{8,12},{12,8},{1,5},{5,1},{9,13},{13,9},{2,6},{6,2},{1... | collective-permute-start | bytes 1572872 | tf_op jit(solution)/shard_map/ppermute | solution.py:230
  5.2 19.9 %collective-permute-start.4 = (bf16[2,32,256]{2,1,0:T(8,128)(2,1)}, bf16[2,32,256]{2,1,0:T(8,128)(2,1)S(1)}, u32[]{:S(2)}, u32[]{:S(2)}) collective-permute-start(bf16[2,32,256]{2,1,0:T(8,128)(2,1)} %bitcast.17), channel_id=1, source_target_pairs={{0,4},{4,0},{8,12},{12,8},{1,5},{5,1},{9,13},{13,9},{2,6},{6,2},{1... | collective-permute-start | bytes 98312 | tf_op jit(solution)/shard_map/ppermute | solution.py:230
  5.7 19.4 %collective-permute-start.5 = (bf16[2,32,256]{2,1,0:T(8,128)(2,1)}, bf16[2,32,256]{2,1,0:T(8,128)(2,1)S(1)}, u32[]{:S(2)}, u32[]{:S(2)}) collective-permute-start(bf16[2,32,256]{2,1,0:T(8,128)(2,1)} %bitcast.18), channel_id=1, source_target_pairs={{0,8},{4,12},{8,0},{12,4},{1,9},{5,13},{9,1},{13,5},{2,10},{6,14},... | collective-permute-start | bytes 98312 | tf_op jit(solution)/shard_map/ppermute | solution.py:230
  11.7 6.9 %collective-permute-start.2 = (bf16[4,4,4096]{2,1,0:T(4,128)(2,1)S(1)}, bf16[4,4,4096]{2,1,0:T(4,128)(2,1)S(1)}, u32[]{:S(2)}, u32[]{:S(2)}) collective-permute-start(bf16[4,4,4096]{2,1,0:T(4,128)(2,1)S(1)} %collective-permute-done.1.refs_1_), channel_id=1, source_target_pairs={{0,2},{4,6},{10,8},{14,12},{1,3},{5,7},{11,9},{15,13},{16,18},{20,... | collective-permute-start | bytes 393224 | tf_op jit(solution)/shard_map/ppermute | solution.py:245
  13.0 1.2 %copy-start.2 = (bf16[2,4,256,256]{3,2,1,0:T(8,128)(2,1)S(1)}, bf16[2,4,256,256]{3,2,1,0:T(8,128)(2,1)}, u32[]{:S(2)}) copy-start(bf16[2,4,256,256]{3,2,1,0:T(8,128)(2,1)} %kv_hbm.1) | copy-start | bytes 3145732
  14.2 1.0 %copy-start.3 = (bf16[2,128,1024]{2,1,0:T(8,128)(2,1)S(1)}, bf16[2,128,1024]{2,1,0:T(8,128)(2,1)}, u32[]{:S(2)}) copy-start(bf16[2,128,1024]{2,1,0:T(8,128)(2,1)} %a_hbm.1) | copy-start | bytes 1572868
  15.3 0.8 %copy-start.4 = (bf16[4,4,2048]{2,1,0:T(4,128)(2,1)S(1)}, bf16[4,4,2048]{2,1,0:T(4,128)(2,1)}, u32[]{:S(2)}) copy-start(bf16[4,4,2048]{2,1,0:T(4,128)(2,1)} %q_hbm.1) | copy-start | bytes 196612
  16.1 0.7 %copy-start.5 = (s32[4]{0:T(128)S(1)}, s32[4]{0:T(128)}, u32[]{:S(2)}) copy-start(s32[4]{0:T(128)} %len_ref.1) | copy-start | bytes 52
  18.6 6.5 %collective-permute-start.6 = (bf16[2,32,256]{2,1,0:T(8,128)(2,1)S(1)}, bf16[2,32,256]{2,1,0:T(8,128)(2,1)S(1)}, u32[]{:S(2)}, u32[]{:S(2)}) collective-permute-start(bf16[2,32,256]{2,1,0:T(8,128)(2,1)S(1)} %bitcast.19), channel_id=1, source_target_pairs={{0,12},{4,8},{8,4},{12,0},{1,13},{5,9},{9,5},{13,1},{2,14},{6,10},... | collective-permute-start | bytes 98312 | tf_op jit(solution)/shard_map/ppermute | solution.py:230
  25.1 2.0 %collective-permute-start.7 = (bf16[2,128,1024]{2,1,0:T(8,128)(2,1)S(1)}, bf16[2,128,1024]{2,1,0:T(8,128)(2,1)S(1)}, u32[]{:S(2)}, u32[]{:S(2)}) collective-permute-start(bf16[2,128,1024]{2,1,0:T(8,128)(2,1)S(1)} %collective-permute-done.refs_0_), channel_id=1, source_target_pairs={{0,1},{1,0},{2,3},{3,2},{4,5},{5,4},{6,7},{7,6},{8,9},{9,8},{10,11... | collective-permute-start | bytes 1572872 | tf_op jit(solution)/shard_map/ppermute | solution.py:233
  28.1 4.8 %collective-permute-start.8 = (bf16[16,768]{1,0:T(8,128)(2,1)S(1)}, bf16[16,768]{1,0:T(8,128)(2,1)S(1)}, u32[]{:S(2)}, u32[]{:S(2)}) collective-permute-start(bf16[16,768]{1,0:T(8,128)(2,1)S(1)} %get-tuple-element.43), channel_id=1, source_target_pairs={{0,8},{4,12},{8,0},{12,4},{1,9},{5,13},{9,1},{13,5},{2,10},{6,14},... | collective-permute-start | bytes 73736 | tf_op jit(solution)/shard_map/ppermute | solution.py:333
  29.6 5.6 %collective-permute-start.10 = (bf16[2,128,256]{2,1,0:T(8,128)(2,1)S(1)}, bf16[2,128,256]{2,1,0:T(8,128)(2,1)S(1)}, u32[]{:S(2)}, u32[]{:S(2)}) collective-permute-start(bf16[2,128,256]{2,1,0:T(8,128)(2,1)S(1)} %collect.1.refs_0_), channel_id=1, source_target_pairs={{0,1},{1,0},{2,3},{3,2},{4,5},{5,4},{6,7},{7,6},{8,9},{9,8},{10,11... | collective-permute-start | bytes 393224 | tf_op jit(solution)/shard_map/ppermute | solution.py:233
  32.8 3.8 %collective-permute-start.9 = (bf16[16,256]{1,0:T(8,128)(2,1)S(1)}, bf16[16,256]{1,0:T(8,128)(2,1)S(1)}, u32[]{:S(2)}, u32[]{:S(2)}) collective-permute-start(bf16[16,256]{1,0:T(8,128)(2,1)S(1)} %ranks.1.refs_1_), channel_id=1, source_target_pairs={{0,2},{2,0},{1,3},{3,1},{4,6},{6,4},{5,7},{7,5},{8,10},{10,8},{9,1... | collective-permute-start | bytes 24584 | tf_op jit(solution)/shard_map/ppermute | solution.py:366

commit v4 on v3

--- a/solution.py
+++ b/solution.py
@@ -11,8 +11,8 @@
 KVH = 4
 QH = 32
 
-C_CACHED = 4.0
-C_EARLY = 0.1
+C_CACHED = 2.0
+C_EARLY = 3.0
 NEG = -1e30
 
 NT = (((1,), (1,)), ((), ()))
@@ -36,18 +36,21 @@
 
 
 def cache_kernel(
-    group, len_ref, q_hbm, kv_hbm, a_hbm,
-    q_out, acc_out, top_out, sum_out, a_out, q_ref, kv_ref, sems,
+    group, count_up, len_ref, tick_ref, q_hbm, kv_hbm, *refs
 ):
+    up_refs, refs = refs[:count_up], refs[count_up:]
+    q_out, acc_out, top_out, sum_out, up_out, q_ref, kv_ref, sems = refs
+    held = up_refs[0].shape[1]
+    for i, up_ref in enumerate(up_refs):
+        up_out[:, i * held : (i + 1) * held] = up_ref[...]
     copies = [
         pltpu.make_async_copy(q_hbm, q_ref, sems.at[0]),
         pltpu.make_async_copy(kv_hbm.at[0], kv_ref.at[0], sems.at[1]),
         pltpu.make_async_copy(kv_hbm.at[1], kv_ref.at[1], sems.at[2]),
-        pltpu.make_async_copy(a_hbm, a_out, sems.at[3]),
     ]
     for copy in copies:
         copy.start()
-    for copy in copies[:3]:
+    for copy in copies:
         copy.wait()
     rows, steps, width = q_ref.shape
     heads, cached = width // (group * HD), kv_ref.shape[2]
@@ -83,8 +86,6 @@
         acc_out[g] = mixed
         top_out[g] = jnp.broadcast_to(top, (count, HD))
         sum_out[g] = jnp.broadcast_to(total, (count, HD))
-    for copy in copies[3:]:
-        copy.wait()
 
 
 def early_kernel(blocks, chunk, place_ref, base_hbm, *refs):
@@ -150,6 +151,10 @@
         out[...] = whole[j * tokens : (j + 1) * tokens].astype(out.dtype)
 
 
+def tick_kernel(out_ref):
+    out_ref[...] = jnp.zeros(out_ref.shape, jnp.float32)
+
+
 def collect_kernel(*refs):
     rows = refs[0].shape[1]
     for k, ref in enumerate(refs[:-1]):
@@ -239,15 +244,18 @@
                 pairs.append((i * tp + j, (j * inner + i % inner) * tp + (i // inner + k) % tp))
         return lax.ppermute(x, ("fsdp", "tp"), pairs)
 
-    if tp == 2:
-        pairs = [(i * tp + i // inner, i * tp + 1 - i // inner) for i in range(fsdp)]
-        near_x = spread(inputs, 1)
-        xs = [inputs, near_x, lax.ppermute(near_x, ("fsdp", "tp"), pairs)]
-    else:
-        xs = jnp.stack([spread(inputs, k) for k in range(tp)])
-        xs = [lax.dynamic_index_in_dim(xs, (t - p - j) % tp, keepdims=False) for j in range(tp)]
-
-    far = [over_fsdp(a_factor, k) for k in range(1, inner)]
+    xs = [spread(inputs, k) for k in range(1 if tp == 2 else 0, tp)]
+
+    tick = pl.pallas_call(
+        tick_kernel,
+        out_shape=jax.ShapeDtypeStruct((8, 128), f32),
+        out_specs=vmem(),
+        cost_estimate=cost(8.0),
+        name="tick",
+    )()
+
+    a_own, tick = lax.optimization_barrier((a_factor, tick))
+    far = [over_fsdp(a_own, k) for k in range(1, inner)]
     near = [(0, e, over_sub(a_factor, e)) for e in range(1, sub)]
 
     def join(mine, other, bit):
@@ -264,41 +272,48 @@
         return x
 
     up = b_factor.transpose(0, 2, 1)
-    direct = fsdp <= 4 and up.shape[1] % 16 == 0
+    direct = fsdp == 4 and inner == 2 and up.shape[1] % 16 == 0
     if direct:
-        up = [up] + [over_fsdp(up, k) for k in range(1, fsdp)]
+        up = [up, over_fsdp(up, 1)]
     else:
         up = gather(gather(up[:, None], "fsdp", f, 1, fsdp), "sub", s, 1, sub)
-        up = up.reshape(2, sub, fsdp, -1, columns).swapaxes(1, 2).reshape(2, -1, columns)
+        up = [up.reshape(2, sub, fsdp, -1, columns).swapaxes(1, 2).reshape(2, -1, columns)]
 
     count = group * tokens
     per_head = jax.ShapeDtypeStruct((heads, count, HD), f32)
-    *state, near_a = pl.pallas_call(
-        functools.partial(cache_kernel, group),
+    *state, up = pl.pallas_call(
+        functools.partial(cache_kernel, group, len(up)),
         out_shape=[
             jax.ShapeDtypeStruct((heads, count, HD), bf16),
             per_head,
             per_head,
             per_head,
-            jax.ShapeDtypeStruct(a_factor.shape, bf16),
+            jax.ShapeDtypeStruct((2, len(up) * up[0].shape[1], columns), bf16),
         ],
-        in_specs=[smem()] + [pl.BlockSpec(memory_space=pltpu.HBM)] * 3,
+        in_specs=[smem(), vmem()] + [pl.BlockSpec(memory_space=pltpu.HBM)] * 2 + [vmem()] * len(up),
         out_specs=[vmem()] * 5,
         scratch_shapes=[
             pltpu.VMEM(queries.shape, bf16),
             pltpu.VMEM(kv_cache.shape, bf16),
-            pltpu.SemaphoreType.DMA((4,)),
+            pltpu.SemaphoreType.DMA((3,)),
         ],
         compiler_params=params(40),
         cost_estimate=cost(C_CACHED),
         name="cached",
-    )(lengths, queries, kv_cache, a_factor)
+    )(lengths, tick, queries, kv_cache, *up)
 
     def place_of(items):
         return [((r ^ k) * sub + (s ^ e)).astype(jnp.int32) for k, e, _ in items]
 
-    xs, near_a = lax.optimization_barrier((xs, near_a))
-    near = [(0, 0, near_a)] + near
+    xs, near_a = lax.optimization_barrier((xs, up))
+    if tp == 2:
+        pairs = [(i * tp + i // inner, i * tp + 1 - i // inner) for i in range(fsdp)]
+        xs = [inputs, xs[0], lax.ppermute(xs[0], ("fsdp", "tp"), pairs)]
+    else:
+        xs = jnp.stack(xs)
+        xs = [lax.dynamic_index_in_dim(xs, (t - p - j) % tp, keepdims=False) for j in range(tp)]
+    near = [(0, 0, a_factor)] + near
+    up = [up, over_fsdp(up, inner)] if direct else [up]
     width = 2 * columns + 2 * ranks
     part, x = pl.pallas_call(
         functools.partial(early_kernel, tp, wide // 4),
@@ -333,11 +348,11 @@
         others.append(lax.ppermute(parts[j], "fsdp", pairs))
 
     if direct:
-        piece = up[0].shape
+        rows_up = up[0].shape[1] * 2
         mine = pl.pallas_call(
             collect_kernel,
-            out_shape=jax.ShapeDtypeStruct((2, fsdp * piece[1], columns), bf16),
-            in_specs=[vmem()] * fsdp,
+            out_shape=jax.ShapeDtypeStruct((2, rows_up, columns), bf16),
+            in_specs=[vmem()] * 2,
             out_specs=vmem(),
             compiler_params=params(),
             name="collect",
@@ -346,12 +361,14 @@
         place = [(f ^ k) * sub + (s ^ e) for e in range(sub) for k in range(fsdp)]
         up = pl.pallas_call(
             functools.partial(order_kernel, fsdp),
-            out_shape=jax.ShapeDtypeStruct((2, sub * fsdp * piece[1], columns), bf16),
+            out_shape=jax.ShapeDtypeStruct((2, sub * rows_up, columns), bf16),
             in_specs=[smem()] + [vmem()] * sub,
             out_specs=vmem(),
             compiler_params=params(),
             name="order",
         )(jnp.stack(place).astype(jnp.int32), *up)
+    else:
+        up = up[0]
 
     own = pl.pallas_call(
         functools.partial(rank_kernel, columns),

time: 38.8 us -> 37.3 us (0.961)
  waiting for transfers between devices: 10.7 us -> 18.4 us
  starting transfers between devices: 14 us -> 6.88 us
  local copies, waits for them, and re-layouts: 3.85 us -> 0.79 us
  Pallas kernels: 8.95 us -> 10 us
    unnamed x12 -> x14, local copies, waits for them, and re-layouts: 3.76 us -> 0.71 us
    ppermute x4 -> x3, waiting for transfers between devices: 0.01 us -> 2.82 us  [over_fsdp(): return lax.ppermute(x, 'fsdp', [(i, i ^ k) for i in range(fsdp)])]
    ppermute x1, waiting for transfers between devices: 0.01 us -> 2.64 us  [local(): xs = [inputs, xs[0], lax.ppermute(xs[0], ('fsdp', 'tp'), pairs)]]
    ppermute x4 -> x3, starting transfers between devices: 5.96 us -> 3.55 us  [over_fsdp(): return lax.ppermute(x, 'fsdp', [(i, i ^ k) for i in range(fsdp)])]
    ppermute x1, starting transfers between devices: 2.16 us -> 0.31 us  [local(): lax.ppermute(own, 'tp', [(j, (j + i) % tp) for j in range(tp)])]
    ppermute x1, waiting for transfers between devices: 0.89 us -> 2.6 us  [local(): lax.ppermute(own, 'tp', [(j, (j + i) % tp) for j in range(tp)])]
    ppermute x1, starting transfers between devices: 2.99 us -> 1.49 us  [spread(): return lax.ppermute(x, ('fsdp', 'tp'), pairs)]
    ppermute x1, starting transfers between devices: 1.49 us -> 0.03 us  [local(): others.append(lax.ppermute(parts[j], 'fsdp', pairs))]
  transfers between devices with their start and end apart: 11 -> 10, of which waited for: 4 -> 6; matrix products, arithmetic and copies ran while one was open for 1% -> 1% of each run, Pallas kernels for 16% -> 19%
where the time goes in v4:
time: 37.3 us; the launch traced here: 37.1 us
  waiting for transfers between devices  18.4 us (49%)
  Pallas kernels  10 us (27%)
  starting transfers between devices  6.88 us (18%)
  between operations  0.82 us (2%)
  local copies, waits for them, and re-layouts  0.79 us (2%)
    ppermute x1, waiting for transfers between devices, local(): others.append(lax.ppermute(parts[j], 'fsdp', pairs))  4.49 us
    pallas_call x1, Pallas kernels, local(): pl.pallas_call(functools.partial(early_kernel, tp, wide // 4), out_shape=...  4.22 us
    ppermute x1, waiting for transfers between devices, spread(): return lax.ppermute(x, ('fsdp', 'tp'), pairs)  3.98 us
    ppermute x3, starting transfers between devices, over_fsdp(): return lax.ppermute(x, 'fsdp', [(i, i ^ k) for i in range(fsdp)])  3.55 us
    ppermute x3, waiting for transfers between devices, over_fsdp(): return lax.ppermute(x, 'fsdp', [(i, i ^ k) for i in range(fsdp)])  2.82 us
    ppermute x1, waiting for transfers between devices, local(): xs = [inputs, xs[0], lax.ppermute(xs[0], ('fsdp', 'tp'), pairs)]  2.64 us
    ppermute x1, waiting for transfers between devices, local(): lax.ppermute(own, 'tp', [(j, (j + i) % tp) for j in range(tp)])  2.6 us
    pallas_call x1, Pallas kernels, local(): pl.pallas_call(functools.partial(final_kernel, tp, steps, group), out_sha...  1.91 us
  transfers between devices with their start and end apart: 10, of which 6 were waited for; matrix products, arithmetic and copies ran while one was open for 1% of the time, Pallas kernels for 19%

profile of v4, /device:TPU:0, one launch (start us, length us, event | category | flops | bytes accessed | tf_op | source)
XLA Modules:
  0.0 37.1 jit_solution(17642702933853080337)
XLA Ops:
  0.6 0.0 copy-start.1
  0.6 0.0 copy-start
  0.7 0.0 copy-start.3
  0.7 0.0 copy-start.4
  0.7 0.0 copy-start.5
  0.7 0.0 copy-start.2
  0.7 3.1 %collective-permute-start.2 = (bf16[2,32,256]{2,1,0:T(8,128)(2,1)}, bf16[2,32,256]{2,1,0:T(8,128)(2,1)S(1)}, u32[]{:S(2)}, u32[]{:S(2)}) collective-permute-start(bf16[2,32,256]{2,1,0:T(8,128)(2,1)} %bitcast.17), channel_id=1, source_target_pairs={{0,4},{4,0},{8,12},{12,8},{1,5},{5,1},{9,13},{13,9},{2,6},{6,2},{1... | collective-permute-start | bytes 98312 | tf_op jit(solution)/shard_map/ppermute | solution.py:235
  3.8 1.5 %collective-permute-start.1 = (bf16[4,4,4096]{2,1,0:T(4,128)(2,1)}, bf16[4,4,4096]{2,1,0:T(4,128)(2,1)S(1)}, u32[]{:S(2)}, u32[]{:S(2)}) collective-permute-start(bf16[4,4,4096]{2,1,0:T(4,128)(2,1)} %refs_0_.1), channel_id=1, source_target_pairs={{0,2},{2,10},{4,6},{6,14},{8,0},{10,8},{12,4},{14,12},{1,3},{3,11}... | collective-permute-start | bytes 393224 | tf_op jit(solution)/shard_map/ppermute | solution.py:245
  5.3 0.0 collective-permute-start.4
  5.3 0.6 %tick.1.tick_ref = f32[8,128]{1,0:T(8,128)} custom-call(), custom_call_target="tpu_custom_call" | custom-call | flops 8000000000 | bytes 24000000 | tf_op jit(solution)/shard_map/tick/pallas_call | solution.py:249
  5.9 0.0 copy-done.1
  5.9 0.4 %collective-permute-start = (bf16[2,128,1024]{2,1,0:T(8,128)(2,1)S(1)}, bf16[2,128,1024]{2,1,0:T(8,128)(2,1)S(1)}, u32[]{:S(2)}, u32[]{:S(2)}) collective-permute-start(bf16[2,128,1024]{2,1,0:T(8,128)(2,1)S(1)} %copy-done.1), channel_id=1, source_target_pairs={{0,4},{4,0},{8,12},{12,8},{1,5},{5,1},{9,13},{13,9},{2,6},{6,2},{1... | collective-permute-start | bytes 1572872 | tf_op jit(solution)/shard_map/ppermute | solution.py:235
  6.3 0.0 collective-permute-done.2.refs_1_
  6.3 0.0 copy-done
  6.3 0.0 copy-done.3
  6.3 0.0 copy-done.4
  6.3 0.0 copy-done.5
  6.4 0.0 copy-start.6
  6.4 0.7 %copy-done.6 = f32[8,128]{1,0:T(8,128)S(1)} copy-done((f32[8,128]{1,0:T(8,128)S(1)}, f32[8,128]{1,0:T(8,128)}, u32[]{:S(2)}) %copy-start.6) | copy-done | bytes 4120
  7.0 1.7 %cached.1 = (bf16[2,128,128]{2,1,0:T(8,128)(2,1)S(1)}, f32[2,128,128]{2,1,0:T(8,128)S(1)}, f32[2,128,128]{2,1,0:T(8,128)S(1)}, f32[2,128,128]{2,1,0:T(8,128)S(1)}, bf16[2,64,256]{2,1,0:T(8,128)(2,1)S(1)}) custom-call(s32[4]{0:T(128)S(1)} %copy-done.5, f32[8,128]{1,0:T(8,128)S(1)} %copy-done.6, bf16[4,4,2048]{2,1,0:T(4,128)(2,1)S(1)} %copy-done.3, ...), custom_call_target="tpu_custom_call" | custom-call | flops 2000000000 | bytes 6000000 | tf_op jit(solution)/shard_map/cached/pallas_call | solution.py:284
  8.8 4.0 %collective-permute-done.1.refs_1_ = bf16[4,4,4096]{2,1,0:T(4,128)(2,1)S(1)} collective-permute-done((bf16[4,4,4096]{2,1,0:T(4,128)(2,1)}, bf16[4,4,4096]{2,1,0:T(4,128)(2,1)S(1)}, u32[]{:S(2)}, u32[]{:S(2)}) %collective-permute-start.1) | collective-permute-done | bytes 131104 | tf_op jit(solution)/shard_map/ppermute | solution.py:245
  12.8 1.3 %collective-permute-start.3 = (bf16[4,4,4096]{2,1,0:T(4,128)(2,1)S(1)}, bf16[4,4,4096]{2,1,0:T(4,128)(2,1)S(1)}, u32[]{:S(2)}, u32[]{:S(2)}) collective-permute-start(bf16[4,4,4096]{2,1,0:T(4,128)(2,1)S(1)} %collective-permute-done.1.refs_1_), channel_id=1, source_target_pairs={{0,2},{4,6},{10,8},{14,12},{1,3},{5,7},{11,9},{15,13},{16,18},{20,... | collective-permute-start | bytes 393224 | tf_op jit(solution)/shard_map/ppermute | solution.py:311
  14.1 0.1 pad_add_fusion.2.place_ref
  14.2 0.0 collective-permute-start.5
  14.2 2.6 %collective-permute-done.3.refs_2_ = bf16[4,4,4096]{2,1,0:T(4,128)(2,1)S(1)} collective-permute-done((bf16[4,4,4096]{2,1,0:T(4,128)(2,1)S(1)}, bf16[4,4,4096]{2,1,0:T(4,128)(2,1)S(1)}, u32[]{:S(2)}, u32[]{:S(2)}) %collective-permute-start.3) | collective-permute-done | bytes 131104 | tf_op jit(solution)/shard_map/ppermute | solution.py:311
  16.8 0.0 collective-permute-done.4.refs_4_
  16.8 0.0 copy-done.2
  16.8 4.2 %early.1 = (f32[32,768]{1,0:T(8,128)S(1)}, bf16[32,4096]{1,0:T(8,128)(2,1)S(1)}) custom-call(s32[4]{0:T(128)S(1)} %pad_add_fusion.2.place_ref, bf16[2,8192,256]{2,1,0:T(8,128)(2,1)} %base_hbm.1, bf16[4,4,4096]{2,1,0:T(4,128)(2,1)S(1)} %copy-done.2, bf16[4,4,4096]{2,1,0:T(4,128)(2,1)S(1)} %collective-permute-done.1.refs_1_, ...), custom_call_target="tpu_custom_call" | custom-call | flops 3000000000 | bytes 9000000 | tf_op jit(solution)/shard_map/early/pallas_call | solution.py:318
  21.1 0.0 collective-permute-done.5.refs_1_
  21.1 2.8 %collective-permute-done.refs_0_ = bf16[2,128,1024]{2,1,0:T(8,128)(2,1)S(1)} collective-permute-done((bf16[2,128,1024]{2,1,0:T(8,128)(2,1)S(1)}, bf16[2,128,1024]{2,1,0:T(8,128)(2,1)S(1)}, u32[]{:S(2)}, u32[]{:S(2)}) %collective-permute-start) | collective-permute-done | bytes 524320 | tf_op jit(solution)/shard_map/ppermute | solution.py:235
  23.9 0.0 collective-permute-start.6
  23.9 0.1 pad_add_fusion.1.place_ref
  24.0 1.8 %collective-permute-done.6.refs_1_ = bf16[2,128,1024]{2,1,0:T(8,128)(2,1)S(1)} collective-permute-done((bf16[2,128,1024]{2,1,0:T(8,128)(2,1)S(1)}, bf16[2,128,1024]{2,1,0:T(8,128)(2,1)S(1)}, u32[]{:S(2)}, u32[]{:S(2)}) %collective-permute-start.6) | collective-permute-done | bytes 524320 | tf_op jit(solution)/shard_map/ppermute | solution.py:238
  25.8 1.0 %late.1 = (f32[16,768]{1,0:T(8,128)S(1)}, bf16[16,768]{1,0:T(8,128)(2,1)S(1)}) custom-call(s32[2]{0:T(128)S(1)} %pad_add_fusion.1.place_ref, f32[32,768]{1,0:T(8,128)S(1)} %get-tuple-element.27.part_ref, bf16[32,4096]{1,0:T(8,128)(2,1)S(1)} %get-tuple-element.28.x_ref, bf16[2,128,1024]{2,1,0:T(8,128)(2,1)S(1)} %collective-permute-done.refs_0_, ...), custom_call_target="tpu_custom_call" | custom-call | tf_op jit(solution)/shard_map/late/pallas_call | solution.py:335
  26.8 0.0 collective-permute-start.7
  26.8 0.2 collective-permute-start.9
  27.0 4.5 %collective-permute-done.7.refs_0_ = bf16[16,768]{1,0:T(8,128)(2,1)S(1)} collective-permute-done((bf16[16,768]{1,0:T(8,128)(2,1)S(1)}, bf16[16,768]{1,0:T(8,128)(2,1)S(1)}, u32[]{:S(2)}, u32[]{:S(2)}) %collective-permute-start.7) | collective-permute-done | bytes 24608 | tf_op jit(solution)/shard_map/ppermute | solution.py:348
  31.5 0.3 collective-permute-start.8
  31.9 0.1 pad_add_fusion.place_ref
  31.9 0.1 stack.83.place_ref
  32.0 0.0 collective-permute-done.9.refs_1_
  32.0 0.6 %order.1.refs_3_ = bf16[2,256,256]{2,1,0:T(8,128)(2,1)S(1)} custom-call(s32[8]{0:T(128)S(1)} %stack.83.place_ref, bf16[2,128,256]{2,1,0:T(8,128)(2,1)S(1)} %collect.1.refs_0_, bf16[2,128,256]{2,1,0:T(8,128)(2,1)S(1)} %collective-permute-done.9.refs_1_), custom_call_target="tpu_custom_call" | custom-call | tf_op jit(solution)/shard_map/order/pallas_call | solution.py:362
  32.6 2.6 %collective-permute-done.8.refs_2_ = bf16[16,256]{1,0:T(8,128)(2,1)S(1)} collective-permute-done((bf16[16,256]{1,0:T(8,128)(2,1)S(1)}, bf16[16,256]{1,0:T(8,128)(2,1)S(1)}, u32[]{:S(2)}, u32[]{:S(2)}) %collective-permute-start.8) | collective-permute-done | bytes 8224 | tf_op jit(solution)/shard_map/ppermute | solution.py:383
  35.2 1.9 %final.1 = (bf16[2,4,4,256]{3,2,1,0:T(4,128)(2,1)}, bf16[4,4,2048]{2,1,0:T(4,128)(2,1)}) custom-call(s32[2]{0:T(128)S(1)} %pad_add_fusion.place_ref, f32[16,768]{1,0:T(8,128)S(1)} %get-tuple-element.34.mine_ref, bf16[16,768]{1,0:T(8,128)(2,1)S(1)} %collective-permute-done.7.refs_0_, bf16[16,256]{1,0:T(8,128)(2,1)S(1)} %ranks.1.refs_1_, ...), custom_call_target="tpu_custom_call" | custom-call | tf_op jit(solution)/shard_map/final/pallas_call | solution.py:386
  (2 shorter events, 0.0 us)
Async XLA Ops:
  0.6 5.2 %copy-start.1 = (bf16[2,128,1024]{2,1,0:T(8,128)(2,1)S(1)}, bf16[2,128,1024]{2,1,0:T(8,128)(2,1)}, u32[]{:S(2)}) copy-start(bf16[2,128,1024]{2,1,0:T(8,128)(2,1)} %refs_3_.1) | copy-start | bytes 1572868
  0.6 5.7 %copy-start = (bf16[2,4,256,256]{3,2,1,0:T(8,128)(2,1)S(1)}, bf16[2,4,256,256]{3,2,1,0:T(8,128)(2,1)}, u32[]{:S(2)}) copy-start(bf16[2,4,256,256]{3,2,1,0:T(8,128)(2,1)} %kv_hbm.1) | copy-start | bytes 3145732
  0.7 5.7 %copy-start.3 = (bf16[4,4,2048]{2,1,0:T(4,128)(2,1)S(1)}, bf16[4,4,2048]{2,1,0:T(4,128)(2,1)}, u32[]{:S(2)}) copy-start(bf16[4,4,2048]{2,1,0:T(4,128)(2,1)} %q_hbm.1) | copy-start | bytes 196612
  0.7 5.7 %copy-start.4 = (bf16[2,256,32]{1,2,0:T(8,128)(2,1)S(1)}, bf16[2,256,32]{1,2,0:T(8,128)(2,1)}, u32[]{:S(2)}) copy-start(bf16[2,256,32]{1,2,0:T(8,128)(2,1)} %param.13) | copy-start | bytes 98308
  0.7 5.7 %copy-start.5 = (s32[4]{0:T(128)S(1)}, s32[4]{0:T(128)}, u32[]{:S(2)}) copy-start(s32[4]{0:T(128)} %len_ref.1) | copy-start | bytes 52
  0.7 16.2 %copy-start.2 = (bf16[4,4,4096]{2,1,0:T(4,128)(2,1)S(1)}, bf16[4,4,4096]{2,1,0:T(4,128)(2,1)}, u32[]{:S(2)}) copy-start(bf16[4,4,4096]{2,1,0:T(4,128)(2,1)} %refs_0_.1) | copy-start | bytes 393220
  0.7 5.6 %collective-permute-start.2 = (bf16[2,32,256]{2,1,0:T(8,128)(2,1)}, bf16[2,32,256]{2,1,0:T(8,128)(2,1)S(1)}, u32[]{:S(2)}, u32[]{:S(2)}) collective-permute-start(bf16[2,32,256]{2,1,0:T(8,128)(2,1)} %bitcast.17), channel_id=1, source_target_pairs={{0,4},{4,0},{8,12},{12,8},{1,5},{5,1},{9,13},{13,9},{2,6},{6,2},{1... | collective-permute-start | bytes 98312 | tf_op jit(solution)/shard_map/ppermute | solution.py:235
  3.8 9.0 %collective-permute-start.1 = (bf16[4,4,4096]{2,1,0:T(4,128)(2,1)}, bf16[4,4,4096]{2,1,0:T(4,128)(2,1)S(1)}, u32[]{:S(2)}, u32[]{:S(2)}) collective-permute-start(bf16[4,4,4096]{2,1,0:T(4,128)(2,1)} %refs_0_.1), channel_id=1, source_target_pairs={{0,2},{2,10},{4,6},{6,14},{8,0},{10,8},{12,4},{14,12},{1,3},{3,11}... | collective-permute-start | bytes 393224 | tf_op jit(solution)/shard_map/ppermute | solution.py:245
  5.3 11.6 %collective-permute-start.4 = (bf16[2,128,1024]{2,1,0:T(8,128)(2,1)}, bf16[2,128,1024]{2,1,0:T(8,128)(2,1)}, u32[]{:S(2)}, u32[]{:S(2)}) collective-permute-start(bf16[2,128,1024]{2,1,0:T(8,128)(2,1)} %refs_3_.1), channel_id=1, source_target_pairs={{0,1},{1,0},{2,3},{3,2},{4,5},{5,4},{6,7},{7,6},{8,9},{9,8},{10,11... | collective-permute-start | bytes 1572872 | tf_op jit(solution)/shard_map/ppermute | solution.py:238
  5.9 18.0 %collective-permute-start = (bf16[2,128,1024]{2,1,0:T(8,128)(2,1)S(1)}, bf16[2,128,1024]{2,1,0:T(8,128)(2,1)S(1)}, u32[]{:S(2)}, u32[]{:S(2)}) collective-permute-start(bf16[2,128,1024]{2,1,0:T(8,128)(2,1)S(1)} %copy-done.1), channel_id=1, source_target_pairs={{0,4},{4,0},{8,12},{12,8},{1,5},{5,1},{9,13},{13,9},{2,6},{6,2},{1... | collective-permute-start | bytes 1572872 | tf_op jit(solution)/shard_map/ppermute | solution.py:235
  6.4 0.7 %copy-start.6 = (f32[8,128]{1,0:T(8,128)S(1)}, f32[8,128]{1,0:T(8,128)}, u32[]{:S(2)}) copy-start(f32[8,128]{1,0:T(8,128)} %tick.1.tick_ref) | copy-start | bytes 12292
  12.8 4.1 %collective-permute-start.3 = (bf16[4,4,4096]{2,1,0:T(4,128)(2,1)S(1)}, bf16[4,4,4096]{2,1,0:T(4,128)(2,1)S(1)}, u32[]{:S(2)}, u32[]{:S(2)}) collective-permute-start(bf16[4,4,4096]{2,1,0:T(4,128)(2,1)S(1)} %collective-permute-done.1.refs_1_), channel_id=1, source_target_pairs={{0,2},{4,6},{10,8},{14,12},{1,3},{5,7},{11,9},{15,13},{16,18},{20,... | collective-permute-start | bytes 393224 | tf_op jit(solution)/shard_map/ppermute | solution.py:311
  14.2 6.9 %collective-permute-start.5 = (bf16[2,64,256]{2,1,0:T(8,128)(2,1)S(1)}, bf16[2,64,256]{2,1,0:T(8,128)(2,1)S(1)}, u32[]{:S(2)}, u32[]{:S(2)}) collective-permute-start(bf16[2,64,256]{2,1,0:T(8,128)(2,1)S(1)} %get-tuple-element.36.refs_0_), channel_id=1, source_target_pairs={{0,8},{4,12},{8,0},{12,4},{1,9},{5,13},{9,1},{13,5},{2,10},{6,14},... | collective-permute-start | bytes 196616 | tf_op jit(solution)/shard_map/ppermute | solution.py:235
  23.9 1.9 %collective-permute-start.6 = (bf16[2,128,1024]{2,1,0:T(8,128)(2,1)S(1)}, bf16[2,128,1024]{2,1,0:T(8,128)(2,1)S(1)}, u32[]{:S(2)}, u32[]{:S(2)}) collective-permute-start(bf16[2,128,1024]{2,1,0:T(8,128)(2,1)S(1)} %collective-permute-done.refs_0_), channel_id=1, source_target_pairs={{0,1},{1,0},{2,3},{3,2},{4,5},{5,4},{6,7},{7,6},{8,9},{9,8},{10,11... | collective-permute-start | bytes 1572872 | tf_op jit(solution)/shard_map/ppermute | solution.py:238
  26.8 4.8 %collective-permute-start.7 = (bf16[16,768]{1,0:T(8,128)(2,1)S(1)}, bf16[16,768]{1,0:T(8,128)(2,1)S(1)}, u32[]{:S(2)}, u32[]{:S(2)}) collective-permute-start(bf16[16,768]{1,0:T(8,128)(2,1)S(1)} %get-tuple-element.35), channel_id=1, source_target_pairs={{0,8},{4,12},{8,0},{12,4},{1,9},{5,13},{9,1},{13,5},{2,10},{6,14},... | collective-permute-start | bytes 73736 | tf_op jit(solution)/shard_map/ppermute | solution.py:348
  26.8 5.2 %collective-permute-start.9 = (bf16[2,128,256]{2,1,0:T(8,128)(2,1)S(1)}, bf16[2,128,256]{2,1,0:T(8,128)(2,1)S(1)}, u32[]{:S(2)}, u32[]{:S(2)}) collective-permute-start(bf16[2,128,256]{2,1,0:T(8,128)(2,1)S(1)} %collect.1.refs_0_), channel_id=1, source_target_pairs={{0,1},{1,0},{2,3},{3,2},{4,5},{5,4},{6,7},{7,6},{8,9},{9,8},{10,11... | collective-permute-start | bytes 393224 | tf_op jit(solution)/shard_map/ppermute | solution.py:238
  31.5 3.7 %collective-permute-start.8 = (bf16[16,256]{1,0:T(8,128)(2,1)S(1)}, bf16[16,256]{1,0:T(8,128)(2,1)S(1)}, u32[]{:S(2)}, u32[]{:S(2)}) collective-permute-start(bf16[16,256]{1,0:T(8,128)(2,1)S(1)} %ranks.1.refs_1_), channel_id=1, source_target_pairs={{0,2},{2,0},{1,3},{3,1},{4,6},{6,4},{5,7},{7,5},{8,10},{10,8},{9,1... | collective-permute-start | bytes 24584 | tf_op jit(solution)/shard_map/ppermute | solution.py:383

commit v5 on v4

--- a/solution.py
+++ b/solution.py
@@ -25,6 +25,11 @@
 
 def cost(us):
     return pl.CostEstimate(flops=int(us * 1e9), bytes_accessed=int(us * 3e6), transcendentals=0)
+
+
+def places(sizes, items):
+    row, core = lax.rem(lax.axis_index("fsdp"), sizes[0] // sizes[1]), lax.axis_index("sub")
+    return [(row ^ k) * sizes[2] + (core ^ e) for k, e in items]
 
 
 def vmem():
@@ -88,14 +93,16 @@
         sum_out[g] = jnp.broadcast_to(total, (count, HD))
 
 
-def early_kernel(blocks, chunk, place_ref, base_hbm, *refs):
+def early_kernel(blocks, chunk, sizes, items, base_hbm, *refs):
     x_refs, refs = refs[:blocks], refs[blocks:]
     if blocks == 2:
         x_refs, refs = x_refs + refs[:1], refs[1:]
     a_refs, (out_ref, x_out, base_ref, sems) = refs[:-4], refs[-4:]
     columns, slab, ranks = base_hbm.shape[2], a_refs[0].shape[2], a_refs[0].shape[1]
     rows, steps, wide = x_refs[0].shape
-    first = pl.multiple_of(place_ref[len(a_refs) + 1] * wide, wide)
+    block = lax.div(lax.axis_index("fsdp"), sizes[0] // sizes[1])
+    place = places(sizes, items)
+    first = pl.multiple_of(block * wide, wide)
     copies = []
     for i in range(wide // chunk):
         for m in range(2):
@@ -108,7 +115,7 @@
             )
     for copy in copies:
         copy.start()
-    moved = place_ref[len(a_refs)] == 1
+    moved = lax.axis_index("tp") != block
     for k in range(blocks):
         pieces = []
         for b in range(rows):
@@ -119,12 +126,11 @@
         x = jnp.concatenate(pieces, axis=0)
         x_out[k * rows * steps : (k + 1) * rows * steps] = x.astype(jnp.bfloat16)
     count = blocks * rows * steps
-    for m in range(2):
-        total = jnp.zeros((count, ranks), jnp.float32)
-        for i, a in enumerate(a_refs):
-            start = pl.multiple_of(place_ref[i] * slab, slab)
-            total = total + dot(x_out[:, pl.ds(start, slab)], a[m], NT)
-        out_ref[:, 2 * columns + m * ranks : 2 * columns + (m + 1) * ranks] = total
+    total = jnp.zeros((count, 2 * ranks), jnp.float32)
+    for i, a in enumerate(a_refs):
+        start = pl.multiple_of(place[i] * slab, slab)
+        total = total + dot(x_out[:, pl.ds(start, slab)], a[...].reshape(2 * ranks, slab), NT)
+    out_ref[:, 2 * columns :] = total
     totals = [jnp.zeros((count, columns), jnp.float32) for _ in range(2)]
     for i in range(wide // chunk):
         at = slice(i * chunk, (i + 1) * chunk)
@@ -135,20 +141,19 @@
         out_ref[:, m * columns : (m + 1) * columns] = totals[m]
 
 
-def late_kernel(blocks, columns, place_ref, part_ref, x_ref, *refs):
+def late_kernel(blocks, columns, sizes, items, part_ref, x_ref, *refs):
     a_refs, outs = refs[:-blocks], refs[-blocks:]
     tokens = outs[0].shape[0]
     slab, ranks = a_refs[0].shape[2], a_refs[0].shape[1]
-    sums = [part_ref[:, : 2 * columns]]
-    for m in range(2):
-        total = part_ref[:, 2 * columns + m * ranks : 2 * columns + (m + 1) * ranks]
-        for i, a in enumerate(a_refs):
-            start = pl.multiple_of(place_ref[i] * slab, slab)
-            total = total + dot(x_ref[:, pl.ds(start, slab)], a[m], NT)
-        sums.append(total)
-    whole = jnp.concatenate(sums, axis=1)
+    place = places(sizes, items)
+    total = part_ref[:, 2 * columns :]
+    for i, a in enumerate(a_refs):
+        start = pl.multiple_of(place[i] * slab, slab)
+        total = total + dot(x_ref[:, pl.ds(start, slab)], a[...].reshape(2 * ranks, slab), NT)
     for j, out in enumerate(outs):
-        out[...] = whole[j * tokens : (j + 1) * tokens].astype(out.dtype)
+        at = slice(j * tokens, (j + 1) * tokens)
+        out[:, : 2 * columns] = part_ref[at, : 2 * columns].astype(out.dtype)
+        out[:, 2 * columns :] = total[at].astype(out.dtype)
 
 
 def tick_kernel(out_ref):
@@ -161,12 +166,13 @@
         refs[-1][:, k * rows : (k + 1) * rows] = ref[...]
 
 
-def order_kernel(count, place_ref, *refs):
+def order_kernel(count, cores, *refs):
     out = refs[-1]
+    f, s = lax.axis_index("fsdp"), lax.axis_index("sub")
     rows = refs[0].shape[1] // count
     for i, ref in enumerate(refs[:-1]):
         for k in range(count):
-            start = pl.multiple_of(place_ref[i * count + k] * rows, rows)
+            start = pl.multiple_of(((f ^ k) * cores + (s ^ i)) * rows, rows)
             out[:, pl.ds(start, rows)] = ref[:, k * rows : (k + 1) * rows]
 
 
@@ -177,21 +183,31 @@
     refs[-1][...] = total.astype(jnp.bfloat16)
 
 
-def final_kernel(blocks, steps, group, place_ref, mine_ref, *refs):
-    others, refs = refs[: blocks - 1], refs[blocks - 1 :]
-    rank_refs, refs = refs[:blocks], refs[blocks:]
-    up_ref, q_ref, acc_ref, top_ref, sum_ref, fresh_out, out = refs
-    tokens, columns = mine_ref.shape[0], fresh_out.shape[3]
-    rows, heads = tokens // steps, columns // HD
-    ranks = rank_refs[0].shape[1] // 2
-    fresh = []
+def first_kernel(blocks, mine_ref, *refs):
+    others, (rank_ref, up_ref, out_ref) = refs[: blocks - 1], refs[blocks - 1 :]
+    columns, ranks = up_ref.shape[2], rank_ref.shape[1] // 2
+    start = pl.multiple_of(lax.axis_index("tp") * ranks, ranks)
     for m in range(2):
         cols = slice(m * columns, (m + 1) * columns)
         total = mine_ref[:, cols]
         for other in others:
             total = total + other[:, cols].astype(jnp.float32)
+        rank = rank_ref[:, m * ranks : (m + 1) * ranks]
+        out_ref[:, cols] = total + dot(rank, up_ref[m, pl.ds(start, ranks)])
+
+
+def final_kernel(blocks, steps, group, sum_in, *refs):
+    rank_refs, refs = refs[: blocks - 1], refs[blocks - 1 :]
+    up_ref, q_ref, acc_ref, top_ref, sum_ref, fresh_out, out = refs
+    tokens, columns = sum_in.shape[0], fresh_out.shape[3]
+    rows, heads = tokens // steps, columns // HD
+    ranks = rank_refs[0].shape[1] // 2
+    fresh = []
+    for m in range(2):
+        total = sum_in[:, m * columns : (m + 1) * columns]
         for i, rank in enumerate(rank_refs):
-            start = pl.multiple_of(place_ref[i] * ranks, ranks)
+            other = lax.rem(lax.axis_index("tp") - (i + 1) + blocks, blocks)
+            start = pl.multiple_of(other * ranks, ranks)
             total = total + dot(rank[:, m * ranks : (m + 1) * ranks], up_ref[m, pl.ds(start, ranks)])
         for b in range(rows):
             fresh_out[m, b] = total[b * steps : (b + 1) * steps].astype(jnp.bfloat16)
@@ -302,9 +318,6 @@
         name="cached",
     )(lengths, tick, queries, kv_cache, *up)
 
-    def place_of(items):
-        return [((r ^ k) * sub + (s ^ e)).astype(jnp.int32) for k, e, _ in items]
-
     xs, near_a = lax.optimization_barrier((xs, up))
     if tp == 2:
         pairs = [(i * tp + i // inner, i * tp + 1 - i // inner) for i in range(fsdp)]
@@ -316,30 +329,30 @@
     up = [up, over_fsdp(up, inner)] if direct else [up]
     width = 2 * columns + 2 * ranks
     part, x = pl.pallas_call(
-        functools.partial(early_kernel, tp, wide // 4),
+        functools.partial(early_kernel, tp, wide // 4, sizes, [(k, e) for k, e, _ in near]),
         out_shape=[
             jax.ShapeDtypeStruct((tp * tokens, width), f32),
             jax.ShapeDtypeStruct((tp * tokens, wide), bf16),
         ],
-        in_specs=[smem(), pl.BlockSpec(memory_space=pltpu.HBM)] + [vmem()] * (len(xs) + len(near)),
+        in_specs=[pl.BlockSpec(memory_space=pltpu.HBM)] + [vmem()] * (len(xs) + len(near)),
         out_specs=[vmem()] * 2,
         scratch_shapes=[pltpu.VMEM((2, wide, columns), bf16), pltpu.SemaphoreType.DMA((8,))],
         compiler_params=params(50),
         cost_estimate=cost(C_EARLY),
         name="early",
-    )(jnp.stack(place_of(near) + [(t != p).astype(jnp.int32), p.astype(jnp.int32)]), base, *xs, *[a for _, _, a in near])
+    )(base, *xs, *[a for _, _, a in near])
 
     far, part, up = lax.optimization_barrier((far, part, up))
     late_at = [(k, e) for k in range(1, inner) for e in range(sub)]
     late = [over_sub(far[k - 1], e) if e else far[k - 1] for k, e in late_at]
     parts = pl.pallas_call(
-        functools.partial(late_kernel, tp, columns),
+        functools.partial(late_kernel, tp, columns, sizes, late_at),
         out_shape=[jax.ShapeDtypeStruct((tokens, width), f32 if j == 0 else bf16) for j in range(tp)],
-        in_specs=[smem()] + [vmem()] * (2 + len(late)),
+        in_specs=[vmem()] * (2 + len(late)),
         out_specs=[vmem()] * tp,
         compiler_params=params(),
         name="late",
-    )(jnp.stack(place_of([(k, e, None) for k, e in late_at])), part, x, *late)
+    )(part, x, *late)
 
     parts, up = lax.optimization_barrier((parts, up))
     others = []
@@ -358,15 +371,14 @@
             name="collect",
         )(*up)
         up = [mine] + [over_sub(mine, e) for e in range(1, sub)]
-        place = [(f ^ k) * sub + (s ^ e) for e in range(sub) for k in range(fsdp)]
         up = pl.pallas_call(
-            functools.partial(order_kernel, fsdp),
+            functools.partial(order_kernel, fsdp, sub),
             out_shape=jax.ShapeDtypeStruct((2, sub * rows_up, columns), bf16),
-            in_specs=[smem()] + [vmem()] * sub,
+            in_specs=[vmem()] * sub,
             out_specs=vmem(),
             compiler_params=params(),
             name="order",
-        )(jnp.stack(place).astype(jnp.int32), *up)
+        )(*up)
     else:
         up = up[0]
 
@@ -381,19 +393,26 @@
     rank_parts = [own]
     for i in range(1, tp):
         rank_parts.append(lax.ppermute(own, "tp", [(j, (j + i) % tp) for j in range(tp)]))
-    rank_place = jnp.stack([((t - i + tp) % tp).astype(jnp.int32) for i in range(tp)])
-
+
+    first = pl.pallas_call(
+        functools.partial(first_kernel, tp),
+        out_shape=jax.ShapeDtypeStruct((tokens, 2 * columns), f32),
+        in_specs=[vmem()] * (tp + 2),
+        out_specs=vmem(),
+        compiler_params=params(),
+        name="first",
+    )(parts[0], *others, own, up)
     fresh, attended = pl.pallas_call(
         functools.partial(final_kernel, tp, steps, group),
         out_shape=(
             jax.ShapeDtypeStruct((2, row_count, steps, columns), bf16),
             jax.ShapeDtypeStruct(queries.shape, bf16),
         ),
-        in_specs=[smem()] + [vmem()] * (2 * tp + 5),
+        in_specs=[vmem()] * (tp + 5),
         out_specs=[vmem(), vmem()],
         compiler_params=params(),
         name="final",
-    )(rank_place, parts[0], *others, *rank_parts, up, *state)
+    )(first, *rank_parts[1:], up, *state)
     return fresh, attended
 
 

time: 37.3 us -> 36.4 us (0.976)
  Pallas kernels: 10 us -> 7.71 us
  waiting for transfers between devices: 18.4 us -> 19.8 us
    pallas_call x3 -> x4, Pallas kernels: 5.77 us -> 4.01 us  [the longest x1 3.43 us: local(): pl.pallas_call(functools.partial(early_kernel, tp, wide // 4, sizes, [(k,...]
    ppermute x3, waiting for transfers between devices: 2.82 us -> 3.61 us  [over_fsdp(): return lax.ppermute(x, 'fsdp', [(i, i ^ k) for i in range(fsdp)])]
    pallas_call x1, Pallas kernels: 1.91 us -> 1.36 us  [local(): pl.pallas_call(functools.partial(final_kernel, tp, steps, group), out_sha...]
  transfers between devices with their start and end apart: 10 -> 10, of which waited for: 6 -> 6; matrix products, arithmetic and copies ran while one was open for 1% -> 0% of each run, Pallas kernels for 19% -> 16%
where the time goes in v5:
time: 36.4 us; the launch traced here: 36.2 us
  waiting for transfers between devices  19.8 us (54%)
  Pallas kernels  7.71 us (21%)
  starting transfers between devices  7.17 us (20%)
  between operations  0.77 us (2%)
  local copies, waits for them, and re-layouts  0.71 us (2%)
    ppermute x1, waiting for transfers between devices, local(): others.append(lax.ppermute(parts[j], 'fsdp', pairs))  4.74 us
    ppermute x1, waiting for transfers between devices, spread(): return lax.ppermute(x, ('fsdp', 'tp'), pairs)  3.98 us
    ppermute x3, starting transfers between devices, over_fsdp(): return lax.ppermute(x, 'fsdp', [(i, i ^ k) for i in range(fsdp)])  3.61 us
    ppermute x3, waiting for transfers between devices, over_fsdp(): return lax.ppermute(x, 'fsdp', [(i, i ^ k) for i in range(fsdp)])  3.61 us
    pallas_call x1, Pallas kernels, local(): pl.pallas_call(functools.partial(early_kernel, tp, wide // 4, sizes, [(k,...  3.43 us
    ppermute x1, waiting for transfers between devices, local(): lax.ppermute(own, 'tp', [(j, (j + i) % tp) for j in range(tp)])  2.89 us
    ppermute x1, waiting for transfers between devices, local(): xs = [inputs, xs[0], lax.ppermute(xs[0], ('fsdp', 'tp'), pairs)]  2.7 us
    ppermute x3, waiting for transfers between devices, over_sub(): return lax.ppermute(x, 'sub', [(i, i ^ k) for i in range(sub)])  1.91 us
  transfers between devices with their start and end apart: 10, of which 6 were waited for; matrix products, arithmetic and copies ran while one was open for 0% of the time, Pallas kernels for 16%

profile of v5, /device:TPU:0, one launch (start us, length us, event | category | flops | bytes accessed | tf_op | source)
XLA Modules:
  0.0 36.2 jit_solution(4170485983520038857)
XLA Ops:
  0.6 0.0 copy-start.1
  0.6 0.0 copy-start
  0.7 0.0 copy-start.3
  0.7 0.0 copy-start.4
  0.7 0.0 copy-start.5
  0.7 0.0 copy-start.2
  0.7 3.1 %collective-permute-start.2 = (bf16[2,32,256]{2,1,0:T(8,128)(2,1)}, bf16[2,32,256]{2,1,0:T(8,128)(2,1)S(1)}, u32[]{:S(2)}, u32[]{:S(2)}) collective-permute-start(bf16[2,32,256]{2,1,0:T(8,128)(2,1)} %bitcast.1), channel_id=1, source_target_pairs={{0,4},{4,0},{8,12},{12,8},{1,5},{5,1},{9,13},{13,9},{2,6},{6,2},{1... | collective-permute-start | bytes 98312 | tf_op jit(solution)/shard_map/ppermute | solution.py:251
  3.8 1.5 %collective-permute-start.1 = (bf16[4,4,4096]{2,1,0:T(4,128)(2,1)}, bf16[4,4,4096]{2,1,0:T(4,128)(2,1)S(1)}, u32[]{:S(2)}, u32[]{:S(2)}) collective-permute-start(bf16[4,4,4096]{2,1,0:T(4,128)(2,1)} %refs_0_.1), channel_id=1, source_target_pairs={{0,2},{2,10},{4,6},{6,14},{8,0},{10,8},{12,4},{14,12},{1,3},{3,11}... | collective-permute-start | bytes 393224 | tf_op jit(solution)/shard_map/ppermute | solution.py:261
  5.3 0.0 collective-permute-start.4
  5.3 0.6 %tick.1.tick_ref = f32[8,128]{1,0:T(8,128)} custom-call(), custom_call_target="tpu_custom_call" | custom-call | flops 8000000000 | bytes 24000000 | tf_op jit(solution)/shard_map/tick/pallas_call | solution.py:265
  5.9 0.0 copy-done.1
  5.9 0.4 %collective-permute-start = (bf16[2,128,1024]{2,1,0:T(8,128)(2,1)S(1)}, bf16[2,128,1024]{2,1,0:T(8,128)(2,1)S(1)}, u32[]{:S(2)}, u32[]{:S(2)}) collective-permute-start(bf16[2,128,1024]{2,1,0:T(8,128)(2,1)S(1)} %copy-done.1), channel_id=1, source_target_pairs={{0,4},{4,0},{8,12},{12,8},{1,5},{5,1},{9,13},{13,9},{2,6},{6,2},{1... | collective-permute-start | bytes 1572872 | tf_op jit(solution)/shard_map/ppermute | solution.py:251
  6.3 0.0 collective-permute-done.2.refs_1_
  6.3 0.0 copy-done
  6.3 0.0 copy-done.3
  6.3 0.0 copy-done.4
  6.3 0.0 copy-done.5
  6.4 0.0 copy-start.6
  6.4 0.7 %copy-done.6 = f32[8,128]{1,0:T(8,128)S(1)} copy-done((f32[8,128]{1,0:T(8,128)S(1)}, f32[8,128]{1,0:T(8,128)}, u32[]{:S(2)}) %copy-start.6) | copy-done | bytes 4120
  7.0 1.7 %cached.1 = (bf16[2,128,128]{2,1,0:T(8,128)(2,1)S(1)}, f32[2,128,128]{2,1,0:T(8,128)S(1)}, f32[2,128,128]{2,1,0:T(8,128)S(1)}, f32[2,128,128]{2,1,0:T(8,128)S(1)}, bf16[2,64,256]{2,1,0:T(8,128)(2,1)S(1)}) custom-call(s32[4]{0:T(128)S(1)} %copy-done.5, f32[8,128]{1,0:T(8,128)S(1)} %copy-done.6, bf16[4,4,2048]{2,1,0:T(4,128)(2,1)S(1)} %copy-done.3, ...), custom_call_target="tpu_custom_call" | custom-call | flops 2000000000 | bytes 6000000 | tf_op jit(solution)/shard_map/cached/pallas_call | solution.py:300
  8.8 4.0 %collective-permute-done.1.refs_1_ = bf16[4,4,4096]{2,1,0:T(4,128)(2,1)S(1)} collective-permute-done((bf16[4,4,4096]{2,1,0:T(4,128)(2,1)}, bf16[4,4,4096]{2,1,0:T(4,128)(2,1)S(1)}, u32[]{:S(2)}, u32[]{:S(2)}) %collective-permute-start.1) | collective-permute-done | bytes 131104 | tf_op jit(solution)/shard_map/ppermute | solution.py:261
  12.8 1.3 %collective-permute-start.3 = (bf16[4,4,4096]{2,1,0:T(4,128)(2,1)S(1)}, bf16[4,4,4096]{2,1,0:T(4,128)(2,1)S(1)}, u32[]{:S(2)}, u32[]{:S(2)}) collective-permute-start(bf16[4,4,4096]{2,1,0:T(4,128)(2,1)S(1)} %collective-permute-done.1.refs_1_), channel_id=1, source_target_pairs={{0,2},{4,6},{10,8},{14,12},{1,3},{5,7},{11,9},{15,13},{16,18},{20,... | collective-permute-start | bytes 393224 | tf_op jit(solution)/shard_map/ppermute | solution.py:324
  14.1 0.1 collective-permute-start.5
  14.1 2.7 %collective-permute-done.3.refs_2_ = bf16[4,4,4096]{2,1,0:T(4,128)(2,1)S(1)} collective-permute-done((bf16[4,4,4096]{2,1,0:T(4,128)(2,1)S(1)}, bf16[4,4,4096]{2,1,0:T(4,128)(2,1)S(1)}, u32[]{:S(2)}, u32[]{:S(2)}) %collective-permute-start.3) | collective-permute-done | bytes 131104 | tf_op jit(solution)/shard_map/ppermute | solution.py:324
  16.8 0.0 collective-permute-done.4.refs_4_
  16.8 0.0 copy-done.2
  16.8 3.4 %early.1 = (f32[32,768]{1,0:T(8,128)S(1)}, bf16[32,4096]{1,0:T(8,128)(2,1)S(1)}) custom-call(bf16[2,8192,256]{2,1,0:T(8,128)(2,1)} %base_hbm.1, bf16[4,4,4096]{2,1,0:T(4,128)(2,1)S(1)} %copy-done.2, bf16[4,4,4096]{2,1,0:T(4,128)(2,1)S(1)} %collective-permute-done.1.refs_1_, bf16[4,4,4096]{2,1,0:T(4,128)(2,1)S(1)} %collective-permute-done.3.refs_2_, ...), custom_call_target="tpu_custom_call" | custom-call | flops 3000000000 | bytes 9000000 | tf_op jit(solution)/shard_map/early/pallas_call | solution.py:331
  20.3 0.0 collective-permute-done.5.refs_1_
  20.3 3.6 %collective-permute-done.refs_0_ = bf16[2,128,1024]{2,1,0:T(8,128)(2,1)S(1)} collective-permute-done((bf16[2,128,1024]{2,1,0:T(8,128)(2,1)S(1)}, bf16[2,128,1024]{2,1,0:T(8,128)(2,1)S(1)}, u32[]{:S(2)}, u32[]{:S(2)}) %collective-permute-start) | collective-permute-done | bytes 524320 | tf_op jit(solution)/shard_map/ppermute | solution.py:251
  23.9 0.0 collective-permute-start.6
  23.9 1.9 %collective-permute-done.6.refs_1_ = bf16[2,128,1024]{2,1,0:T(8,128)(2,1)S(1)} collective-permute-done((bf16[2,128,1024]{2,1,0:T(8,128)(2,1)S(1)}, bf16[2,128,1024]{2,1,0:T(8,128)(2,1)S(1)}, u32[]{:S(2)}, u32[]{:S(2)}) %collective-permute-start.6) | collective-permute-done | bytes 524320 | tf_op jit(solution)/shard_map/ppermute | solution.py:254
  25.8 0.4 %late.1 = (f32[16,768]{1,0:T(8,128)S(1)}, bf16[16,768]{1,0:T(8,128)(2,1)S(1)}) custom-call(f32[32,768]{1,0:T(8,128)S(1)} %get-tuple-element.27.part_ref, bf16[32,4096]{1,0:T(8,128)(2,1)S(1)} %get-tuple-element.28.x_ref, bf16[2,128,1024]{2,1,0:T(8,128)(2,1)S(1)} %collective-permute-done.refs_0_, bf16[2,128,1024]{2,1,0:T(8,128)(2,1)S(1)} %collective-permute-done.6.refs_1_), custom_call_target="tpu_custom_call" | custom-call | tf_op jit(solution)/shard_map/late/pallas_call | solution.py:348
  26.2 0.2 collective-permute-start.8
  26.4 0.0 collective-permute-start.7
  26.4 4.7 %collective-permute-done.7.refs_0_ = bf16[16,768]{1,0:T(8,128)(2,1)S(1)} collective-permute-done((bf16[16,768]{1,0:T(8,128)(2,1)S(1)}, bf16[16,768]{1,0:T(8,128)(2,1)S(1)}, u32[]{:S(2)}, u32[]{:S(2)}) %collective-permute-start.7) | collective-permute-done | bytes 24608 | tf_op jit(solution)/shard_map/ppermute | solution.py:361
  31.2 0.6 %collective-permute-start.9 = (bf16[16,256]{1,0:T(8,128)(2,1)S(1)}, bf16[16,256]{1,0:T(8,128)(2,1)S(1)}, u32[]{:S(2)}, u32[]{:S(2)}) collective-permute-start(bf16[16,256]{1,0:T(8,128)(2,1)S(1)} %ranks.1.refs_1_), channel_id=1, source_target_pairs={{0,2},{2,0},{1,3},{3,1},{4,6},{6,4},{5,7},{7,5},{8,10},{10,8},{9,1... | collective-permute-start | bytes 24584 | tf_op jit(solution)/shard_map/ppermute | solution.py:395
  31.8 0.0 collective-permute-done.8.refs_1_
  31.8 0.1 first.1.sum_in
  31.9 2.9 %collective-permute-done.9.refs_0_ = bf16[16,256]{1,0:T(8,128)(2,1)S(1)} collective-permute-done((bf16[16,256]{1,0:T(8,128)(2,1)S(1)}, bf16[16,256]{1,0:T(8,128)(2,1)S(1)}, u32[]{:S(2)}, u32[]{:S(2)}) %collective-permute-start.9) | collective-permute-done | bytes 8224 | tf_op jit(solution)/shard_map/ppermute | solution.py:395
  34.8 1.4 %final.1 = (bf16[2,4,4,256]{3,2,1,0:T(4,128)(2,1)}, bf16[4,4,2048]{2,1,0:T(4,128)(2,1)}) custom-call(f32[16,512]{1,0:T(8,128)S(1)} %first.1.sum_in, bf16[16,256]{1,0:T(8,128)(2,1)S(1)} %collective-permute-done.9.refs_0_, bf16[2,256,256]{2,1,0:T(8,128)(2,1)S(1)} %order.1.refs_2_.refs_1_, bf16[2,128,128]{2,1,0:T(8,128)(2,1)S(1)} %get-tuple-element.38.refs_2_, ...), custom_call_target="tpu_custom_call" | custom-call | tf_op jit(solution)/shard_map/final/pallas_call | solution.py:405
  (3 shorter events, 0.1 us)
Async XLA Ops:
  0.6 5.2 %copy-start.1 = (bf16[2,128,1024]{2,1,0:T(8,128)(2,1)S(1)}, bf16[2,128,1024]{2,1,0:T(8,128)(2,1)}, u32[]{:S(2)}) copy-start(bf16[2,128,1024]{2,1,0:T(8,128)(2,1)} %refs_3_.1) | copy-start | bytes 1572868
  0.6 5.7 %copy-start = (bf16[2,4,256,256]{3,2,1,0:T(8,128)(2,1)S(1)}, bf16[2,4,256,256]{3,2,1,0:T(8,128)(2,1)}, u32[]{:S(2)}) copy-start(bf16[2,4,256,256]{3,2,1,0:T(8,128)(2,1)} %kv_hbm.1) | copy-start | bytes 3145732
  0.7 5.7 %copy-start.3 = (bf16[4,4,2048]{2,1,0:T(4,128)(2,1)S(1)}, bf16[4,4,2048]{2,1,0:T(4,128)(2,1)}, u32[]{:S(2)}) copy-start(bf16[4,4,2048]{2,1,0:T(4,128)(2,1)} %q_hbm.1) | copy-start | bytes 196612
  0.7 5.7 %copy-start.4 = (bf16[2,256,32]{1,2,0:T(8,128)(2,1)S(1)}, bf16[2,256,32]{1,2,0:T(8,128)(2,1)}, u32[]{:S(2)}) copy-start(bf16[2,256,32]{1,2,0:T(8,128)(2,1)} %param.13) | copy-start | bytes 98308
  0.7 5.7 %copy-start.5 = (s32[4]{0:T(128)S(1)}, s32[4]{0:T(128)}, u32[]{:S(2)}) copy-start(s32[4]{0:T(128)} %len_ref.1) | copy-start | bytes 52
  0.7 16.2 %copy-start.2 = (bf16[4,4,4096]{2,1,0:T(4,128)(2,1)S(1)}, bf16[4,4,4096]{2,1,0:T(4,128)(2,1)}, u32[]{:S(2)}) copy-start(bf16[4,4,4096]{2,1,0:T(4,128)(2,1)} %refs_0_.1) | copy-start | bytes 393220
  0.7 5.6 %collective-permute-start.2 = (bf16[2,32,256]{2,1,0:T(8,128)(2,1)}, bf16[2,32,256]{2,1,0:T(8,128)(2,1)S(1)}, u32[]{:S(2)}, u32[]{:S(2)}) collective-permute-start(bf16[2,32,256]{2,1,0:T(8,128)(2,1)} %bitcast.1), channel_id=1, source_target_pairs={{0,4},{4,0},{8,12},{12,8},{1,5},{5,1},{9,13},{13,9},{2,6},{6,2},{1... | collective-permute-start | bytes 98312 | tf_op jit(solution)/shard_map/ppermute | solution.py:251
  3.8 9.0 %collective-permute-start.1 = (bf16[4,4,4096]{2,1,0:T(4,128)(2,1)}, bf16[4,4,4096]{2,1,0:T(4,128)(2,1)S(1)}, u32[]{:S(2)}, u32[]{:S(2)}) collective-permute-start(bf16[4,4,4096]{2,1,0:T(4,128)(2,1)} %refs_0_.1), channel_id=1, source_target_pairs={{0,2},{2,10},{4,6},{6,14},{8,0},{10,8},{12,4},{14,12},{1,3},{3,11}... | collective-permute-start | bytes 393224 | tf_op jit(solution)/shard_map/ppermute | solution.py:261
  5.3 11.6 %collective-permute-start.4 = (bf16[2,128,1024]{2,1,0:T(8,128)(2,1)}, bf16[2,128,1024]{2,1,0:T(8,128)(2,1)S(1)}, u32[]{:S(2)}, u32[]{:S(2)}) collective-permute-start(bf16[2,128,1024]{2,1,0:T(8,128)(2,1)} %refs_3_.1), channel_id=1, source_target_pairs={{0,1},{1,0},{2,3},{3,2},{4,5},{5,4},{6,7},{7,6},{8,9},{9,8},{10,11... | collective-permute-start | bytes 1572872 | tf_op jit(solution)/shard_map/ppermute | solution.py:254
  5.9 18.0 %collective-permute-start = (bf16[2,128,1024]{2,1,0:T(8,128)(2,1)S(1)}, bf16[2,128,1024]{2,1,0:T(8,128)(2,1)S(1)}, u32[]{:S(2)}, u32[]{:S(2)}) collective-permute-start(bf16[2,128,1024]{2,1,0:T(8,128)(2,1)S(1)} %copy-done.1), channel_id=1, source_target_pairs={{0,4},{4,0},{8,12},{12,8},{1,5},{5,1},{9,13},{13,9},{2,6},{6,2},{1... | collective-permute-start | bytes 1572872 | tf_op jit(solution)/shard_map/ppermute | solution.py:251
  6.4 0.7 %copy-start.6 = (f32[8,128]{1,0:T(8,128)S(1)}, f32[8,128]{1,0:T(8,128)}, u32[]{:S(2)}) copy-start(f32[8,128]{1,0:T(8,128)} %tick.1.tick_ref) | copy-start | bytes 12292
  12.8 4.1 %collective-permute-start.3 = (bf16[4,4,4096]{2,1,0:T(4,128)(2,1)S(1)}, bf16[4,4,4096]{2,1,0:T(4,128)(2,1)S(1)}, u32[]{:S(2)}, u32[]{:S(2)}) collective-permute-start(bf16[4,4,4096]{2,1,0:T(4,128)(2,1)S(1)} %collective-permute-done.1.refs_1_), channel_id=1, source_target_pairs={{0,2},{4,6},{10,8},{14,12},{1,3},{5,7},{11,9},{15,13},{16,18},{20,... | collective-permute-start | bytes 393224 | tf_op jit(solution)/shard_map/ppermute | solution.py:324
  14.1 6.2 %collective-permute-start.5 = (bf16[2,64,256]{2,1,0:T(8,128)(2,1)S(1)}, bf16[2,64,256]{2,1,0:T(8,128)(2,1)S(1)}, u32[]{:S(2)}, u32[]{:S(2)}) collective-permute-start(bf16[2,64,256]{2,1,0:T(8,128)(2,1)S(1)} %get-tuple-element.36.refs_0_), channel_id=1, source_target_pairs={{0,8},{4,12},{8,0},{12,4},{1,9},{5,13},{9,1},{13,5},{2,10},{6,14},... | collective-permute-start | bytes 196616 | tf_op jit(solution)/shard_map/ppermute | solution.py:251
  23.9 1.9 %collective-permute-start.6 = (bf16[2,128,1024]{2,1,0:T(8,128)(2,1)S(1)}, bf16[2,128,1024]{2,1,0:T(8,128)(2,1)S(1)}, u32[]{:S(2)}, u32[]{:S(2)}) collective-permute-start(bf16[2,128,1024]{2,1,0:T(8,128)(2,1)S(1)} %collective-permute-done.refs_0_), channel_id=1, source_target_pairs={{0,1},{1,0},{2,3},{3,2},{4,5},{5,4},{6,7},{7,6},{8,9},{9,8},{10,11... | collective-permute-start | bytes 1572872 | tf_op jit(solution)/shard_map/ppermute | solution.py:254
  26.2 5.5 %collective-permute-start.8 = (bf16[2,128,256]{2,1,0:T(8,128)(2,1)S(1)}, bf16[2,128,256]{2,1,0:T(8,128)(2,1)S(1)}, u32[]{:S(2)}, u32[]{:S(2)}) collective-permute-start(bf16[2,128,256]{2,1,0:T(8,128)(2,1)S(1)} %collect.1.refs_0_), channel_id=1, source_target_pairs={{0,1},{1,0},{2,3},{3,2},{4,5},{5,4},{6,7},{7,6},{8,9},{9,8},{10,11... | collective-permute-start | bytes 393224 | tf_op jit(solution)/shard_map/ppermute | solution.py:254
  26.4 4.7 %collective-permute-start.7 = (bf16[16,768]{1,0:T(8,128)(2,1)S(1)}, bf16[16,768]{1,0:T(8,128)(2,1)S(1)}, u32[]{:S(2)}, u32[]{:S(2)}) collective-permute-start(bf16[16,768]{1,0:T(8,128)(2,1)S(1)} %get-tuple-element.35), channel_id=1, source_target_pairs={{0,8},{4,12},{8,0},{12,4},{1,9},{5,13},{9,1},{13,5},{2,10},{6,14},... | collective-permute-start | bytes 73736 | tf_op jit(solution)/shard_map/ppermute | solution.py:361
  31.2 3.7 %collective-permute-start.9 = (bf16[16,256]{1,0:T(8,128)(2,1)S(1)}, bf16[16,256]{1,0:T(8,128)(2,1)S(1)}, u32[]{:S(2)}, u32[]{:S(2)}) collective-permute-start(bf16[16,256]{1,0:T(8,128)(2,1)S(1)} %ranks.1.refs_1_), channel_id=1, source_target_pairs={{0,2},{2,0},{1,3},{3,1},{4,6},{6,4},{5,7},{7,5},{8,10},{10,8},{9,1... | collective-permute-start | bytes 24584 | tf_op jit(solution)/shard_map/ppermute | solution.py:395

commit v6 on v5

--- a/solution.py
+++ b/solution.py
@@ -377,6 +377,7 @@
             in_specs=[vmem()] * sub,
             out_specs=vmem(),
             compiler_params=params(),
+        cost_estimate=cost(1.0),
             name="order",
         )(*up)
     else:
@@ -388,6 +389,7 @@
         in_specs=[vmem()] * tp,
         out_specs=vmem(),
         compiler_params=params(),
+        cost_estimate=cost(4.0),
         name="ranks",
     )(parts[0], *others)
     rank_parts = [own]

time: 36.4 us -> 36.2 us (level)
  no operation moved by 1% of the time
where the time goes in v6:
time: 36.2 us; the launch traced here: 36 us
  waiting for transfers between devices  19.8 us (55%)
  Pallas kernels  7.7 us (21%)
  starting transfers between devices  6.97 us (19%)
  between operations  0.78 us (2%)
  local copies, waits for them, and re-layouts  0.71 us (2%)
    ppermute x1, waiting for transfers between devices, local(): others.append(lax.ppermute(parts[j], 'fsdp', pairs))  4.49 us
    ppermute x1, waiting for transfers between devices, spread(): return lax.ppermute(x, ('fsdp', 'tp'), pairs)  3.98 us
    ppermute x3, starting transfers between devices, over_fsdp(): return lax.ppermute(x, 'fsdp', [(i, i ^ k) for i in range(fsdp)])  3.61 us
    ppermute x3, waiting for transfers between devices, over_fsdp(): return lax.ppermute(x, 'fsdp', [(i, i ^ k) for i in range(fsdp)])  3.61 us
    pallas_call x1, Pallas kernels, local(): pl.pallas_call(functools.partial(early_kernel, tp, wide // 4, sizes, [(k,...  3.43 us
    ppermute x1, waiting for transfers between devices, local(): lax.ppermute(own, 'tp', [(j, (j + i) % tp) for j in range(tp)])  3.14 us
    ppermute x1, waiting for transfers between devices, local(): xs = [inputs, xs[0], lax.ppermute(xs[0], ('fsdp', 'tp'), pairs)]  2.7 us
    ppermute x3, waiting for transfers between devices, over_sub(): return lax.ppermute(x, 'sub', [(i, i ^ k) for i in range(sub)])  1.91 us
  transfers between devices with their start and end apart: 10, of which 6 were waited for; matrix products, arithmetic and copies ran while one was open for 0% of the time, Pallas kernels for 16%

profile of v6, /device:TPU:0, one launch (start us, length us, event | category | flops | bytes accessed | tf_op | source)
XLA Modules:
  0.0 36.0 jit_solution(5650501537358264249)
XLA Ops:
  0.6 0.0 copy-start.1
  0.6 0.0 copy-start
  0.7 0.0 copy-start.3
  0.7 0.0 copy-start.4
  0.7 0.0 copy-start.5
  0.7 0.0 copy-start.2
  0.7 3.1 %collective-permute-start.2 = (bf16[2,32,256]{2,1,0:T(8,128)(2,1)}, bf16[2,32,256]{2,1,0:T(8,128)(2,1)S(1)}, u32[]{:S(2)}, u32[]{:S(2)}) collective-permute-start(bf16[2,32,256]{2,1,0:T(8,128)(2,1)} %bitcast.1), channel_id=1, source_target_pairs={{0,4},{4,0},{8,12},{12,8},{1,5},{5,1},{9,13},{13,9},{2,6},{6,2},{1... | collective-permute-start | bytes 98312 | tf_op jit(solution)/shard_map/ppermute | solution.py:251
  3.8 1.5 %collective-permute-start.1 = (bf16[4,4,4096]{2,1,0:T(4,128)(2,1)}, bf16[4,4,4096]{2,1,0:T(4,128)(2,1)S(1)}, u32[]{:S(2)}, u32[]{:S(2)}) collective-permute-start(bf16[4,4,4096]{2,1,0:T(4,128)(2,1)} %refs_0_.1), channel_id=1, source_target_pairs={{0,2},{2,10},{4,6},{6,14},{8,0},{10,8},{12,4},{14,12},{1,3},{3,11}... | collective-permute-start | bytes 393224 | tf_op jit(solution)/shard_map/ppermute | solution.py:261
  5.3 0.0 collective-permute-start.4
  5.3 0.6 %tick.1.tick_ref = f32[8,128]{1,0:T(8,128)} custom-call(), custom_call_target="tpu_custom_call" | custom-call | flops 8000000000 | bytes 24000000 | tf_op jit(solution)/shard_map/tick/pallas_call | solution.py:265
  5.9 0.0 copy-done.1
  5.9 0.4 %collective-permute-start = (bf16[2,128,1024]{2,1,0:T(8,128)(2,1)S(1)}, bf16[2,128,1024]{2,1,0:T(8,128)(2,1)S(1)}, u32[]{:S(2)}, u32[]{:S(2)}) collective-permute-start(bf16[2,128,1024]{2,1,0:T(8,128)(2,1)S(1)} %copy-done.1), channel_id=1, source_target_pairs={{0,4},{4,0},{8,12},{12,8},{1,5},{5,1},{9,13},{13,9},{2,6},{6,2},{1... | collective-permute-start | bytes 1572872 | tf_op jit(solution)/shard_map/ppermute | solution.py:251
  6.3 0.0 collective-permute-done.2.refs_1_
  6.3 0.0 copy-done
  6.3 0.0 copy-done.3
  6.3 0.0 copy-done.4
  6.3 0.0 copy-done.5
  6.4 0.0 copy-start.6
  6.4 0.7 %copy-done.6 = f32[8,128]{1,0:T(8,128)S(1)} copy-done((f32[8,128]{1,0:T(8,128)S(1)}, f32[8,128]{1,0:T(8,128)}, u32[]{:S(2)}) %copy-start.6) | copy-done | bytes 4120
  7.0 1.7 %cached.1 = (bf16[2,128,128]{2,1,0:T(8,128)(2,1)S(1)}, f32[2,128,128]{2,1,0:T(8,128)S(1)}, f32[2,128,128]{2,1,0:T(8,128)S(1)}, f32[2,128,128]{2,1,0:T(8,128)S(1)}, bf16[2,64,256]{2,1,0:T(8,128)(2,1)S(1)}) custom-call(s32[4]{0:T(128)S(1)} %copy-done.5, f32[8,128]{1,0:T(8,128)S(1)} %copy-done.6, bf16[4,4,2048]{2,1,0:T(4,128)(2,1)S(1)} %copy-done.3, ...), custom_call_target="tpu_custom_call" | custom-call | flops 2000000000 | bytes 6000000 | tf_op jit(solution)/shard_map/cached/pallas_call | solution.py:300
  8.8 4.0 %collective-permute-done.1.refs_1_ = bf16[4,4,4096]{2,1,0:T(4,128)(2,1)S(1)} collective-permute-done((bf16[4,4,4096]{2,1,0:T(4,128)(2,1)}, bf16[4,4,4096]{2,1,0:T(4,128)(2,1)S(1)}, u32[]{:S(2)}, u32[]{:S(2)}) %collective-permute-start.1) | collective-permute-done | bytes 131104 | tf_op jit(solution)/shard_map/ppermute | solution.py:261
  12.8 1.3 %collective-permute-start.3 = (bf16[4,4,4096]{2,1,0:T(4,128)(2,1)S(1)}, bf16[4,4,4096]{2,1,0:T(4,128)(2,1)S(1)}, u32[]{:S(2)}, u32[]{:S(2)}) collective-permute-start(bf16[4,4,4096]{2,1,0:T(4,128)(2,1)S(1)} %collective-permute-done.1.refs_1_), channel_id=1, source_target_pairs={{0,2},{4,6},{10,8},{14,12},{1,3},{5,7},{11,9},{15,13},{16,18},{20,... | collective-permute-start | bytes 393224 | tf_op jit(solution)/shard_map/ppermute | solution.py:324
  14.1 0.1 collective-permute-start.5
  14.1 2.7 %collective-permute-done.3.refs_2_ = bf16[4,4,4096]{2,1,0:T(4,128)(2,1)S(1)} collective-permute-done((bf16[4,4,4096]{2,1,0:T(4,128)(2,1)S(1)}, bf16[4,4,4096]{2,1,0:T(4,128)(2,1)S(1)}, u32[]{:S(2)}, u32[]{:S(2)}) %collective-permute-start.3) | collective-permute-done | bytes 131104 | tf_op jit(solution)/shard_map/ppermute | solution.py:324
  16.8 0.0 collective-permute-done.4.refs_4_
  16.8 0.0 copy-done.2
  16.8 3.4 %early.1 = (f32[32,768]{1,0:T(8,128)S(1)}, bf16[32,4096]{1,0:T(8,128)(2,1)S(1)}) custom-call(bf16[2,8192,256]{2,1,0:T(8,128)(2,1)} %base_hbm.1, bf16[4,4,4096]{2,1,0:T(4,128)(2,1)S(1)} %copy-done.2, bf16[4,4,4096]{2,1,0:T(4,128)(2,1)S(1)} %collective-permute-done.1.refs_1_, bf16[4,4,4096]{2,1,0:T(4,128)(2,1)S(1)} %collective-permute-done.3.refs_2_, ...), custom_call_target="tpu_custom_call" | custom-call | flops 3000000000 | bytes 9000000 | tf_op jit(solution)/shard_map/early/pallas_call | solution.py:331
  20.3 0.0 collective-permute-done.5.refs_1_
  20.3 3.6 %collective-permute-done.refs_0_ = bf16[2,128,1024]{2,1,0:T(8,128)(2,1)S(1)} collective-permute-done((bf16[2,128,1024]{2,1,0:T(8,128)(2,1)S(1)}, bf16[2,128,1024]{2,1,0:T(8,128)(2,1)S(1)}, u32[]{:S(2)}, u32[]{:S(2)}) %collective-permute-start) | collective-permute-done | bytes 524320 | tf_op jit(solution)/shard_map/ppermute | solution.py:251
  23.9 0.0 collective-permute-start.6
  23.9 1.9 %collective-permute-done.6.refs_1_ = bf16[2,128,1024]{2,1,0:T(8,128)(2,1)S(1)} collective-permute-done((bf16[2,128,1024]{2,1,0:T(8,128)(2,1)S(1)}, bf16[2,128,1024]{2,1,0:T(8,128)(2,1)S(1)}, u32[]{:S(2)}, u32[]{:S(2)}) %collective-permute-start.6) | collective-permute-done | bytes 524320 | tf_op jit(solution)/shard_map/ppermute | solution.py:254
  25.8 0.4 %late.1 = (f32[16,768]{1,0:T(8,128)S(1)}, bf16[16,768]{1,0:T(8,128)(2,1)S(1)}) custom-call(f32[32,768]{1,0:T(8,128)S(1)} %get-tuple-element.27.part_ref, bf16[32,4096]{1,0:T(8,128)(2,1)S(1)} %get-tuple-element.28.x_ref, bf16[2,128,1024]{2,1,0:T(8,128)(2,1)S(1)} %collective-permute-done.refs_0_, bf16[2,128,1024]{2,1,0:T(8,128)(2,1)S(1)} %collective-permute-done.6.refs_1_), custom_call_target="tpu_custom_call" | custom-call | tf_op jit(solution)/shard_map/late/pallas_call | solution.py:348
  26.2 0.1 collective-permute-start.7
  26.3 0.2 collective-permute-start.8
  26.5 4.5 %collective-permute-done.7.refs_0_ = bf16[16,768]{1,0:T(8,128)(2,1)S(1)} collective-permute-done((bf16[16,768]{1,0:T(8,128)(2,1)S(1)}, bf16[16,768]{1,0:T(8,128)(2,1)S(1)}, u32[]{:S(2)}, u32[]{:S(2)}) %collective-permute-start.7) | collective-permute-done | bytes 24608 | tf_op jit(solution)/shard_map/ppermute | solution.py:361
  31.0 0.3 collective-permute-start.9
  31.3 0.0 collective-permute-done.8.refs_1_
  31.3 0.1 first.1.sum_in
  31.5 3.1 %collective-permute-done.9.refs_0_ = bf16[16,256]{1,0:T(8,128)(2,1)S(1)} collective-permute-done((bf16[16,256]{1,0:T(8,128)(2,1)S(1)}, bf16[16,256]{1,0:T(8,128)(2,1)S(1)}, u32[]{:S(2)}, u32[]{:S(2)}) %collective-permute-start.9) | collective-permute-done | bytes 8224 | tf_op jit(solution)/shard_map/ppermute | solution.py:397
  34.6 1.4 %final.1 = (bf16[2,4,4,256]{3,2,1,0:T(4,128)(2,1)}, bf16[4,4,2048]{2,1,0:T(4,128)(2,1)}) custom-call(f32[16,512]{1,0:T(8,128)S(1)} %first.1.sum_in, bf16[16,256]{1,0:T(8,128)(2,1)S(1)} %collective-permute-done.9.refs_0_, bf16[2,256,256]{2,1,0:T(8,128)(2,1)S(1)} %order.1.refs_2_.refs_1_, bf16[2,128,128]{2,1,0:T(8,128)(2,1)S(1)} %get-tuple-element.38.refs_2_, ...), custom_call_target="tpu_custom_call" | custom-call | tf_op jit(solution)/shard_map/final/pallas_call | solution.py:407
  (3 shorter events, 0.0 us)
Async XLA Ops:
  0.6 5.2 %copy-start.1 = (bf16[2,128,1024]{2,1,0:T(8,128)(2,1)S(1)}, bf16[2,128,1024]{2,1,0:T(8,128)(2,1)}, u32[]{:S(2)}) copy-start(bf16[2,128,1024]{2,1,0:T(8,128)(2,1)} %refs_3_.1) | copy-start | bytes 1572868
  0.6 5.7 %copy-start = (bf16[2,4,256,256]{3,2,1,0:T(8,128)(2,1)S(1)}, bf16[2,4,256,256]{3,2,1,0:T(8,128)(2,1)}, u32[]{:S(2)}) copy-start(bf16[2,4,256,256]{3,2,1,0:T(8,128)(2,1)} %kv_hbm.1) | copy-start | bytes 3145732
  0.7 5.7 %copy-start.3 = (bf16[4,4,2048]{2,1,0:T(4,128)(2,1)S(1)}, bf16[4,4,2048]{2,1,0:T(4,128)(2,1)}, u32[]{:S(2)}) copy-start(bf16[4,4,2048]{2,1,0:T(4,128)(2,1)} %q_hbm.1) | copy-start | bytes 196612
  0.7 5.7 %copy-start.4 = (bf16[2,256,32]{1,2,0:T(8,128)(2,1)S(1)}, bf16[2,256,32]{1,2,0:T(8,128)(2,1)}, u32[]{:S(2)}) copy-start(bf16[2,256,32]{1,2,0:T(8,128)(2,1)} %param.13) | copy-start | bytes 98308
  0.7 5.7 %copy-start.5 = (s32[4]{0:T(128)S(1)}, s32[4]{0:T(128)}, u32[]{:S(2)}) copy-start(s32[4]{0:T(128)} %len_ref.1) | copy-start | bytes 52
  0.7 16.2 %copy-start.2 = (bf16[4,4,4096]{2,1,0:T(4,128)(2,1)S(1)}, bf16[4,4,4096]{2,1,0:T(4,128)(2,1)}, u32[]{:S(2)}) copy-start(bf16[4,4,4096]{2,1,0:T(4,128)(2,1)} %refs_0_.1) | copy-start | bytes 393220
  0.7 5.6 %collective-permute-start.2 = (bf16[2,32,256]{2,1,0:T(8,128)(2,1)}, bf16[2,32,256]{2,1,0:T(8,128)(2,1)S(1)}, u32[]{:S(2)}, u32[]{:S(2)}) collective-permute-start(bf16[2,32,256]{2,1,0:T(8,128)(2,1)} %bitcast.1), channel_id=1, source_target_pairs={{0,4},{4,0},{8,12},{12,8},{1,5},{5,1},{9,13},{13,9},{2,6},{6,2},{1... | collective-permute-start | bytes 98312 | tf_op jit(solution)/shard_map/ppermute | solution.py:251
  3.8 9.0 %collective-permute-start.1 = (bf16[4,4,4096]{2,1,0:T(4,128)(2,1)}, bf16[4,4,4096]{2,1,0:T(4,128)(2,1)S(1)}, u32[]{:S(2)}, u32[]{:S(2)}) collective-permute-start(bf16[4,4,4096]{2,1,0:T(4,128)(2,1)} %refs_0_.1), channel_id=1, source_target_pairs={{0,2},{2,10},{4,6},{6,14},{8,0},{10,8},{12,4},{14,12},{1,3},{3,11}... | collective-permute-start | bytes 393224 | tf_op jit(solution)/shard_map/ppermute | solution.py:261
  5.3 11.6 %collective-permute-start.4 = (bf16[2,128,1024]{2,1,0:T(8,128)(2,1)}, bf16[2,128,1024]{2,1,0:T(8,128)(2,1)S(1)}, u32[]{:S(2)}, u32[]{:S(2)}) collective-permute-start(bf16[2,128,1024]{2,1,0:T(8,128)(2,1)} %refs_3_.1), channel_id=1, source_target_pairs={{0,1},{1,0},{2,3},{3,2},{4,5},{5,4},{6,7},{7,6},{8,9},{9,8},{10,11... | collective-permute-start | bytes 1572872 | tf_op jit(solution)/shard_map/ppermute | solution.py:254
  5.9 18.0 %collective-permute-start = (bf16[2,128,1024]{2,1,0:T(8,128)(2,1)S(1)}, bf16[2,128,1024]{2,1,0:T(8,128)(2,1)S(1)}, u32[]{:S(2)}, u32[]{:S(2)}) collective-permute-start(bf16[2,128,1024]{2,1,0:T(8,128)(2,1)S(1)} %copy-done.1), channel_id=1, source_target_pairs={{0,4},{4,0},{8,12},{12,8},{1,5},{5,1},{9,13},{13,9},{2,6},{6,2},{1... | collective-permute-start | bytes 1572872 | tf_op jit(solution)/shard_map/ppermute | solution.py:251
  6.4 0.7 %copy-start.6 = (f32[8,128]{1,0:T(8,128)S(1)}, f32[8,128]{1,0:T(8,128)}, u32[]{:S(2)}) copy-start(f32[8,128]{1,0:T(8,128)} %tick.1.tick_ref) | copy-start | bytes 12292
  12.8 4.1 %collective-permute-start.3 = (bf16[4,4,4096]{2,1,0:T(4,128)(2,1)S(1)}, bf16[4,4,4096]{2,1,0:T(4,128)(2,1)S(1)}, u32[]{:S(2)}, u32[]{:S(2)}) collective-permute-start(bf16[4,4,4096]{2,1,0:T(4,128)(2,1)S(1)} %collective-permute-done.1.refs_1_), channel_id=1, source_target_pairs={{0,2},{4,6},{10,8},{14,12},{1,3},{5,7},{11,9},{15,13},{16,18},{20,... | collective-permute-start | bytes 393224 | tf_op jit(solution)/shard_map/ppermute | solution.py:324
  14.1 6.2 %collective-permute-start.5 = (bf16[2,64,256]{2,1,0:T(8,128)(2,1)S(1)}, bf16[2,64,256]{2,1,0:T(8,128)(2,1)S(1)}, u32[]{:S(2)}, u32[]{:S(2)}) collective-permute-start(bf16[2,64,256]{2,1,0:T(8,128)(2,1)S(1)} %get-tuple-element.36.refs_0_), channel_id=1, source_target_pairs={{0,8},{4,12},{8,0},{12,4},{1,9},{5,13},{9,1},{13,5},{2,10},{6,14},... | collective-permute-start | bytes 196616 | tf_op jit(solution)/shard_map/ppermute | solution.py:251
  23.9 1.9 %collective-permute-start.6 = (bf16[2,128,1024]{2,1,0:T(8,128)(2,1)S(1)}, bf16[2,128,1024]{2,1,0:T(8,128)(2,1)S(1)}, u32[]{:S(2)}, u32[]{:S(2)}) collective-permute-start(bf16[2,128,1024]{2,1,0:T(8,128)(2,1)S(1)} %collective-permute-done.refs_0_), channel_id=1, source_target_pairs={{0,1},{1,0},{2,3},{3,2},{4,5},{5,4},{6,7},{7,6},{8,9},{9,8},{10,11... | collective-permute-start | bytes 1572872 | tf_op jit(solution)/shard_map/ppermute | solution.py:254
  26.2 4.8 %collective-permute-start.7 = (bf16[16,768]{1,0:T(8,128)(2,1)S(1)}, bf16[16,768]{1,0:T(8,128)(2,1)S(1)}, u32[]{:S(2)}, u32[]{:S(2)}) collective-permute-start(bf16[16,768]{1,0:T(8,128)(2,1)S(1)} %get-tuple-element.35), channel_id=1, source_target_pairs={{0,8},{4,12},{8,0},{12,4},{1,9},{5,13},{9,1},{13,5},{2,10},{6,14},... | collective-permute-start | bytes 73736 | tf_op jit(solution)/shard_map/ppermute | solution.py:361
  26.3 5.0 %collective-permute-start.8 = (bf16[2,128,256]{2,1,0:T(8,128)(2,1)S(1)}, bf16[2,128,256]{2,1,0:T(8,128)(2,1)S(1)}, u32[]{:S(2)}, u32[]{:S(2)}) collective-permute-start(bf16[2,128,256]{2,1,0:T(8,128)(2,1)S(1)} %collect.1.refs_0_), channel_id=1, source_target_pairs={{0,1},{1,0},{2,3},{3,2},{4,5},{5,4},{6,7},{7,6},{8,9},{9,8},{10,11... | collective-permute-start | bytes 393224 | tf_op jit(solution)/shard_map/ppermute | solution.py:254
  31.0 3.7 %collective-permute-start.9 = (bf16[16,256]{1,0:T(8,128)(2,1)S(1)}, bf16[16,256]{1,0:T(8,128)(2,1)S(1)}, u32[]{:S(2)}, u32[]{:S(2)}) collective-permute-start(bf16[16,256]{1,0:T(8,128)(2,1)S(1)} %ranks.1.refs_1_), channel_id=1, source_target_pairs={{0,2},{2,0},{1,3},{3,1},{4,6},{6,4},{5,7},{7,5},{8,10},{10,8},{9,1... | collective-permute-start | bytes 24584 | tf_op jit(solution)/shard_map/ppermute | solution.py:397

commit v7 on v6

--- a/solution.py
+++ b/solution.py
@@ -97,7 +97,8 @@
     x_refs, refs = refs[:blocks], refs[blocks:]
     if blocks == 2:
         x_refs, refs = x_refs + refs[:1], refs[1:]
-    a_refs, (out_ref, x_out, base_ref, sems) = refs[:-4], refs[-4:]
+    a_refs, refs = refs[: len(items)], refs[len(items) :]
+    out_ref, x_out, *send_outs, base_ref, sems = refs
     columns, slab, ranks = base_hbm.shape[2], a_refs[0].shape[2], a_refs[0].shape[1]
     rows, steps, wide = x_refs[0].shape
     block = lax.div(lax.axis_index("fsdp"), sizes[0] // sizes[1])
@@ -131,6 +132,8 @@
         start = pl.multiple_of(place[i] * slab, slab)
         total = total + dot(x_out[:, pl.ds(start, slab)], a[...].reshape(2 * ranks, slab), NT)
     out_ref[:, 2 * columns :] = total
+    for place_to, send in zip(places(sizes, [(k + 1, 1) for k in range(len(send_outs))]), send_outs):
+        send[...] = x_out[:, pl.ds(pl.multiple_of(place_to * slab, slab), slab)]
     totals = [jnp.zeros((count, columns), jnp.float32) for _ in range(2)]
     for i in range(wide // chunk):
         at = slice(i * chunk, (i + 1) * chunk)
@@ -141,15 +144,25 @@
         out_ref[:, m * columns : (m + 1) * columns] = totals[m]
 
 
-def late_kernel(blocks, columns, sizes, items, part_ref, x_ref, *refs):
-    a_refs, outs = refs[:-blocks], refs[-blocks:]
+def far_kernel(sizes, count, part_ref, x_ref, *refs):
+    other_refs, a_refs, (own_out, other_out) = refs[:count], refs[count:-2], refs[-2:]
+    slab, ranks = a_refs[0].shape[2], a_refs[0].shape[1]
+    columns = part_ref.shape[1] - 2 * ranks
+    place = places(sizes, [(k + 1, 0) for k in range(count)])
+    own = part_ref[:, columns:]
+    other = jnp.zeros(own.shape, jnp.float32)
+    for k, a in enumerate(a_refs):
+        factor = a[...].reshape(2 * ranks, slab)
+        start = pl.multiple_of(place[k] * slab, slab)
+        own = own + dot(x_ref[:, pl.ds(start, slab)], factor, NT)
+        other = other + dot(other_refs[k][...], factor, NT)
+    own_out[...] = own
+    other_out[...] = other.astype(jnp.bfloat16)
+
+
+def late_kernel(columns, part_ref, own_ref, other_ref, *outs):
     tokens = outs[0].shape[0]
-    slab, ranks = a_refs[0].shape[2], a_refs[0].shape[1]
-    place = places(sizes, items)
-    total = part_ref[:, 2 * columns :]
-    for i, a in enumerate(a_refs):
-        start = pl.multiple_of(place[i] * slab, slab)
-        total = total + dot(x_ref[:, pl.ds(start, slab)], a[...].reshape(2 * ranks, slab), NT)
+    total = own_ref[...] + other_ref[...].astype(jnp.float32)
     for j, out in enumerate(outs):
         at = slice(j * tokens, (j + 1) * tokens)
         out[:, : 2 * columns] = part_ref[at, : 2 * columns].astype(out.dtype)
@@ -328,31 +341,42 @@
     near = [(0, 0, a_factor)] + near
     up = [up, over_fsdp(up, inner)] if direct else [up]
     width = 2 * columns + 2 * ranks
-    part, x = pl.pallas_call(
+    part, x, *x_sends = pl.pallas_call(
         functools.partial(early_kernel, tp, wide // 4, sizes, [(k, e) for k, e, _ in near]),
         out_shape=[
             jax.ShapeDtypeStruct((tp * tokens, width), f32),
             jax.ShapeDtypeStruct((tp * tokens, wide), bf16),
-        ],
+        ]
+        + [jax.ShapeDtypeStruct((tp * tokens, a_factor.shape[2]), bf16)] * (inner - 1),
         in_specs=[pl.BlockSpec(memory_space=pltpu.HBM)] + [vmem()] * (len(xs) + len(near)),
-        out_specs=[vmem()] * 2,
+        out_specs=[vmem()] * (1 + inner),
         scratch_shapes=[pltpu.VMEM((2, wide, columns), bf16), pltpu.SemaphoreType.DMA((8,))],
         compiler_params=params(50),
         cost_estimate=cost(C_EARLY),
         name="early",
     )(base, *xs, *[a for _, _, a in near])
 
-    far, part, up = lax.optimization_barrier((far, part, up))
-    late_at = [(k, e) for k in range(1, inner) for e in range(sub)]
-    late = [over_sub(far[k - 1], e) if e else far[k - 1] for k, e in late_at]
+    x_others = [over_sub(x, 1) for x in x_sends]
+    far, part, up, x_others = lax.optimization_barrier((far, part, up, x_others))
+    far_own, far_other = pl.pallas_call(
+        functools.partial(far_kernel, sizes, inner - 1),
+        out_shape=[
+            jax.ShapeDtypeStruct((tp * tokens, 2 * ranks), f32),
+            jax.ShapeDtypeStruct((tp * tokens, 2 * ranks), bf16),
+        ],
+        in_specs=[vmem()] * (2 * inner),
+        out_specs=[vmem()] * 2,
+        compiler_params=params(),
+        name="far",
+    )(part, x, *x_others, *far)
     parts = pl.pallas_call(
-        functools.partial(late_kernel, tp, columns, sizes, late_at),
+        functools.partial(late_kernel, columns),
         out_shape=[jax.ShapeDtypeStruct((tokens, width), f32 if j == 0 else bf16) for j in range(tp)],
-        in_specs=[vmem()] * (2 + len(late)),
+        in_specs=[vmem()] * 3,
         out_specs=[vmem()] * tp,
         compiler_params=params(),
         name="late",
-    )(part, x, *late)
+    )(part, far_own, over_sub(far_other, 1))
 
     parts, up = lax.optimization_barrier((parts, up))
     others = []

time: 36.2 us -> 35.5 us (0.981)
  waiting for transfers between devices: 19.8 us -> 18.8 us
    ppermute x3 -> x4, waiting for transfers between devices: 1.91 us -> 1.19 us  [over_sub(): return lax.ppermute(x, 'sub', [(i, i ^ k) for i in range(sub)])]
  transfers between devices with their start and end apart: 10 -> 11, of which waited for: 6 -> 6; matrix products, arithmetic and copies ran while one was open for 0% -> 0% of each run, Pallas kernels for 16% -> 17%
where the time goes in v7:
time: 35.5 us; the launch traced here: 35.3 us
  waiting for transfers between devices  18.8 us (53%)
  Pallas kernels  7.68 us (22%)
  starting transfers between devices  7.33 us (21%)
  between operations  0.79 us (2%)
  local copies, waits for them, and re-layouts  0.71 us (2%)
    ppermute x1, waiting for transfers between devices, local(): others.append(lax.ppermute(parts[j], 'fsdp', pairs))  4.46 us
    ppermute x1, waiting for transfers between devices, spread(): return lax.ppermute(x, ('fsdp', 'tp'), pairs)  3.98 us
    ppermute x3, starting transfers between devices, over_fsdp(): return lax.ppermute(x, 'fsdp', [(i, i ^ k) for i in range(fsdp)])  3.61 us
    ppermute x3, waiting for transfers between devices, over_fsdp(): return lax.ppermute(x, 'fsdp', [(i, i ^ k) for i in range(fsdp)])  3.53 us
    pallas_call x1, Pallas kernels, local(): pl.pallas_call(functools.partial(early_kernel, tp, wide // 4, sizes, [(k,...  3.43 us
    ppermute x1, waiting for transfers between devices, local(): lax.ppermute(own, 'tp', [(j, (j + i) % tp) for j in range(tp)])  2.94 us
    ppermute x1, waiting for transfers between devices, local(): xs = [inputs, xs[0], lax.ppermute(xs[0], ('fsdp', 'tp'), pairs)]  2.7 us
    pallas_call x1, Pallas kernels, local(): pl.pallas_call(functools.partial(cache_kernel, group, len(up)), out_shape...  1.73 us
  transfers between devices with their start and end apart: 11, of which 6 were waited for; matrix products, arithmetic and copies ran while one was open for 0% of the time, Pallas kernels for 17%

profile of v7, /device:TPU:0, one launch (start us, length us, event | category | flops | bytes accessed | tf_op | source)
XLA Modules:
  0.0 35.3 jit_solution(15410287112630410522)
XLA Ops:
  0.6 0.0 copy-start.1
  0.6 0.0 copy-start
  0.7 0.0 copy-start.3
  0.7 0.0 copy-start.4
  0.7 0.0 copy-start.5
  0.7 0.0 copy-start.2
  0.7 3.1 %collective-permute-start.2 = (bf16[2,32,256]{2,1,0:T(8,128)(2,1)}, bf16[2,32,256]{2,1,0:T(8,128)(2,1)S(1)}, u32[]{:S(2)}, u32[]{:S(2)}) collective-permute-start(bf16[2,32,256]{2,1,0:T(8,128)(2,1)} %bitcast.1), channel_id=1, source_target_pairs={{0,4},{4,0},{8,12},{12,8},{1,5},{5,1},{9,13},{13,9},{2,6},{6,2},{1... | collective-permute-start | bytes 98312 | tf_op jit(solution)/shard_map/ppermute | solution.py:264
  3.8 1.5 %collective-permute-start.1 = (bf16[4,4,4096]{2,1,0:T(4,128)(2,1)}, bf16[4,4,4096]{2,1,0:T(4,128)(2,1)S(1)}, u32[]{:S(2)}, u32[]{:S(2)}) collective-permute-start(bf16[4,4,4096]{2,1,0:T(4,128)(2,1)} %refs_0_.1), channel_id=1, source_target_pairs={{0,2},{2,10},{4,6},{6,14},{8,0},{10,8},{12,4},{14,12},{1,3},{3,11}... | collective-permute-start | bytes 393224 | tf_op jit(solution)/shard_map/ppermute | solution.py:274
  5.3 0.0 collective-permute-start.4
  5.3 0.6 %tick.1.tick_ref = f32[8,128]{1,0:T(8,128)} custom-call(), custom_call_target="tpu_custom_call" | custom-call | flops 8000000000 | bytes 24000000 | tf_op jit(solution)/shard_map/tick/pallas_call | solution.py:278
  5.9 0.0 copy-done.1
  5.9 0.4 %collective-permute-start = (bf16[2,128,1024]{2,1,0:T(8,128)(2,1)S(1)}, bf16[2,128,1024]{2,1,0:T(8,128)(2,1)S(1)}, u32[]{:S(2)}, u32[]{:S(2)}) collective-permute-start(bf16[2,128,1024]{2,1,0:T(8,128)(2,1)S(1)} %copy-done.1), channel_id=1, source_target_pairs={{0,4},{4,0},{8,12},{12,8},{1,5},{5,1},{9,13},{13,9},{2,6},{6,2},{1... | collective-permute-start | bytes 1572872 | tf_op jit(solution)/shard_map/ppermute | solution.py:264
  6.3 0.0 collective-permute-done.2.refs_1_
  6.3 0.0 copy-done
  6.3 0.0 copy-done.3
  6.3 0.0 copy-done.4
  6.3 0.0 copy-done.5
  6.4 0.0 copy-start.6
  6.4 0.7 %copy-done.6 = f32[8,128]{1,0:T(8,128)S(1)} copy-done((f32[8,128]{1,0:T(8,128)S(1)}, f32[8,128]{1,0:T(8,128)}, u32[]{:S(2)}) %copy-start.6) | copy-done | bytes 4120
  7.0 1.7 %cached.1 = (bf16[2,128,128]{2,1,0:T(8,128)(2,1)S(1)}, f32[2,128,128]{2,1,0:T(8,128)S(1)}, f32[2,128,128]{2,1,0:T(8,128)S(1)}, f32[2,128,128]{2,1,0:T(8,128)S(1)}, bf16[2,64,256]{2,1,0:T(8,128)(2,1)S(1)}) custom-call(s32[4]{0:T(128)S(1)} %copy-done.5, f32[8,128]{1,0:T(8,128)S(1)} %copy-done.6, bf16[4,4,2048]{2,1,0:T(4,128)(2,1)S(1)} %copy-done.3, ...), custom_call_target="tpu_custom_call" | custom-call | flops 2000000000 | bytes 6000000 | tf_op jit(solution)/shard_map/cached/pallas_call | solution.py:313
  8.8 4.0 %collective-permute-done.1.refs_1_ = bf16[4,4,4096]{2,1,0:T(4,128)(2,1)S(1)} collective-permute-done((bf16[4,4,4096]{2,1,0:T(4,128)(2,1)}, bf16[4,4,4096]{2,1,0:T(4,128)(2,1)S(1)}, u32[]{:S(2)}, u32[]{:S(2)}) %collective-permute-start.1) | collective-permute-done | bytes 131104 | tf_op jit(solution)/shard_map/ppermute | solution.py:274
  12.8 1.3 %collective-permute-start.3 = (bf16[4,4,4096]{2,1,0:T(4,128)(2,1)S(1)}, bf16[4,4,4096]{2,1,0:T(4,128)(2,1)S(1)}, u32[]{:S(2)}, u32[]{:S(2)}) collective-permute-start(bf16[4,4,4096]{2,1,0:T(4,128)(2,1)S(1)} %collective-permute-done.1.refs_1_), channel_id=1, source_target_pairs={{0,2},{4,6},{10,8},{14,12},{1,3},{5,7},{11,9},{15,13},{16,18},{20,... | collective-permute-start | bytes 393224 | tf_op jit(solution)/shard_map/ppermute | solution.py:337
  14.1 0.1 collective-permute-start.5
  14.1 2.7 %collective-permute-done.3.refs_2_ = bf16[4,4,4096]{2,1,0:T(4,128)(2,1)S(1)} collective-permute-done((bf16[4,4,4096]{2,1,0:T(4,128)(2,1)S(1)}, bf16[4,4,4096]{2,1,0:T(4,128)(2,1)S(1)}, u32[]{:S(2)}, u32[]{:S(2)}) %collective-permute-start.3) | collective-permute-done | bytes 131104 | tf_op jit(solution)/shard_map/ppermute | solution.py:337
  16.8 0.0 collective-permute-done.4.refs_4_
  16.8 0.0 copy-done.2
  16.8 3.4 %early.1 = (f32[32,768]{1,0:T(8,128)S(1)}, bf16[32,4096]{1,0:T(8,128)(2,1)S(1)}, bf16[32,1024]{1,0:T(8,128)(2,1)S(1)}) custom-call(bf16[2,8192,256]{2,1,0:T(8,128)(2,1)} %base_hbm.1, bf16[4,4,4096]{2,1,0:T(4,128)(2,1)S(1)} %copy-done.2, bf16[4,4,4096]{2,1,0:T(4,128)(2,1)S(1)} %collective-permute-done.1.refs_1_, ...), custom_call_target="tpu_custom_call" | custom-call | flops 3000000000 | bytes 9000000 | tf_op jit(solution)/shard_map/early/pallas_call | solution.py:344
  20.3 0.1 collective-permute-start.6
  20.4 0.0 collective-permute-done.5.refs_1_
  20.4 3.5 %collective-permute-done.refs_1_ = bf16[2,128,1024]{2,1,0:T(8,128)(2,1)S(1)} collective-permute-done((bf16[2,128,1024]{2,1,0:T(8,128)(2,1)S(1)}, bf16[2,128,1024]{2,1,0:T(8,128)(2,1)S(1)}, u32[]{:S(2)}, u32[]{:S(2)}) %collective-permute-start) | collective-permute-done | bytes 524320 | tf_op jit(solution)/shard_map/ppermute | solution.py:264
  23.9 0.0 collective-permute-done.6.refs_0_
  23.9 0.4 %far.1 = (f32[32,256]{1,0:T(8,128)S(1)}, bf16[32,256]{1,0:T(8,128)(2,1)S(1)}) custom-call(f32[32,768]{1,0:T(8,128)S(1)} %get-tuple-element.32.part_ref, bf16[32,4096]{1,0:T(8,128)(2,1)S(1)} %get-tuple-element.33.x_ref, bf16[32,1024]{1,0:T(8,128)(2,1)S(1)} %collective-permute-done.6.refs_0_, bf16[2,128,1024]{2,1,0:T(8,128)(2,1)S(1)} %collective-permute-done.refs_1_), custom_call_target="tpu_custom_call" | custom-call | tf_op jit(solution)/shard_map/far/pallas_call | solution.py:361
  24.3 0.0 collective-permute-start.7
  24.3 1.2 %collective-permute-done.7.other_ref = bf16[32,256]{1,0:T(8,128)(2,1)S(1)} collective-permute-done((bf16[32,256]{1,0:T(8,128)(2,1)S(1)}, bf16[32,256]{1,0:T(8,128)(2,1)S(1)}, u32[]{:S(2)}, u32[]{:S(2)}) %collective-permute-start.7) | collective-permute-done | bytes 16416 | tf_op jit(solution)/shard_map/ppermute | solution.py:267
  25.5 0.2 collective-permute-start.8
  25.8 0.1 collective-permute-start.9
  25.8 4.5 %collective-permute-done.8.refs_0_ = bf16[16,768]{1,0:T(8,128)(2,1)S(1)} collective-permute-done((bf16[16,768]{1,0:T(8,128)(2,1)S(1)}, bf16[16,768]{1,0:T(8,128)(2,1)S(1)}, u32[]{:S(2)}, u32[]{:S(2)}) %collective-permute-start.8) | collective-permute-done | bytes 24608 | tf_op jit(solution)/shard_map/ppermute | solution.py:385
  30.3 0.5 %collective-permute-start.10 = (bf16[16,256]{1,0:T(8,128)(2,1)S(1)}, bf16[16,256]{1,0:T(8,128)(2,1)S(1)}, u32[]{:S(2)}, u32[]{:S(2)}) collective-permute-start(bf16[16,256]{1,0:T(8,128)(2,1)S(1)} %ranks.1.refs_1_), channel_id=1, source_target_pairs={{0,2},{2,0},{1,3},{3,1},{4,6},{6,4},{5,7},{7,5},{8,10},{10,8},{9,1... | collective-permute-start | bytes 24584 | tf_op jit(solution)/shard_map/ppermute | solution.py:421
  30.8 0.0 collective-permute-done.9.refs_1_
  30.9 0.1 first.1.sum_in
  31.0 2.9 %collective-permute-done.10.refs_0_ = bf16[16,256]{1,0:T(8,128)(2,1)S(1)} collective-permute-done((bf16[16,256]{1,0:T(8,128)(2,1)S(1)}, bf16[16,256]{1,0:T(8,128)(2,1)S(1)}, u32[]{:S(2)}, u32[]{:S(2)}) %collective-permute-start.10) | collective-permute-done | bytes 8224 | tf_op jit(solution)/shard_map/ppermute | solution.py:421
  34.0 1.4 %final.1 = (bf16[2,4,4,256]{3,2,1,0:T(4,128)(2,1)}, bf16[4,4,2048]{2,1,0:T(4,128)(2,1)}) custom-call(f32[16,512]{1,0:T(8,128)S(1)} %first.1.sum_in, bf16[16,256]{1,0:T(8,128)(2,1)S(1)} %collective-permute-done.10.refs_0_, bf16[2,256,256]{2,1,0:T(8,128)(2,1)S(1)} %order.1.refs_2_.refs_1_, bf16[2,128,128]{2,1,0:T(8,128)(2,1)S(1)} %get-tuple-element.46.refs_2_, ...), custom_call_target="tpu_custom_call" | custom-call | tf_op jit(solution)/shard_map/final/pallas_call | solution.py:431
  (4 shorter events, 0.1 us)
Async XLA Ops:
  0.6 5.2 %copy-start.1 = (bf16[2,128,1024]{2,1,0:T(8,128)(2,1)S(1)}, bf16[2,128,1024]{2,1,0:T(8,128)(2,1)}, u32[]{:S(2)}) copy-start(bf16[2,128,1024]{2,1,0:T(8,128)(2,1)} %refs_3_.1) | copy-start | bytes 1572868
  0.6 5.7 %copy-start = (bf16[2,4,256,256]{3,2,1,0:T(8,128)(2,1)S(1)}, bf16[2,4,256,256]{3,2,1,0:T(8,128)(2,1)}, u32[]{:S(2)}) copy-start(bf16[2,4,256,256]{3,2,1,0:T(8,128)(2,1)} %kv_hbm.1) | copy-start | bytes 3145732
  0.7 5.7 %copy-start.3 = (bf16[4,4,2048]{2,1,0:T(4,128)(2,1)S(1)}, bf16[4,4,2048]{2,1,0:T(4,128)(2,1)}, u32[]{:S(2)}) copy-start(bf16[4,4,2048]{2,1,0:T(4,128)(2,1)} %q_hbm.1) | copy-start | bytes 196612
  0.7 5.7 %copy-start.4 = (bf16[2,256,32]{1,2,0:T(8,128)(2,1)S(1)}, bf16[2,256,32]{1,2,0:T(8,128)(2,1)}, u32[]{:S(2)}) copy-start(bf16[2,256,32]{1,2,0:T(8,128)(2,1)} %param.13) | copy-start | bytes 98308
  0.7 5.7 %copy-start.5 = (s32[4]{0:T(128)S(1)}, s32[4]{0:T(128)}, u32[]{:S(2)}) copy-start(s32[4]{0:T(128)} %len_ref.1) | copy-start | bytes 52
  0.7 16.2 %copy-start.2 = (bf16[4,4,4096]{2,1,0:T(4,128)(2,1)S(1)}, bf16[4,4,4096]{2,1,0:T(4,128)(2,1)}, u32[]{:S(2)}) copy-start(bf16[4,4,4096]{2,1,0:T(4,128)(2,1)} %refs_0_.1) | copy-start | bytes 393220
  0.7 5.6 %collective-permute-start.2 = (bf16[2,32,256]{2,1,0:T(8,128)(2,1)}, bf16[2,32,256]{2,1,0:T(8,128)(2,1)S(1)}, u32[]{:S(2)}, u32[]{:S(2)}) collective-permute-start(bf16[2,32,256]{2,1,0:T(8,128)(2,1)} %bitcast.1), channel_id=1, source_target_pairs={{0,4},{4,0},{8,12},{12,8},{1,5},{5,1},{9,13},{13,9},{2,6},{6,2},{1... | collective-permute-start | bytes 98312 | tf_op jit(solution)/shard_map/ppermute | solution.py:264
  3.8 9.0 %collective-permute-start.1 = (bf16[4,4,4096]{2,1,0:T(4,128)(2,1)}, bf16[4,4,4096]{2,1,0:T(4,128)(2,1)S(1)}, u32[]{:S(2)}, u32[]{:S(2)}) collective-permute-start(bf16[4,4,4096]{2,1,0:T(4,128)(2,1)} %refs_0_.1), channel_id=1, source_target_pairs={{0,2},{2,10},{4,6},{6,14},{8,0},{10,8},{12,4},{14,12},{1,3},{3,11}... | collective-permute-start | bytes 393224 | tf_op jit(solution)/shard_map/ppermute | solution.py:274
  5.3 11.6 %collective-permute-start.4 = (bf16[2,128,1024]{2,1,0:T(8,128)(2,1)}, bf16[2,128,1024]{2,1,0:T(8,128)(2,1)S(1)}, u32[]{:S(2)}, u32[]{:S(2)}) collective-permute-start(bf16[2,128,1024]{2,1,0:T(8,128)(2,1)} %refs_3_.1), channel_id=1, source_target_pairs={{0,1},{1,0},{2,3},{3,2},{4,5},{5,4},{6,7},{7,6},{8,9},{9,8},{10,11... | collective-permute-start | bytes 1572872 | tf_op jit(solution)/shard_map/ppermute | solution.py:267
  5.9 18.0 %collective-permute-start = (bf16[2,128,1024]{2,1,0:T(8,128)(2,1)S(1)}, bf16[2,128,1024]{2,1,0:T(8,128)(2,1)S(1)}, u32[]{:S(2)}, u32[]{:S(2)}) collective-permute-start(bf16[2,128,1024]{2,1,0:T(8,128)(2,1)S(1)} %copy-done.1), channel_id=1, source_target_pairs={{0,4},{4,0},{8,12},{12,8},{1,5},{5,1},{9,13},{13,9},{2,6},{6,2},{1... | collective-permute-start | bytes 1572872 | tf_op jit(solution)/shard_map/ppermute | solution.py:264
  6.4 0.7 %copy-start.6 = (f32[8,128]{1,0:T(8,128)S(1)}, f32[8,128]{1,0:T(8,128)}, u32[]{:S(2)}) copy-start(f32[8,128]{1,0:T(8,128)} %tick.1.tick_ref) | copy-start | bytes 12292
  12.8 4.1 %collective-permute-start.3 = (bf16[4,4,4096]{2,1,0:T(4,128)(2,1)S(1)}, bf16[4,4,4096]{2,1,0:T(4,128)(2,1)S(1)}, u32[]{:S(2)}, u32[]{:S(2)}) collective-permute-start(bf16[4,4,4096]{2,1,0:T(4,128)(2,1)S(1)} %collective-permute-done.1.refs_1_), channel_id=1, source_target_pairs={{0,2},{4,6},{10,8},{14,12},{1,3},{5,7},{11,9},{15,13},{16,18},{20,... | collective-permute-start | bytes 393224 | tf_op jit(solution)/shard_map/ppermute | solution.py:337
  14.1 6.3 %collective-permute-start.5 = (bf16[2,64,256]{2,1,0:T(8,128)(2,1)S(1)}, bf16[2,64,256]{2,1,0:T(8,128)(2,1)S(1)}, u32[]{:S(2)}, u32[]{:S(2)}) collective-permute-start(bf16[2,64,256]{2,1,0:T(8,128)(2,1)S(1)} %get-tuple-element.44.refs_0_), channel_id=1, source_target_pairs={{0,8},{4,12},{8,0},{12,4},{1,9},{5,13},{9,1},{13,5},{2,10},{6,14},... | collective-permute-start | bytes 196616 | tf_op jit(solution)/shard_map/ppermute | solution.py:264
  20.3 3.6 %collective-permute-start.6 = (bf16[32,1024]{1,0:T(8,128)(2,1)S(1)}, bf16[32,1024]{1,0:T(8,128)(2,1)S(1)}, u32[]{:S(2)}, u32[]{:S(2)}) collective-permute-start(bf16[32,1024]{1,0:T(8,128)(2,1)S(1)} %get-tuple-element.31), channel_id=1, source_target_pairs={{0,1},{1,0},{2,3},{3,2},{4,5},{5,4},{6,7},{7,6},{8,9},{9,8},{10,11... | collective-permute-start | bytes 196616 | tf_op jit(solution)/shard_map/ppermute | solution.py:267
  24.3 1.2 %collective-permute-start.7 = (bf16[32,256]{1,0:T(8,128)(2,1)S(1)}, bf16[32,256]{1,0:T(8,128)(2,1)S(1)}, u32[]{:S(2)}, u32[]{:S(2)}) collective-permute-start(bf16[32,256]{1,0:T(8,128)(2,1)S(1)} %get-tuple-element.37), channel_id=1, source_target_pairs={{0,1},{1,0},{2,3},{3,2},{4,5},{5,4},{6,7},{7,6},{8,9},{9,8},{10,11... | collective-permute-start | bytes 49160 | tf_op jit(solution)/shard_map/ppermute | solution.py:267
  25.5 4.8 %collective-permute-start.8 = (bf16[16,768]{1,0:T(8,128)(2,1)S(1)}, bf16[16,768]{1,0:T(8,128)(2,1)S(1)}, u32[]{:S(2)}, u32[]{:S(2)}) collective-permute-start(bf16[16,768]{1,0:T(8,128)(2,1)S(1)} %get-tuple-element.43), channel_id=1, source_target_pairs={{0,8},{4,12},{8,0},{12,4},{1,9},{5,13},{9,1},{13,5},{2,10},{6,14},... | collective-permute-start | bytes 73736 | tf_op jit(solution)/shard_map/ppermute | solution.py:385
  25.8 5.1 %collective-permute-start.9 = (bf16[2,128,256]{2,1,0:T(8,128)(2,1)S(1)}, bf16[2,128,256]{2,1,0:T(8,128)(2,1)S(1)}, u32[]{:S(2)}, u32[]{:S(2)}) collective-permute-start(bf16[2,128,256]{2,1,0:T(8,128)(2,1)S(1)} %collect.1.refs_0_), channel_id=1, source_target_pairs={{0,1},{1,0},{2,3},{3,2},{4,5},{5,4},{6,7},{7,6},{8,9},{9,8},{10,11... | collective-permute-start | bytes 393224 | tf_op jit(solution)/shard_map/ppermute | solution.py:267
  30.3 3.7 %collective-permute-start.10 = (bf16[16,256]{1,0:T(8,128)(2,1)S(1)}, bf16[16,256]{1,0:T(8,128)(2,1)S(1)}, u32[]{:S(2)}, u32[]{:S(2)}) collective-permute-start(bf16[16,256]{1,0:T(8,128)(2,1)S(1)} %ranks.1.refs_1_), channel_id=1, source_target_pairs={{0,2},{2,0},{1,3},{3,1},{4,6},{6,4},{5,7},{7,5},{8,10},{10,8},{9,1... | collective-permute-start | bytes 24584 | tf_op jit(solution)/shard_map/ppermute | solution.py:421

commit v8 on v7

--- a/solution.py
+++ b/solution.py
@@ -132,7 +132,7 @@
         start = pl.multiple_of(place[i] * slab, slab)
         total = total + dot(x_out[:, pl.ds(start, slab)], a[...].reshape(2 * ranks, slab), NT)
     out_ref[:, 2 * columns :] = total
-    for place_to, send in zip(places(sizes, [(k + 1, 1) for k in range(len(send_outs))]), send_outs):
+    for place_to, send in zip(places(sizes, [(k, 1) for k in range(len(send_outs))]), send_outs):
         send[...] = x_out[:, pl.ds(pl.multiple_of(place_to * slab, slab), slab)]
     totals = [jnp.zeros((count, columns), jnp.float32) for _ in range(2)]
     for i in range(wide // chunk):
@@ -148,14 +148,15 @@
     other_refs, a_refs, (own_out, other_out) = refs[:count], refs[count:-2], refs[-2:]
     slab, ranks = a_refs[0].shape[2], a_refs[0].shape[1]
     columns = part_ref.shape[1] - 2 * ranks
-    place = places(sizes, [(k + 1, 0) for k in range(count)])
+    place = places(sizes, [(k, 0) for k in range(count)])
     own = part_ref[:, columns:]
     other = jnp.zeros(own.shape, jnp.float32)
     for k, a in enumerate(a_refs):
         factor = a[...].reshape(2 * ranks, slab)
-        start = pl.multiple_of(place[k] * slab, slab)
-        own = own + dot(x_ref[:, pl.ds(start, slab)], factor, NT)
         other = other + dot(other_refs[k][...], factor, NT)
+        if k > 0:
+            start = pl.multiple_of(place[k] * slab, slab)
+            own = own + dot(x_ref[:, pl.ds(start, slab)], factor, NT)
     own_out[...] = own
     other_out[...] = other.astype(jnp.bfloat16)
 
@@ -285,7 +286,6 @@
 
     a_own, tick = lax.optimization_barrier((a_factor, tick))
     far = [over_fsdp(a_own, k) for k in range(1, inner)]
-    near = [(0, e, over_sub(a_factor, e)) for e in range(1, sub)]
 
     def join(mine, other, bit):
         low = jnp.where(bit == 0, mine, other)
@@ -338,7 +338,7 @@
     else:
         xs = jnp.stack(xs)
         xs = [lax.dynamic_index_in_dim(xs, (t - p - j) % tp, keepdims=False) for j in range(tp)]
-    near = [(0, 0, a_factor)] + near
+    near = [(0, 0, a_factor)]
     up = [up, over_fsdp(up, inner)] if direct else [up]
     width = 2 * columns + 2 * ranks
     part, x, *x_sends = pl.pallas_call(
@@ -347,9 +347,9 @@
             jax.ShapeDtypeStruct((tp * tokens, width), f32),
             jax.ShapeDtypeStruct((tp * tokens, wide), bf16),
         ]
-        + [jax.ShapeDtypeStruct((tp * tokens, a_factor.shape[2]), bf16)] * (inner - 1),
+        + [jax.ShapeDtypeStruct((tp * tokens, a_factor.shape[2]), bf16)] * inner,
         in_specs=[pl.BlockSpec(memory_space=pltpu.HBM)] + [vmem()] * (len(xs) + len(near)),
-        out_specs=[vmem()] * (1 + inner),
+        out_specs=[vmem()] * (2 + inner),
         scratch_shapes=[pltpu.VMEM((2, wide, columns), bf16), pltpu.SemaphoreType.DMA((8,))],
         compiler_params=params(50),
         cost_estimate=cost(C_EARLY),
@@ -359,16 +359,16 @@
     x_others = [over_sub(x, 1) for x in x_sends]
     far, part, up, x_others = lax.optimization_barrier((far, part, up, x_others))
     far_own, far_other = pl.pallas_call(
-        functools.partial(far_kernel, sizes, inner - 1),
+        functools.partial(far_kernel, sizes, inner),
         out_shape=[
             jax.ShapeDtypeStruct((tp * tokens, 2 * ranks), f32),
             jax.ShapeDtypeStruct((tp * tokens, 2 * ranks), bf16),
         ],
-        in_specs=[vmem()] * (2 * inner),
+        in_specs=[vmem()] * (2 + 2 * inner),
         out_specs=[vmem()] * 2,
         compiler_params=params(),
         name="far",
-    )(part, x, *x_others, *far)
+    )(part, x, *x_others, a_factor, *far)
     parts = pl.pallas_call(
         functools.partial(late_kernel, columns),
         out_shape=[jax.ShapeDtypeStruct((tokens, width), f32 if j == 0 else bf16) for j in range(tp)],

time: 35.5 us -> 35 us (0.986)
  waiting for transfers between devices: 18.8 us -> 17.1 us
  starting transfers between devices: 7.33 us -> 8.86 us
    ppermute x3, waiting for transfers between devices: 3.53 us -> 1.7 us  [over_fsdp(): return lax.ppermute(x, 'fsdp', [(i, i ^ k) for i in range(fsdp)])]
    ppermute x1, starting transfers between devices: 0.24 us -> 1.2 us  [local(): others.append(lax.ppermute(parts[j], 'fsdp', pairs))]
    ppermute x4, waiting for transfers between devices: 1.19 us -> 2.08 us  [over_sub(): return lax.ppermute(x, 'sub', [(i, i ^ k) for i in range(sub)])]
    ppermute x1, waiting for transfers between devices: 4.46 us -> 3.71 us  [local(): others.append(lax.ppermute(parts[j], 'fsdp', pairs))]
    ppermute x4, starting transfers between devices: 0.19 us -> 0.73 us  [over_sub(): return lax.ppermute(x, 'sub', [(i, i ^ k) for i in range(sub)])]
    pallas_call x1, Pallas kernels: 3.43 us -> 2.93 us  [local(): pl.pallas_call(functools.partial(early_kernel, tp, wide // 4, sizes, [(k,...]
  transfers between devices with their start and end apart: 11 -> 11, of which waited for: 6 -> 8; matrix products, arithmetic and copies ran while one was open for 0% -> 0% of each run, Pallas kernels for 17% -> 16%
where the time goes in v8:
time: 35 us; the launch traced here: 34.7 us
  waiting for transfers between devices  17.1 us (49%)
  starting transfers between devices  8.86 us (25%)
  Pallas kernels  7.33 us (21%)
  between operations  0.78 us (2%)
  local copies, waits for them, and re-layouts  0.71 us (2%)
    ppermute x1, waiting for transfers between devices, spread(): return lax.ppermute(x, ('fsdp', 'tp'), pairs)  3.99 us
    ppermute x1, waiting for transfers between devices, local(): others.append(lax.ppermute(parts[j], 'fsdp', pairs))  3.71 us
    ppermute x3, starting transfers between devices, over_fsdp(): return lax.ppermute(x, 'fsdp', [(i, i ^ k) for i in range(fsdp)])  3.61 us
    pallas_call x1, Pallas kernels, local(): pl.pallas_call(functools.partial(early_kernel, tp, wide // 4, sizes, [(k,...  2.93 us
    ppermute x1, waiting for transfers between devices, local(): lax.ppermute(own, 'tp', [(j, (j + i) % tp) for j in range(tp)])  2.93 us
    ppermute x1, waiting for transfers between devices, local(): xs = [inputs, xs[0], lax.ppermute(xs[0], ('fsdp', 'tp'), pairs)]  2.65 us
    ppermute x4, waiting for transfers between devices, over_sub(): return lax.ppermute(x, 'sub', [(i, i ^ k) for i in range(sub)])  2.08 us
    pallas_call x1, Pallas kernels, local(): pl.pallas_call(functools.partial(cache_kernel, group, len(up)), out_shape...  1.72 us
  transfers between devices with their start and end apart: 11, of which 8 were waited for; matrix products, arithmetic and copies ran while one was open for 0% of the time, Pallas kernels for 16%

profile of v8, /device:TPU:0, one launch (start us, length us, event | category | flops | bytes accessed | tf_op | source)
XLA Modules:
  0.0 34.7 jit_solution(1325908527004990258)
XLA Ops:
  0.6 0.0 copy-start
  0.6 0.0 copy-start.1
  0.7 0.0 copy-start.3
  0.7 0.0 copy-start.4
  0.7 0.0 copy-start.5
  0.7 0.0 copy-start.2
  0.7 3.1 %collective-permute-start.2 = (bf16[2,32,256]{2,1,0:T(8,128)(2,1)}, bf16[2,32,256]{2,1,0:T(8,128)(2,1)S(1)}, u32[]{:S(2)}, u32[]{:S(2)}) collective-permute-start(bf16[2,32,256]{2,1,0:T(8,128)(2,1)} %bitcast.1), channel_id=1, source_target_pairs={{0,4},{4,0},{8,12},{12,8},{1,5},{5,1},{9,13},{13,9},{2,6},{6,2},{1... | collective-permute-start | bytes 98312 | tf_op jit(solution)/shard_map/ppermute | solution.py:265
  3.8 1.5 %collective-permute-start.1 = (bf16[4,4,4096]{2,1,0:T(4,128)(2,1)}, bf16[4,4,4096]{2,1,0:T(4,128)(2,1)S(1)}, u32[]{:S(2)}, u32[]{:S(2)}) collective-permute-start(bf16[4,4,4096]{2,1,0:T(4,128)(2,1)} %refs_0_.1), channel_id=1, source_target_pairs={{0,2},{2,10},{4,6},{6,14},{8,0},{10,8},{12,4},{14,12},{1,3},{3,11}... | collective-permute-start | bytes 393224 | tf_op jit(solution)/shard_map/ppermute | solution.py:275
  5.3 0.6 %tick.1.tick_ref = f32[8,128]{1,0:T(8,128)} custom-call(), custom_call_target="tpu_custom_call" | custom-call | flops 8000000000 | bytes 24000000 | tf_op jit(solution)/shard_map/tick/pallas_call | solution.py:279
  5.9 0.0 copy-done
  5.9 0.4 %collective-permute-start = (bf16[2,128,1024]{2,1,0:T(8,128)(2,1)S(1)}, bf16[2,128,1024]{2,1,0:T(8,128)(2,1)S(1)}, u32[]{:S(2)}, u32[]{:S(2)}) collective-permute-start(bf16[2,128,1024]{2,1,0:T(8,128)(2,1)S(1)} %copy-done), channel_id=1, source_target_pairs={{0,4},{4,0},{8,12},{12,8},{1,5},{5,1},{9,13},{13,9},{2,6},{6,2},{1... | collective-permute-start | bytes 1572872 | tf_op jit(solution)/shard_map/ppermute | solution.py:265
  6.3 0.0 collective-permute-done.2.refs_1_
  6.3 0.0 copy-done.1
  6.3 0.0 copy-done.3
  6.3 0.0 copy-done.4
  6.3 0.0 copy-done.5
  6.3 0.0 copy-start.6
  6.4 0.7 %copy-done.6 = f32[8,128]{1,0:T(8,128)S(1)} copy-done((f32[8,128]{1,0:T(8,128)S(1)}, f32[8,128]{1,0:T(8,128)}, u32[]{:S(2)}) %copy-start.6) | copy-done | bytes 4120
  7.0 1.7 %cached.1 = (bf16[2,128,128]{2,1,0:T(8,128)(2,1)S(1)}, f32[2,128,128]{2,1,0:T(8,128)S(1)}, f32[2,128,128]{2,1,0:T(8,128)S(1)}, f32[2,128,128]{2,1,0:T(8,128)S(1)}, bf16[2,64,256]{2,1,0:T(8,128)(2,1)S(1)}) custom-call(s32[4]{0:T(128)S(1)} %copy-done.5, f32[8,128]{1,0:T(8,128)S(1)} %copy-done.6, bf16[4,4,2048]{2,1,0:T(4,128)(2,1)S(1)} %copy-done.3, ...), custom_call_target="tpu_custom_call" | custom-call | flops 2000000000 | bytes 6000000 | tf_op jit(solution)/shard_map/cached/pallas_call | solution.py:313
  8.8 4.0 %collective-permute-done.1.refs_1_ = bf16[4,4,4096]{2,1,0:T(4,128)(2,1)S(1)} collective-permute-done((bf16[4,4,4096]{2,1,0:T(4,128)(2,1)}, bf16[4,4,4096]{2,1,0:T(4,128)(2,1)S(1)}, u32[]{:S(2)}, u32[]{:S(2)}) %collective-permute-start.1) | collective-permute-done | bytes 131104 | tf_op jit(solution)/shard_map/ppermute | solution.py:275
  12.8 1.3 %collective-permute-start.3 = (bf16[4,4,4096]{2,1,0:T(4,128)(2,1)S(1)}, bf16[4,4,4096]{2,1,0:T(4,128)(2,1)S(1)}, u32[]{:S(2)}, u32[]{:S(2)}) collective-permute-start(bf16[4,4,4096]{2,1,0:T(4,128)(2,1)S(1)} %collective-permute-done.1.refs_1_), channel_id=1, source_target_pairs={{0,2},{4,6},{10,8},{14,12},{1,3},{5,7},{11,9},{15,13},{16,18},{20,... | collective-permute-start | bytes 393224 | tf_op jit(solution)/shard_map/ppermute | solution.py:337
  14.1 0.1 collective-permute-start.4
  14.1 2.7 %collective-permute-done.3.refs_2_ = bf16[4,4,4096]{2,1,0:T(4,128)(2,1)S(1)} collective-permute-done((bf16[4,4,4096]{2,1,0:T(4,128)(2,1)S(1)}, bf16[4,4,4096]{2,1,0:T(4,128)(2,1)S(1)}, u32[]{:S(2)}, u32[]{:S(2)}) %collective-permute-start.3) | collective-permute-done | bytes 131104 | tf_op jit(solution)/shard_map/ppermute | solution.py:337
  16.8 0.0 copy-done.2
  16.8 2.9 %early.1 = (f32[32,768]{1,0:T(8,128)S(1)}, bf16[32,4096]{1,0:T(8,128)(2,1)S(1)}, bf16[32,1024]{1,0:T(8,128)(2,1)S(1)}, bf16[32,1024]{1,0:T(8,128)(2,1)S(1)}) custom-call(bf16[2,8192,256]{2,1,0:T(8,128)(2,1)} %base_hbm.1, bf16[4,4,4096]{2,1,0:T(4,128)(2,1)S(1)} %copy-done.2, bf16[4,4,4096]{2,1,0:T(4,128)(2,1)S(1)} %collective-permute-done.1.refs_1_, ...), custom_call_target="tpu_custom_call" | custom-call | flops 3000000000 | bytes 9000000 | tf_op jit(solution)/shard_map/early/pallas_call | solution.py:344
  19.7 0.1 collective-permute-start.5
  19.8 0.5 %collective-permute-start.6 = (bf16[32,1024]{1,0:T(8,128)(2,1)S(1)}, bf16[32,1024]{1,0:T(8,128)(2,1)S(1)}, u32[]{:S(2)}, u32[]{:S(2)}) collective-permute-start(bf16[32,1024]{1,0:T(8,128)(2,1)S(1)} %get-tuple-element.34), channel_id=1, source_target_pairs={{0,1},{1,0},{2,3},{3,2},{4,5},{5,4},{6,7},{7,6},{8,9},{9,8},{10,11... | collective-permute-start | bytes 196616 | tf_op jit(solution)/shard_map/ppermute | solution.py:268
  20.3 0.0 collective-permute-done.4.refs_1_
  20.3 0.7 %collective-permute-done.5.refs_0_ = bf16[32,1024]{1,0:T(8,128)(2,1)S(1)} collective-permute-done((bf16[32,1024]{1,0:T(8,128)(2,1)S(1)}, bf16[32,1024]{1,0:T(8,128)(2,1)S(1)}, u32[]{:S(2)}, u32[]{:S(2)}) %collective-permute-start.5) | collective-permute-done | bytes 65568 | tf_op jit(solution)/shard_map/ppermute | solution.py:268
  21.1 0.2 collective-permute-done.6.refs_1_
  21.2 1.7 %collective-permute-done.refs_3_ = bf16[2,128,1024]{2,1,0:T(8,128)(2,1)S(1)} collective-permute-done((bf16[2,128,1024]{2,1,0:T(8,128)(2,1)S(1)}, bf16[2,128,1024]{2,1,0:T(8,128)(2,1)S(1)}, u32[]{:S(2)}, u32[]{:S(2)}) %collective-permute-start) | collective-permute-done | bytes 524320 | tf_op jit(solution)/shard_map/ppermute | solution.py:265
  22.9 0.5 %far.1 = (f32[32,256]{1,0:T(8,128)S(1)}, bf16[32,256]{1,0:T(8,128)(2,1)S(1)}) custom-call(f32[32,768]{1,0:T(8,128)S(1)} %get-tuple-element.35.part_ref, bf16[32,4096]{1,0:T(8,128)(2,1)S(1)} %get-tuple-element.36.x_ref, bf16[32,1024]{1,0:T(8,128)(2,1)S(1)} %collective-permute-done.5.refs_0_, bf16[32,1024]{1,0:T(8,128)(2,1)S(1)} %collective-permute-done.6.refs_1_, ...), custom_call_target="tpu_custom_call" | custom-call | tf_op jit(solution)/shard_map/far/pallas_call | solution.py:361
  23.4 0.0 collective-permute-start.7
  23.5 1.2 %collective-permute-done.7.other_ref = bf16[32,256]{1,0:T(8,128)(2,1)S(1)} collective-permute-done((bf16[32,256]{1,0:T(8,128)(2,1)S(1)}, bf16[32,256]{1,0:T(8,128)(2,1)S(1)}, u32[]{:S(2)}, u32[]{:S(2)}) %collective-permute-start.7) | collective-permute-done | bytes 16416 | tf_op jit(solution)/shard_map/ppermute | solution.py:268
  24.7 1.2 %collective-permute-start.8 = (bf16[16,768]{1,0:T(8,128)(2,1)S(1)}, bf16[16,768]{1,0:T(8,128)(2,1)S(1)}, u32[]{:S(2)}, u32[]{:S(2)}) collective-permute-start(bf16[16,768]{1,0:T(8,128)(2,1)S(1)} %get-tuple-element.47), channel_id=1, source_target_pairs={{0,8},{4,12},{8,0},{12,4},{1,9},{5,13},{9,1},{13,5},{2,10},{6,14},... | collective-permute-start | bytes 73736 | tf_op jit(solution)/shard_map/ppermute | solution.py:385
  25.9 0.1 collective-permute-start.9
  26.0 3.7 %collective-permute-done.8.refs_0_ = bf16[16,768]{1,0:T(8,128)(2,1)S(1)} collective-permute-done((bf16[16,768]{1,0:T(8,128)(2,1)S(1)}, bf16[16,768]{1,0:T(8,128)(2,1)S(1)}, u32[]{:S(2)}, u32[]{:S(2)}) %collective-permute-start.8) | collective-permute-done | bytes 24608 | tf_op jit(solution)/shard_map/ppermute | solution.py:385
  29.7 0.5 %collective-permute-start.10 = (bf16[16,256]{1,0:T(8,128)(2,1)S(1)}, bf16[16,256]{1,0:T(8,128)(2,1)S(1)}, u32[]{:S(2)}, u32[]{:S(2)}) collective-permute-start(bf16[16,256]{1,0:T(8,128)(2,1)S(1)} %ranks.1.refs_1_), channel_id=1, source_target_pairs={{0,2},{2,0},{1,3},{3,1},{4,6},{6,4},{5,7},{7,5},{8,10},{10,8},{9,1... | collective-permute-start | bytes 24584 | tf_op jit(solution)/shard_map/ppermute | solution.py:421
  30.3 0.0 collective-permute-done.9.refs_1_
  30.3 0.1 first.1.sum_in
  30.5 2.9 %collective-permute-done.10.refs_0_ = bf16[16,256]{1,0:T(8,128)(2,1)S(1)} collective-permute-done((bf16[16,256]{1,0:T(8,128)(2,1)S(1)}, bf16[16,256]{1,0:T(8,128)(2,1)S(1)}, u32[]{:S(2)}, u32[]{:S(2)}) %collective-permute-start.10) | collective-permute-done | bytes 8224 | tf_op jit(solution)/shard_map/ppermute | solution.py:421
  33.4 1.4 %final.1 = (bf16[2,4,4,256]{3,2,1,0:T(4,128)(2,1)}, bf16[4,4,2048]{2,1,0:T(4,128)(2,1)}) custom-call(f32[16,512]{1,0:T(8,128)S(1)} %first.1.sum_in, bf16[16,256]{1,0:T(8,128)(2,1)S(1)} %collective-permute-done.10.refs_0_, bf16[2,256,256]{2,1,0:T(8,128)(2,1)S(1)} %order.1.refs_2_.refs_1_, bf16[2,128,128]{2,1,0:T(8,128)(2,1)S(1)} %get-tuple-element.50.refs_2_, ...), custom_call_target="tpu_custom_call" | custom-call | tf_op jit(solution)/shard_map/final/pallas_call | solution.py:431
  (4 shorter events, 0.1 us)
Async XLA Ops:
  0.6 5.2 %copy-start = (bf16[2,128,1024]{2,1,0:T(8,128)(2,1)S(1)}, bf16[2,128,1024]{2,1,0:T(8,128)(2,1)}, u32[]{:S(2)}) copy-start(bf16[2,128,1024]{2,1,0:T(8,128)(2,1)} %refs_2_.1) | copy-start | bytes 1572868
  0.6 5.7 %copy-start.1 = (bf16[2,4,256,256]{3,2,1,0:T(8,128)(2,1)S(1)}, bf16[2,4,256,256]{3,2,1,0:T(8,128)(2,1)}, u32[]{:S(2)}) copy-start(bf16[2,4,256,256]{3,2,1,0:T(8,128)(2,1)} %kv_hbm.1) | copy-start | bytes 3145732
  0.7 5.7 %copy-start.3 = (bf16[4,4,2048]{2,1,0:T(4,128)(2,1)S(1)}, bf16[4,4,2048]{2,1,0:T(4,128)(2,1)}, u32[]{:S(2)}) copy-start(bf16[4,4,2048]{2,1,0:T(4,128)(2,1)} %q_hbm.1) | copy-start | bytes 196612
  0.7 5.7 %copy-start.4 = (bf16[2,256,32]{1,2,0:T(8,128)(2,1)S(1)}, bf16[2,256,32]{1,2,0:T(8,128)(2,1)}, u32[]{:S(2)}) copy-start(bf16[2,256,32]{1,2,0:T(8,128)(2,1)} %param.13) | copy-start | bytes 98308
  0.7 5.7 %copy-start.5 = (s32[4]{0:T(128)S(1)}, s32[4]{0:T(128)}, u32[]{:S(2)}) copy-start(s32[4]{0:T(128)} %len_ref.1) | copy-start | bytes 52
  0.7 16.1 %copy-start.2 = (bf16[4,4,4096]{2,1,0:T(4,128)(2,1)S(1)}, bf16[4,4,4096]{2,1,0:T(4,128)(2,1)}, u32[]{:S(2)}) copy-start(bf16[4,4,4096]{2,1,0:T(4,128)(2,1)} %refs_0_.1) | copy-start | bytes 393220
  0.7 5.6 %collective-permute-start.2 = (bf16[2,32,256]{2,1,0:T(8,128)(2,1)}, bf16[2,32,256]{2,1,0:T(8,128)(2,1)S(1)}, u32[]{:S(2)}, u32[]{:S(2)}) collective-permute-start(bf16[2,32,256]{2,1,0:T(8,128)(2,1)} %bitcast.1), channel_id=1, source_target_pairs={{0,4},{4,0},{8,12},{12,8},{1,5},{5,1},{9,13},{13,9},{2,6},{6,2},{1... | collective-permute-start | bytes 98312 | tf_op jit(solution)/shard_map/ppermute | solution.py:265
  3.8 9.0 %collective-permute-start.1 = (bf16[4,4,4096]{2,1,0:T(4,128)(2,1)}, bf16[4,4,4096]{2,1,0:T(4,128)(2,1)S(1)}, u32[]{:S(2)}, u32[]{:S(2)}) collective-permute-start(bf16[4,4,4096]{2,1,0:T(4,128)(2,1)} %refs_0_.1), channel_id=1, source_target_pairs={{0,2},{2,10},{4,6},{6,14},{8,0},{10,8},{12,4},{14,12},{1,3},{3,11}... | collective-permute-start | bytes 393224 | tf_op jit(solution)/shard_map/ppermute | solution.py:275
  5.9 17.0 %collective-permute-start = (bf16[2,128,1024]{2,1,0:T(8,128)(2,1)S(1)}, bf16[2,128,1024]{2,1,0:T(8,128)(2,1)S(1)}, u32[]{:S(2)}, u32[]{:S(2)}) collective-permute-start(bf16[2,128,1024]{2,1,0:T(8,128)(2,1)S(1)} %copy-done), channel_id=1, source_target_pairs={{0,4},{4,0},{8,12},{12,8},{1,5},{5,1},{9,13},{13,9},{2,6},{6,2},{1... | collective-permute-start | bytes 1572872 | tf_op jit(solution)/shard_map/ppermute | solution.py:265
  6.3 0.7 %copy-start.6 = (f32[8,128]{1,0:T(8,128)S(1)}, f32[8,128]{1,0:T(8,128)}, u32[]{:S(2)}) copy-start(f32[8,128]{1,0:T(8,128)} %tick.1.tick_ref) | copy-start | bytes 12292
  12.8 4.0 %collective-permute-start.3 = (bf16[4,4,4096]{2,1,0:T(4,128)(2,1)S(1)}, bf16[4,4,4096]{2,1,0:T(4,128)(2,1)S(1)}, u32[]{:S(2)}, u32[]{:S(2)}) collective-permute-start(bf16[4,4,4096]{2,1,0:T(4,128)(2,1)S(1)} %collective-permute-done.1.refs_1_), channel_id=1, source_target_pairs={{0,2},{4,6},{10,8},{14,12},{1,3},{5,7},{11,9},{15,13},{16,18},{20,... | collective-permute-start | bytes 393224 | tf_op jit(solution)/shard_map/ppermute | solution.py:337
  14.1 6.3 %collective-permute-start.4 = (bf16[2,64,256]{2,1,0:T(8,128)(2,1)S(1)}, bf16[2,64,256]{2,1,0:T(8,128)(2,1)S(1)}, u32[]{:S(2)}, u32[]{:S(2)}) collective-permute-start(bf16[2,64,256]{2,1,0:T(8,128)(2,1)S(1)} %get-tuple-element.48.refs_0_), channel_id=1, source_target_pairs={{0,8},{4,12},{8,0},{12,4},{1,9},{5,13},{9,1},{13,5},{2,10},{6,14},... | collective-permute-start | bytes 196616 | tf_op jit(solution)/shard_map/ppermute | solution.py:265
  19.7 1.3 %collective-permute-start.5 = (bf16[32,1024]{1,0:T(8,128)(2,1)S(1)}, bf16[32,1024]{1,0:T(8,128)(2,1)S(1)}, u32[]{:S(2)}, u32[]{:S(2)}) collective-permute-start(bf16[32,1024]{1,0:T(8,128)(2,1)S(1)} %get-tuple-element.33), channel_id=1, source_target_pairs={{0,1},{1,0},{2,3},{3,2},{4,5},{5,4},{6,7},{7,6},{8,9},{9,8},{10,11... | collective-permute-start | bytes 196616 | tf_op jit(solution)/shard_map/ppermute | solution.py:268
  19.8 1.4 %collective-permute-start.6 = (bf16[32,1024]{1,0:T(8,128)(2,1)S(1)}, bf16[32,1024]{1,0:T(8,128)(2,1)S(1)}, u32[]{:S(2)}, u32[]{:S(2)}) collective-permute-start(bf16[32,1024]{1,0:T(8,128)(2,1)S(1)} %get-tuple-element.34), channel_id=1, source_target_pairs={{0,1},{1,0},{2,3},{3,2},{4,5},{5,4},{6,7},{7,6},{8,9},{9,8},{10,11... | collective-permute-start | bytes 196616 | tf_op jit(solution)/shard_map/ppermute | solution.py:268
  23.4 1.2 %collective-permute-start.7 = (bf16[32,256]{1,0:T(8,128)(2,1)S(1)}, bf16[32,256]{1,0:T(8,128)(2,1)S(1)}, u32[]{:S(2)}, u32[]{:S(2)}) collective-permute-start(bf16[32,256]{1,0:T(8,128)(2,1)S(1)} %get-tuple-element.41), channel_id=1, source_target_pairs={{0,1},{1,0},{2,3},{3,2},{4,5},{5,4},{6,7},{7,6},{8,9},{9,8},{10,11... | collective-permute-start | bytes 49160 | tf_op jit(solution)/shard_map/ppermute | solution.py:268
  24.7 5.1 %collective-permute-start.8 = (bf16[16,768]{1,0:T(8,128)(2,1)S(1)}, bf16[16,768]{1,0:T(8,128)(2,1)S(1)}, u32[]{:S(2)}, u32[]{:S(2)}) collective-permute-start(bf16[16,768]{1,0:T(8,128)(2,1)S(1)} %get-tuple-element.47), channel_id=1, source_target_pairs={{0,8},{4,12},{8,0},{12,4},{1,9},{5,13},{9,1},{13,5},{2,10},{6,14},... | collective-permute-start | bytes 73736 | tf_op jit(solution)/shard_map/ppermute | solution.py:385
  25.9 4.4 %collective-permute-start.9 = (bf16[2,128,256]{2,1,0:T(8,128)(2,1)S(1)}, bf16[2,128,256]{2,1,0:T(8,128)(2,1)S(1)}, u32[]{:S(2)}, u32[]{:S(2)}) collective-permute-start(bf16[2,128,256]{2,1,0:T(8,128)(2,1)S(1)} %collect.1.refs_0_), channel_id=1, source_target_pairs={{0,1},{1,0},{2,3},{3,2},{4,5},{5,4},{6,7},{7,6},{8,9},{9,8},{10,11... | collective-permute-start | bytes 393224 | tf_op jit(solution)/shard_map/ppermute | solution.py:268
  29.7 3.7 %collective-permute-start.10 = (bf16[16,256]{1,0:T(8,128)(2,1)S(1)}, bf16[16,256]{1,0:T(8,128)(2,1)S(1)}, u32[]{:S(2)}, u32[]{:S(2)}) collective-permute-start(bf16[16,256]{1,0:T(8,128)(2,1)S(1)} %ranks.1.refs_1_), channel_id=1, source_target_pairs={{0,2},{2,0},{1,3},{3,1},{4,6},{6,4},{5,7},{7,5},{8,10},{10,8},{9,1... | collective-permute-start | bytes 24584 | tf_op jit(solution)/shard_map/ppermute | solution.py:421
